TPU v7x, 32 devices: a whole 2x2x4 slice. The times are simulated.
32 devices in a mesh: pb: 8 (over z, y), col: 4 (over x, core).
Axes of the slice: x: 2, y: 2, z: 4, core: 2. Of those that a mesh axis runs over, the one named last changes fastest.
Arguments:
- hidden: bfloat16 [8, 4, 1024, 768], P('pb', 'col'), may hold values from -6 to 6
- lengths: int32 [8, 4], P('pb', 'col'), may hold values from 256 to 1024, as said below
- counts: int32 [8], P('pb'), may hold values from 2 to 4, as said below
- targets: float32 [8, 4], P('pb', 'col'), may hold values from 0.01 to 100
- out_grad: bfloat16 [8, 4, 1024, 768], P('pb', 'col'), may hold values from -6 to 6
- qkv_weight: bfloat16 [768, 2304], P(('pb', 'col')), may hold values from -0.21875 to 0.21875
- qv_bias: bfloat16 [2, 768], P(None, ('pb', 'col')), may hold values from -3 to 3
- out_weight: bfloat16 [768, 768], P(('pb', 'col')), may hold values from -1.75 to 1.75
- out_bias: bfloat16 [768], P(('pb', 'col')), may hold values from -2 to 2
- norm1_gain: bfloat16 [768], P(('pb', 'col')), may hold values from 0.099609375 to 1.8984375
- norm1_bias: bfloat16 [768], P(('pb', 'col')), may hold values from -2 to 2
- up_weight: bfloat16 [768, 3072], P(('pb', 'col')), may hold values from -0.21875 to 0.21875
- up_bias: bfloat16 [3072], P(('pb', 'col')), may hold values from -3 to 3
- down_weight: bfloat16 [3072, 768], P(('pb', 'col')), may hold values from -0.15625 to 0.15625
- down_bias: bfloat16 [768], P(('pb', 'col')), may hold values from -2 to 2
- norm2_gain: bfloat16 [768], P(('pb', 'col')), may hold values from 0.099609375 to 1.8984375
- norm2_bias: bfloat16 [768], P(('pb', 'col')), may hold values from -2 to 2
- rel_bias: bfloat16 [32, 12], replicated, may hold values from -4 to 4
- score_weight: bfloat16 [768], P(('pb', 'col')), may hold values from -0.625 to 0.625
Outputs:
- layer_out: bfloat16 [8, 4, 1024, 768], P('pb', 'col')
- loss: float32 [], replicated
- hidden_grad: bfloat16 [8, 4, 1024, 768], P('pb', 'col')
- qkv_weight_grad: float32 [768, 2304], P(('pb', 'col'))
- qv_bias_grad: float32 [2, 768], P(None, ('pb', 'col'))
- out_weight_grad: float32 [768, 768], P(('pb', 'col'))
- out_bias_grad: float32 [768], P(('pb', 'col'))
- norm1_gain_grad: float32 [768], P(('pb', 'col'))
- norm1_bias_grad: float32 [768], P(('pb', 'col'))
- up_weight_grad: float32 [768, 3072], P(('pb', 'col'))
- up_bias_grad: float32 [3072], P(('pb', 'col'))
- down_weight_grad: float32 [3072, 768], P(('pb', 'col'))
- down_bias_grad: float32 [768], P(('pb', 'col'))
- norm2_gain_grad: float32 [768], P(('pb', 'col'))
- norm2_bias_grad: float32 [768], P(('pb', 'col'))
- rel_bias_grad: float32 [32, 12], replicated
- score_weight_grad: float32 [768], P(('pb', 'col'))
Inputs may be any that keep to these rules, and one draw needn't show every extreme that they name: lengths[q, c] counts the live tokens of a pair, the first ones of its 1024 slots; one pair of every draw has all 1024. counts[q] counts the live candidates of a query, the first ones of its 4 slots; one query of every draw has all 4.
All inputs are finite; a program needn't handle non-finite values.
Results may differ from a plain program's by a relative error of at most 0.015.
Values may be sent and summed in bfloat16 or wider, within the bound.
No kernel may reach another device: no remote copies, remote signals or barrier semaphores. Data moves between devices by JAX's collectives and lax.ppermute only.
A program may use at most 320 MiB of HBM per device.

v0:
```python
import jax
import jax.numpy as jnp
from jax import lax
from jax.sharding import PartitionSpec as P

EDGES = (1, 2, 3, 4, 5, 6, 7, 8, 12, 16, 23, 32, 45, 64, 91)


def bucket_ids(length):
    places = jnp.arange(length, dtype=jnp.int32)
    offset = places[None, :] - places[:, None]
    magnitude = jnp.abs(offset)
    ids = jnp.where(offset > 0, 16, 0).astype(jnp.int32)
    for edge in EDGES:
        ids = ids + (magnitude >= edge).astype(jnp.int32)
    return ids


def norm_forward(resid, gain, shift):
    centered = resid - jnp.mean(resid, axis=-1, keepdims=True)
    scaled = lax.rsqrt(jnp.mean(centered * centered, axis=-1, keepdims=True) + 1e-05)
    unit = centered * scaled
    return (unit * gain + shift, unit, scaled)


def norm_backward(upstream, unit, scaled, gain):
    pushed = upstream * gain
    inner = (
        pushed
        - jnp.mean(pushed, axis=-1, keepdims=True)
        - unit * jnp.mean(pushed * unit, axis=-1, keepdims=True)
    )
    return (inner * scaled, jnp.sum(upstream * unit, axis=0), jnp.sum(upstream, axis=0))


def matmul(left, right):
    return jnp.dot(left, right, preferred_element_type=jnp.float32)


def left_product(left, right):
    return jnp.einsum("ra,rb->ab", left, right, preferred_element_type=jnp.float32)


def right_product(left, right):
    return jnp.einsum("ra,ba->rb", left, right, preferred_element_type=jnp.float32)


def gelu_exact(inner):
    return jax.nn.gelu(inner, approximate=False)


def block_scores(queries, keys, table, live, factor):
    raw = jnp.einsum("ihd,jhd->hij", queries, keys, preferred_element_type=jnp.float32)
    return jnp.where(live[None, None, :], raw * factor + table, -1e30)


def listwise(scores, weights, counts):
    slots = scores.shape[1]
    live = jnp.arange(slots, dtype=jnp.float32)[None, :] < counts[:, None]
    share = jnp.where(live, weights, 0.0)
    target = share / jnp.sum(share, axis=1, keepdims=True)
    masked = jnp.where(live, scores, -1e30)
    top = jnp.max(masked, axis=1, keepdims=True)
    lognorm = top + jnp.log(jnp.sum(jnp.exp(masked - top), axis=1, keepdims=True))
    entropy = lognorm[:, 0] - jnp.sum(target * scores, axis=1)
    probs = jnp.where(live, jnp.exp(masked - lognorm), 0.0)
    return (entropy, probs - target)


def shards(
    hidden,
    lengths,
    counts,
    targets,
    out_grad,
    qkv_weight,
    qv_bias,
    out_weight,
    out_bias,
    norm1_gain,
    norm1_bias,
    up_weight,
    up_bias,
    down_weight,
    down_bias,
    norm2_gain,
    norm2_bias,
    rel_bias,
    score_weight,
):
    cand_dev = hidden.shape[1]
    pair_length = hidden.shape[2]
    model_width = hidden.shape[3]
    head_count = rel_bias.shape[1]
    head_size = model_width // head_count
    token_count = cand_dev * pair_length
    block_rows = min(512, pair_length)
    factor = head_size ** (-0.5)
    fetched = (
        lax.all_gather(qkv_weight, ("pb", "col"), axis=0, tiled=True),
        lax.all_gather(qv_bias, ("pb", "col"), axis=1, tiled=True),
        lax.all_gather(out_weight, ("pb", "col"), axis=0, tiled=True),
        lax.all_gather(out_bias, ("pb", "col"), axis=0, tiled=True),
        lax.all_gather(norm1_gain, ("pb", "col"), axis=0, tiled=True),
        lax.all_gather(norm1_bias, ("pb", "col"), axis=0, tiled=True),
        lax.all_gather(up_weight, ("pb", "col"), axis=0, tiled=True),
        lax.all_gather(up_bias, ("pb", "col"), axis=0, tiled=True),
        lax.all_gather(down_weight, ("pb", "col"), axis=0, tiled=True),
        lax.all_gather(down_bias, ("pb", "col"), axis=0, tiled=True),
        lax.all_gather(norm2_gain, ("pb", "col"), axis=0, tiled=True),
        lax.all_gather(norm2_bias, ("pb", "col"), axis=0, tiled=True),
        lax.all_gather(score_weight, ("pb", "col"), axis=0, tiled=True),
    )
    (
        qkv_w,
        qv_b,
        out_w,
        out_b,
        gain1,
        shift1,
        up_w,
        up_b,
        down_w,
        down_b,
        gain2,
        shift2,
        score_vec,
    ) = fetched
    gain1_f = gain1.astype(jnp.float32)
    gain2_f = gain2.astype(jnp.float32)
    score_f = score_vec.astype(jnp.float32)
    ids = bucket_ids(pair_length)
    onehot = (
        ids[None, :, :] == jnp.arange(rel_bias.shape[0], dtype=jnp.int32)[:, None, None]
    ).astype(jnp.bfloat16)
    table = jnp.einsum("bij,bh->hij", onehot, rel_bias, preferred_element_type=jnp.float32)
    tokens = hidden.reshape(token_count, model_width)
    qv_f = qv_b.astype(jnp.float32)
    zeros = jnp.zeros((model_width,), jnp.float32)
    qkv_low = (matmul(tokens, qkv_w) + jnp.concatenate([qv_f[0], zeros, qv_f[1]])).astype(
        jnp.bfloat16
    )
    places = jnp.arange(pair_length, dtype=jnp.int32)
    mixed_parts = []
    lognorms = []
    member = 0
    base = member * pair_length
    keys = qkv_low[base : base + pair_length, model_width : 2 * model_width].reshape(
        pair_length, head_count, head_size
    )
    values = qkv_low[base : base + pair_length, 2 * model_width :].reshape(
        pair_length, head_count, head_size
    )
    live = places < lengths[0, member]
    for offset in range(0, pair_length, block_rows):
        queries = qkv_low[base + offset : base + offset + block_rows, :model_width].reshape(
            block_rows, head_count, head_size
        )
        scores = block_scores(
            queries, keys, table[:, offset : offset + block_rows, :], live, factor
        )
        top = jnp.max(scores, axis=-1, keepdims=True)
        expo = jnp.exp(scores - top)
        total = jnp.sum(expo, axis=-1, keepdims=True)
        probs_low = (expo / total).astype(jnp.bfloat16)
        lognorms.append(top + jnp.log(total))
        mixed_parts.append(
            jnp.einsum(
                "hij,jhd->ihd", probs_low, values, preferred_element_type=jnp.float32
            ).reshape(block_rows, model_width)
        )
    mixed_low = jnp.concatenate(mixed_parts, axis=0).astype(jnp.bfloat16)
    attended = matmul(mixed_low, out_w) + out_b.astype(jnp.float32)
    normed, unit1, scaled1 = norm_forward(
        tokens.astype(jnp.float32) + attended, gain1_f, shift1.astype(jnp.float32)
    )
    normed_low = normed.astype(jnp.bfloat16)
    inner = matmul(normed_low, up_w) + up_b.astype(jnp.float32)
    activ_low = gelu_exact(inner).astype(jnp.bfloat16)
    branch = matmul(activ_low, down_w) + down_b.astype(jnp.float32)
    final, unit2, scaled2 = norm_forward(normed + branch, gain2_f, shift2.astype(jnp.float32))
    token_mask = (jnp.tile(places, cand_dev) < jnp.repeat(lengths[0], pair_length)).astype(
        jnp.float32
    )
    layer_out = (final * token_mask[:, None]).astype(jnp.bfloat16).reshape(hidden.shape)
    first_rows = final.reshape(cand_dev, pair_length, model_width)[:, 0, :]
    own_scores = jnp.sum(first_rows * score_f[None, :], axis=1)
    count_f = counts.astype(jnp.float32)
    col_index = lax.axis_index("col")
    near_scores, near_targets = (
        lax.all_gather(own_scores.reshape(1, cand_dev), "col", axis=1, tiled=True),
        lax.all_gather(targets, "col", axis=1, tiled=True),
    )
    entropy, difference = listwise(near_scores, near_targets, count_f)
    weighted, total_count = lax.psum((count_f[0] * entropy[0], count_f[0]), "pb")
    loss = weighted / total_count
    grad_row = count_f[0] / total_count * difference[0]
    grad_score = lax.dynamic_slice_in_dim(grad_row, col_index * cand_dev, cand_dev)
    refetched = (
        lax.all_gather(qkv_weight, ("pb", "col"), axis=0, tiled=True),
        lax.all_gather(out_weight, ("pb", "col"), axis=0, tiled=True),
        lax.all_gather(up_weight, ("pb", "col"), axis=0, tiled=True),
        lax.all_gather(down_weight, ("pb", "col"), axis=0, tiled=True),
        lax.all_gather(norm1_gain, ("pb", "col"), axis=0, tiled=True),
        lax.all_gather(norm2_gain, ("pb", "col"), axis=0, tiled=True),
        lax.all_gather(score_weight, ("pb", "col"), axis=0, tiled=True),
    )
    qkv_w, out_w, up_w, down_w, gain1, gain2, score_vec = refetched
    gain1_f = gain1.astype(jnp.float32)
    gain2_f = gain2.astype(jnp.float32)
    score_f = score_vec.astype(jnp.float32)
    score_weight_grad = jnp.sum(grad_score[:, None] * first_rows, axis=0)
    upstream = out_grad.reshape(cand_dev, pair_length, model_width).astype(jnp.float32)
    head_rows = upstream[:, :1, :] + (grad_score[:, None] * score_f[None, :])[:, None, :]
    grad_final = jnp.concatenate([head_rows, upstream[:, 1:, :]], axis=1).reshape(
        token_count, model_width
    )
    grad_final = grad_final * token_mask[:, None]
    grad_resid2, gain2_grad, shift2_grad = norm_backward(grad_final, unit2, scaled2, gain2_f)
    grad_branch = grad_resid2.astype(jnp.bfloat16)
    down_weight_grad = left_product(activ_low, grad_branch)
    down_bias_grad = jnp.sum(grad_branch.astype(jnp.float32), axis=0)
    grad_activ = right_product(grad_branch, down_w)
    grad_inner = jax.vjp(gelu_exact, inner)[1](grad_activ)[0].astype(jnp.bfloat16)
    up_weight_grad = left_product(normed_low, grad_inner)
    up_bias_grad = jnp.sum(grad_inner.astype(jnp.float32), axis=0)
    grad_normed = grad_resid2 + right_product(grad_inner, up_w)
    grad_resid1, gain1_grad, shift1_grad = norm_backward(grad_normed, unit1, scaled1, gain1_f)
    grad_attended = grad_resid1.astype(jnp.bfloat16)
    out_weight_grad = left_product(mixed_low, grad_attended)
    out_bias_grad = jnp.sum(grad_attended.astype(jnp.float32), axis=0)
    grad_mixed = right_product(grad_attended, out_w).astype(jnp.bfloat16)
    bucket_grad = jnp.zeros((rel_bias.shape[0], head_count), jnp.float32)
    counter = 0
    member = 0
    base = member * pair_length
    keys = qkv_low[base : base + pair_length, model_width : 2 * model_width].reshape(
        pair_length, head_count, head_size
    )
    values = qkv_low[base : base + pair_length, 2 * model_width :].reshape(
        pair_length, head_count, head_size
    )
    live = places < lengths[0, member]
    grad_keys = jnp.zeros((pair_length, head_count, head_size), jnp.float32)
    grad_values = jnp.zeros((pair_length, head_count, head_size), jnp.float32)
    query_parts = []
    for offset in range(0, pair_length, block_rows):
        queries = qkv_low[base + offset : base + offset + block_rows, :model_width].reshape(
            block_rows, head_count, head_size
        )
        scores = block_scores(
            queries, keys, table[:, offset : offset + block_rows, :], live, factor
        )
        probs = jnp.exp(scores - lognorms[counter])
        counter = counter + 1
        probs_low = probs.astype(jnp.bfloat16)
        grad_out = grad_mixed[base + offset : base + offset + block_rows].reshape(
            block_rows, head_count, head_size
        )
        grad_values = grad_values + jnp.einsum(
            "hij,ihd->jhd", probs_low, grad_out, preferred_element_type=jnp.float32
        )
        grad_probs = jnp.einsum(
            "ihd,jhd->hij", grad_out, values, preferred_element_type=jnp.float32
        )
        grad_scores = probs * (grad_probs - jnp.sum(probs * grad_probs, axis=-1, keepdims=True))
        scores_low = grad_scores.astype(jnp.bfloat16)
        query_parts.append(
            jnp.einsum(
                "hij,jhd->ihd", scores_low, keys, preferred_element_type=jnp.float32
            ).reshape(block_rows, model_width)
            * factor
        )
        grad_keys = (
            grad_keys
            + jnp.einsum("hij,ihd->jhd", scores_low, queries, preferred_element_type=jnp.float32)
            * factor
        )
        bucket_grad = bucket_grad + jnp.einsum(
            "hij,bij->bh",
            scores_low,
            onehot[:, offset : offset + block_rows, :],
            preferred_element_type=jnp.float32,
        )
    grad_parts = jnp.concatenate(
        [
            jnp.concatenate(query_parts, axis=0),
            grad_keys.reshape(pair_length, model_width),
            grad_values.reshape(pair_length, model_width),
        ],
        axis=1,
    )
    grad_qkv = grad_parts.astype(jnp.bfloat16)
    qkv_weight_grad = left_product(tokens, grad_qkv)
    grad_qkv_f = grad_qkv.astype(jnp.float32)
    qv_bias_grad = jnp.stack(
        [
            jnp.sum(grad_qkv_f[:, :model_width], axis=0),
            jnp.sum(grad_qkv_f[:, 2 * model_width :], axis=0),
        ]
    )
    hidden_grad = (
        (grad_resid1 + right_product(grad_qkv, qkv_w)).astype(jnp.bfloat16).reshape(hidden.shape)
    )
    summed = (
        lax.psum_scatter(qkv_weight_grad, ("pb", "col"), scatter_dimension=0, tiled=True),
        lax.psum_scatter(qv_bias_grad, ("pb", "col"), scatter_dimension=1, tiled=True),
        lax.psum_scatter(out_weight_grad, ("pb", "col"), scatter_dimension=0, tiled=True),
        lax.psum_scatter(out_bias_grad, ("pb", "col"), scatter_dimension=0, tiled=True),
        lax.psum_scatter(gain1_grad, ("pb", "col"), scatter_dimension=0, tiled=True),
        lax.psum_scatter(shift1_grad, ("pb", "col"), scatter_dimension=0, tiled=True),
        lax.psum_scatter(up_weight_grad, ("pb", "col"), scatter_dimension=0, tiled=True),
        lax.psum_scatter(up_bias_grad, ("pb", "col"), scatter_dimension=0, tiled=True),
        lax.psum_scatter(down_weight_grad, ("pb", "col"), scatter_dimension=0, tiled=True),
        lax.psum_scatter(down_bias_grad, ("pb", "col"), scatter_dimension=0, tiled=True),
        lax.psum_scatter(gain2_grad, ("pb", "col"), scatter_dimension=0, tiled=True),
        lax.psum_scatter(shift2_grad, ("pb", "col"), scatter_dimension=0, tiled=True),
        lax.psum_scatter(score_weight_grad, ("pb", "col"), scatter_dimension=0, tiled=True),
    )
    rel_bias_grad = lax.psum(bucket_grad, ("pb", "col"))
    return (
        layer_out,
        loss,
        hidden_grad,
        summed[0],
        summed[1],
        summed[2],
        summed[3],
        summed[4],
        summed[5],
        summed[6],
        summed[7],
        summed[8],
        summed[9],
        summed[10],
        summed[11],
        rel_bias_grad,
        summed[12],
    )


def solution(mesh):
    placed = (
        P("pb", "col", None, None),
        P("pb", "col"),
        P("pb"),
        P("pb", "col"),
        P("pb", "col", None, None),
        P(("pb", "col"), None),
        P(None, ("pb", "col")),
        P(("pb", "col"), None),
        P(("pb", "col")),
        P(("pb", "col")),
        P(("pb", "col")),
        P(("pb", "col"), None),
        P(("pb", "col")),
        P(("pb", "col"), None),
        P(("pb", "col")),
        P(("pb", "col")),
        P(("pb", "col")),
        P(),
        P(("pb", "col")),
    )
    return jax.shard_map(
        shards,
        mesh=mesh,
        in_specs=placed,
        out_specs=(
            P("pb", "col", None, None),
            P(),
            P("pb", "col", None, None),
            P(("pb", "col"), None),
            P(None, ("pb", "col")),
            P(("pb", "col"), None),
            P(("pb", "col")),
            P(("pb", "col")),
            P(("pb", "col")),
            P(("pb", "col"), None),
            P(("pb", "col")),
            P(("pb", "col"), None),
            P(("pb", "col")),
            P(("pb", "col")),
            P(("pb", "col")),
            P(),
            P(("pb", "col")),
        ),
        check_vma=False,
    )
```

profile of v0, /device:TPU:0, one launch (start us, length us, event | category | flops | bytes accessed | tf_op | source)
XLA Modules:
  0.0 972.8 jit_solution(15890420717733398986)
XLA Ops:
  18.1 43.0 %all-gather = bf16[32,24,2]{1,2,0:T(2,128)(2,1)S(1)} all-gather(bf16[1,24,2]{1,2,0:T(2,128)(2,1)S(1)} %bitcast.174), channel_id=1, replica_groups=mesh['pb'=8,'col'=4] {'pb','col'}, dimensions={0}, use_global_device_ids=true | all-gather | bytes 3168 | tf_op jit(solution)/shard_map/all_gather | solution.py:101
  61.5 27.4 %fusion.2 = f32[1024,1024,12]{1,2,0:T(8,128)} fusion(s32[1024,1024]{1,0:T(8,128)} %convert_add_fusion, bf16[32,12]{0,1:T(8,128)(2,1)S(1)} %copy-done), kind=kOutput, calls=%fused_computation.3 | convolution fusion | flops 838860800 | bytes 54526720 | tf_op jit(solution)/shard_map/bij,bh->hij/dot_general | solution.py:136
  89.0 44.5 %copy.95 = f32[1024,1024,12]{1,0,2:T(8,128)} copy(f32[1024,1024,12]{1,2,0:T(8,128)} %fusion.2) | data formatting | bytes 100663296 | tf_op jit(solution)/shard_map/bij,bh->hij/dot_general | solution.py:136
  136.1 37.9 %all-reduce.22 = (bf16[768]{0:T(1024)(128)(2,1)S(1)}, bf16[768]{0:T(1024)(128)(2,1)S(1)}, bf16[768]{0:T(1024)(128)(2,1)S(1)}, bf16[3072]{0:T(1024)(128)(2,1)S(1)...) all-reduce(bf16[768]{0:T(1024)(128)(2,1)S(1)} %dynamic-update-slice, ...), channel_id=1, replica_groups=mesh['pb'=8,'col'=4] {'pb','col'}, use_global_device_ids=true, to_apply=%add | all-reduce | flops 8448 | bytes 33792
  199.8 15.9 %fusion.90 = (f32[12,512]{1,0:T(8,128)S(1)}, f32[12,512,1024]{2,1,0:T(8,128)}) fusion(f32[12,1024,1024]{2,1,0:T(8,128)} %bitcast.139, bf16[512,12,64]{0,2,1:T(8,128)(2,1)} %bitcast.158, bf16[1024,12,64]{0,2,1:T(8,128)(2,1)S(1)} %bitcast.145, pred[1024]{0:T(1024)(128)(4,1)S(1)} %iota_compare_fusion.10), kind=kOutput, calls=%fused_computation.169 | convolution fusion | flops 830466048 | bytes 52716544 | tf_op jit(solution)/shard_map/ihd,jhd->hij/dot_general | solution.py:53
  215.7 15.9 %fusion.89 = (f32[12,512]{1,0:T(8,128)S(1)}, f32[12,512,1024]{2,1,0:T(8,128)}) fusion(f32[12,1024,1024]{2,1,0:T(8,128)} %bitcast.140, bf16[512,12,64]{0,2,1:T(8,128)(2,1)} %bitcast.156, bf16[1024,12,64]{0,2,1:T(8,128)(2,1)S(1)} %bitcast.146, pred[1024]{0:T(1024)(128)(4,1)S(1)} %iota_compare_fusion.10), kind=kOutput, calls=%fused_computation.168 | convolution fusion | flops 830466048 | bytes 52716544 | tf_op jit(solution)/shard_map/ihd,jhd->hij/dot_general | solution.py:53
  231.6 11.2 %fusion.8 = f32[12,512]{1,0:T(8,128)S(1)} fusion(f32[12,512,1024]{2,1,0:T(8,128)} %get-tuple-element.137, f32[12,512]{1,0:T(8,128)S(1)} %get-tuple-element.136), kind=kLoop, calls=%fused_computation.22 | loop fusion | flops 12576768 | bytes 25214976 | tf_op jit(solution)/shard_map/reduce_sum | solution.py:164
  242.8 11.4 %fusion.55 = bf16[12,64,512]{2,1,0:T(8,128)(2,1)} fusion(bf16[1024,12,64]{0,2,1:T(8,128)(2,1)S(1)} %bitcast.149, f32[12,512,1024]{2,1,0:T(8,128)} %get-tuple-element.137, f32[12,512]{1,0:T(8,128)S(1)} %fusion.8, f32[12,512]{1,0:T(8,128)S(1)} %get-tuple-element.136), kind=kOutput, calls=%fused_computation.113 | convolution fusion | flops 824573952 | bytes 27574272 | tf_op jit(solution)/shard_map/hij,jhd->ihd/dot_general | solution.py:168
  254.2 11.1 %fusion.9 = f32[12,512]{1,0:T(8,128)S(1)} fusion(f32[12,512,1024]{2,1,0:T(8,128)} %get-tuple-element.135, f32[12,512]{1,0:T(8,128)S(1)} %get-tuple-element.134), kind=kLoop, calls=%fused_computation.23 | loop fusion | flops 12576768 | bytes 25214976 | tf_op jit(solution)/shard_map/reduce_sum | solution.py:164
  265.3 11.5 %fusion.54 = bf16[12,64,512]{2,1,0:T(8,128)(2,1)} fusion(bf16[1024,12,64]{0,2,1:T(8,128)(2,1)S(1)} %bitcast.150, f32[12,512,1024]{2,1,0:T(8,128)} %get-tuple-element.135, f32[12,512]{1,0:T(8,128)S(1)} %fusion.9, f32[12,512]{1,0:T(8,128)S(1)} %get-tuple-element.134), kind=kOutput, calls=%fused_computation.112 | convolution fusion | flops 824573952 | bytes 27574272 | tf_op jit(solution)/shard_map/hij,jhd->ihd/dot_general | solution.py:168
  281.3 36.4 %multiply_convert_fusion.2 = (bf16[1024,3072]{1,0:T(8,128)(2,1)}, f32[1024,3072]{1,0:T(8,128)}, f32[1024,3072]{1,0:T(8,128)}) fusion(f32[3072]{0:T(1024)S(1)} %convert_element_type.306, bf16[768,3072]{1,0:T(8,128)(2,1)} %all-gather.10.cloned.1.call-done, f32[1024,768]{1,0:T(8,128)S(1)} %get-tuple-element.139, f32[768]{0:T(1024)S(1)} %convert_element_type.304, ...), kind=kOutput, calls=%fused_computation.36 | convolution fusion | flops 5043388416 | bytes 39348224 | tf_op jit(solution)/shard_map/dot_general | solution.py:37
  341.0 21.7 %all-reduce.20 = (f32[]{:T(128)}, f32[]{:T(128)}) all-reduce(f32[]{:T(128)S(6)} %mul.234, f32[]{:T(128)} %bitcast.16), channel_id=1, replica_groups=mesh['pb'=8,'col'=4] {'pb'}, use_global_device_ids=true, to_apply=%region_13.14 | all-reduce | flops 2 | bytes 16 | tf_op jit(solution)/shard_map/psum | solution.py:195
  374.5 19.5 %convert_reduce_fusion = (f32[3072]{0:T(1024)}, bf16[1024,3072]{1,0:T(8,128)(2,1)}) fusion(f32[1024,3072]{1,0:T(8,128)} %get-tuple-element.126, bf16[3072,768]{1,0:T(8,128)(2,1)} %all-gather.12.cloned.1.call-done, f32[1024,768]{1,0:T(8,128)} %get-tuple-element.122, f32[1024,3072]{1,0:T(8,128)} %get-tuple-element.140, f32[3072]{0:T(1024)S(1)} %convert_element_type.306), kind=kOutput, calls=%fused_computation.32 | convolution fusion | flops 4886098944 | bytes 39346176 | tf_op jit(solution)/shard_map/ra,ba->rb/dot_general | solution.py:45
  416.0 20.1 %multiply_reduce_fusion = (f32[12,512]{1,0:T(8,128)S(1)}, f32[12,512,1024]{2,1,0:T(8,128)}) fusion(f32[12,512,1024]{2,1,0:T(8,128)} %get-tuple-element.135, f32[12,512]{1,0:T(8,128)S(1)} %log_add_fusion, bf16[512,12,64]{0,2,1:T(8,128)(2,1)S(1)} %bitcast.162, bf16[1024,12,64]{0,2,1:T(8,128)(2,1)S(1)} %bitcast.152), kind=kOutput, calls=%fused_computation.13 | convolution fusion | flops 824174592 | bytes 52740096 | tf_op jit(solution)/shard_map/ihd,jhd->hij/dot_general | solution.py:263
  436.1 11.9 %fusion.15 = f32[12,64,1024]{2,1,0:T(8,128)} fusion(bf16[512,12,64]{0,2,1:T(8,128)(2,1)S(1)} %bitcast.163, f32[12,512,1024]{2,1,0:T(8,128)} %get-tuple-element.135, f32[12,512]{1,0:T(8,128)S(1)} %log_add_fusion), kind=kOutput, calls=%fused_computation.30 | convolution fusion | flops 817889280 | bytes 29122560 | tf_op jit(solution)/shard_map/hij,ihd->jhd/dot_general | solution.py:260
  448.1 17.1 %multiply_convert_fusion = bf16[12,512,1024]{2,1,0:T(8,128)(2,1)S(1)} fusion(f32[12,512,1024]{2,1,0:T(8,128)} %get-tuple-element.147, f32[12,512,1024]{2,1,0:T(8,128)} %get-tuple-element.135, f32[12,512]{1,0:T(8,128)S(1)} %get-tuple-element.146, f32[12,512]{1,0:T(8,128)S(1)} %log_add_fusion), kind=kLoop, calls=%fused_computation.12 | loop fusion | flops 25165824 | bytes 62963712 | tf_op jit(solution)/shard_map/convert_element_type | solution.py:267
  472.8 16.8 %multiply_reduce_fusion.1 = (f32[12,512]{1,0:T(8,128)S(1)}, f32[12,512,1024]{2,1,0:T(8,128)}) fusion(f32[12,512,1024]{2,1,0:T(8,128)} %get-tuple-element.137, f32[12,512]{1,0:T(8,128)S(1)} %log_add_fusion.1, bf16[512,12,64]{0,2,1:T(8,128)(2,1)} %bitcast.160, bf16[1024,12,64]{0,2,1:T(8,128)(2,1)} %bitcast.151), kind=kOutput, calls=%fused_computation.16 | convolution fusion | flops 824174592 | bytes 52740096 | tf_op jit(solution)/shard_map/ihd,jhd->hij/dot_general | solution.py:263
  489.6 22.2 %multiply_convert_fusion.1 = bf16[12,512,1024]{2,1,0:T(8,128)(2,1)} fusion(f32[12,512,1024]{2,1,0:T(8,128)} %get-tuple-element.145, f32[12,512,1024]{2,1,0:T(8,128)} %get-tuple-element.137, f32[12,512]{1,0:T(8,128)S(1)} %get-tuple-element.144, f32[12,512]{1,0:T(8,128)S(1)} %log_add_fusion.1), kind=kLoop, calls=%fused_computation.15 | loop fusion | flops 25165824 | bytes 62963712 | tf_op jit(solution)/shard_map/convert_element_type | solution.py:267
  544.4 13.0 %convolution_bitcast_fusion = f32[768,2304]{0,1:T(8,128)} fusion(bf16[1,1,1024,768]{3,2,1,0:T(8,128)(2,1)S(1)} %copy-done.44, bf16[1024,768]{0,1:T(8,128)(2,1)S(1)} %bitcast.164, bf16[1024,768]{0,1:T(8,128)(2,1)S(1)} %bitcast.153, bf16[512,768]{0,1:T(8,128)(2,1)S(1)} %bitcast.169, bf16[512,768]{0,1:T(8,128)(2,1)S(1)} %bitcast.172), kind=kOutput, calls=%fused_computation.53 | convolution fusion | flops 3642753024 | bytes 13369344 | tf_op jit(solution)/shard_map/ra,rb->ab/dot_general | solution.py:41
  597.9 23.2 %fusion.56 = f32[32,12]{0,1:T(8,128)S(1)} fusion(bf16[12,512,1024]{2,1,0:T(8,128)(2,1)} %multiply_convert_fusion.1, s32[1024,1024]{1,0:T(8,128)S(1)} %copy-done.9), kind=kOutput, calls=%fused_computation.114 | convolution fusion | flops 436207616 | bytes 16778752 | tf_op jit(solution)/shard_map/hij,bij->bh/dot_general | solution.py:279
  621.1 16.4 %fusion.62 = f32[32,12]{0,1:T(8,128)S(1)} fusion(f32[32,12]{0,1:T(8,128)S(1)} %fusion.56, bf16[12,512,1024]{2,1,0:T(8,128)(2,1)S(1)} %bitcast.144, s32[1024,1024]{1,0:T(8,128)S(1)} %copy-done.9), kind=kOutput, calls=%fused_computation.116 | convolution fusion | flops 436208000 | bytes 16780288 | tf_op jit(solution)/shard_map/hij,bij->bh/dot_general | solution.py:279
  637.6 39.1 %all-reduce.19 = (f32[2,768]{1,0:T(2,128)S(1)}, f32[768]{0:T(1024)S(1)}, f32[768]{0:T(1024)S(1)}, f32[768]{0:T(1024)S(1)}, f32[3072]{0:T(1024)S(1)}, /*index=5*/...) all-reduce(f32[2,768]{1,0:T(2,128)S(1)} %pad_maximum_fusion.5, ...), channel_id=3, replica_groups=mesh['pb'=8,'col'=4] {'pb','col'}, use_global_device_ids=true, to_apply=%region_24.25.clone | all-reduce | flops 10368 | bytes 82944
  691.9 130.3 %reduce-scatter.12.cloned.1.call-done = f32[96,768]{1,0:T(8,128)} async-done(((f32[3072,768]{1,0:T(8,128)}), f32[96,768]{1,0:T(8,128)}) %reduce-scatter.12.cloned.1.call-update) | async-done | bytes 294928 | tf_op jit(solution)/shard_map/reduce_scatter | solution.py:314
  822.2 142.1 %reduce-scatter.10.cloned.1.call-done = f32[24,3072]{1,0:T(8,128)} async-done(((f32[768,3072]{1,0:T(8,128)}), f32[24,3072]{1,0:T(8,128)}) %reduce-scatter.10.cloned.1.call-update) | async-done | bytes 294928 | tf_op jit(solution)/shard_map/reduce_scatter | solution.py:312
  (255 shorter events, 190.3 us)
Async XLA Ops:
  7.2 54.3 %copy-start = (bf16[32,12]{0,1:T(8,128)(2,1)S(1)}, bf16[32,12]{0,1:T(8,128)(2,1)}, u32[]{:S(2)}) copy-start(bf16[32,12]{0,1:T(8,128)(2,1)} %param.36) | copy-start | bytes 2308
  7.2 175.6 %all-gather.6.cloned.1.call-start = ((), (), s32[]{:S(2)}) async-start(), calls=%async_computation.4 | async-start | bytes 3649536 | tf_op jit(solution)/shard_map/all_gather | solution.py:100
  7.9 268.9 %all-gather.8.cloned.1.call-start = ((), (), s32[]{:S(2)}) async-start(), calls=%async_computation.5 | async-start | bytes 1216512 | tf_op jit(solution)/shard_map/all_gather | solution.py:102
  8.7 272.6 %all-gather.10.cloned.1.call-start = ((), (), s32[]{:S(2)}) async-start(), calls=%async_computation.6 | async-start | bytes 4866048 | tf_op jit(solution)/shard_map/all_gather | solution.py:106
  9.4 308.3 %all-gather.12.cloned.1.call-start = ((), (), s32[]{:S(2)}) async-start(), calls=%async_computation.7 | async-start | bytes 4866048 | tf_op jit(solution)/shard_map/all_gather | solution.py:108
  10.0 681.9 %reduce-scatter.8.cloned.1.call-start = ((), (), s32[]{:S(2)}) async-start(), calls=%async_computation.8 | async-start | bytes 2433024 | tf_op jit(solution)/shard_map/reduce_scatter | solution.py:308
  88.9 45.3 %copy-start.46 = (bf16[24]{0:T(256)(128)(2,1)S(1)}, bf16[24]{0:T(256)(128)(2,1)}, u32[]{:S(2)}) copy-start(bf16[24]{0:T(256)(128)(2,1)} %param.27) | copy-start | bytes 148
  88.9 45.5 %copy-start.47 = (bf16[24]{0:T(256)(128)(2,1)S(1)}, bf16[24]{0:T(256)(128)(2,1)}, u32[]{:S(2)}) copy-start(bf16[24]{0:T(256)(128)(2,1)} %param.28) | copy-start | bytes 148
  88.9 45.7 %copy-start.48 = (bf16[24]{0:T(256)(128)(2,1)S(1)}, bf16[24]{0:T(256)(128)(2,1)}, u32[]{:S(2)}) copy-start(bf16[24]{0:T(256)(128)(2,1)} %param.29) | copy-start | bytes 148
  88.9 46.0 %copy-start.49 = (bf16[24]{0:T(256)(128)(2,1)S(1)}, bf16[24]{0:T(256)(128)(2,1)}, u32[]{:S(2)}) copy-start(bf16[24]{0:T(256)(128)(2,1)} %param.33) | copy-start | bytes 148
  89.0 46.2 %copy-start.50 = (bf16[24]{0:T(256)(128)(2,1)S(1)}, bf16[24]{0:T(256)(128)(2,1)}, u32[]{:S(2)}) copy-start(bf16[24]{0:T(256)(128)(2,1)} %param.34) | copy-start | bytes 148
  89.0 46.4 %copy-start.51 = (bf16[24]{0:T(256)(128)(2,1)S(1)}, bf16[24]{0:T(256)(128)(2,1)}, u32[]{:S(2)}) copy-start(bf16[24]{0:T(256)(128)(2,1)} %param.35) | copy-start | bytes 148
  89.0 46.7 %copy-start.52 = (bf16[24]{0:T(256)(128)(2,1)S(1)}, bf16[24]{0:T(256)(128)(2,1)}, u32[]{:S(2)}) copy-start(bf16[24]{0:T(256)(128)(2,1)} %param.37) | copy-start | bytes 148
  89.0 46.9 %copy-start.53 = (bf16[96]{0:T(256)(128)(2,1)S(1)}, bf16[96]{0:T(256)(128)(2,1)}, u32[]{:S(2)}) copy-start(bf16[96]{0:T(256)(128)(2,1)} %param.31) | copy-start | bytes 580
  89.0 86.9 %copy-start.56 = (u32[32]{0:T(128)S(1)}, u32[32]{0:T(128)}, u32[]{:S(2)}) copy-start(u32[32]{0:T(128)} %constant.174) | copy-start | bytes 388
  89.0 88.7 %copy-start.25 = (bf16[1,1,1024,768]{3,2,1,0:T(8,128)(2,1)S(1)}, bf16[1,1,1024,768]{3,2,1,0:T(8,128)(2,1)}, u32[]{:S(2)}) copy-start(bf16[1,1,1024,768]{3,2,1,0:T(8,128)(2,1)} %param.23) | copy-start | bytes 4718596
  174.0 143.7 %copy-start.26 = (f32[768]{0:T(1024)}, f32[768]{0:T(1024)S(1)}, u32[]{:S(2)}) copy-start(f32[768]{0:T(1024)S(1)} %convert_element_type.304) | copy-start | bytes 9220
  196.9 68.4 %copy-start.10 = (bf16[1024,768]{0,1:T(8,128)(2,1)}, bf16[1024,768]{0,1:T(8,128)(2,1)S(1)}, u32[]{:S(2)}) copy-start(bf16[1024,768]{0,1:T(8,128)(2,1)S(1)} %copy.72) | copy-start | bytes 4718596
  280.7 37.0 %copy-start.5 = (f32[1024,768]{1,0:T(8,128)}, f32[1024,768]{1,0:T(8,128)S(1)}, u32[]{:S(2)}) copy-start(f32[1024,768]{1,0:T(8,128)S(1)} %get-tuple-element.139) | copy-start | bytes 9437188
  327.1 39.1 %copy-start.30 = (f32[1024]{0:T(1024)S(1)}, f32[1024]{0:T(1024)}, u32[]{:S(2)}) copy-start(f32[1024]{0:T(1024)} %fusion.69) | copy-start | bytes 12292
  448.1 243.8 %reduce-scatter.14.cloned.1.call-start = ((), (), s32[]{:S(2)}) async-start(), calls=%async_computation.11 | async-start | bytes 7299072
  565.5 256.7 %reduce-scatter.12.cloned.1.call-start = ((), (), s32[]{:S(2)}) async-start(), calls=%async_computation.10 | async-start | bytes 9732096 | tf_op jit(solution)/shard_map/reduce_scatter | solution.py:314
  577.9 386.4 %reduce-scatter.10.cloned.1.call-start = ((), (), s32[]{:S(2)}) async-start(), calls=%async_computation.9 | async-start | bytes 9732096 | tf_op jit(solution)/shard_map/reduce_scatter | solution.py:312
  683.4 281.0 %copy-start.1 = (bf16[32,12]{0,1:T(8,128)(2,1)S(1)}, bf16[32,12]{0,1:T(8,128)(2,1)}, u32[]{:S(2)}) copy-start(bf16[32,12]{0,1:T(8,128)(2,1)} %param.36) | copy-start | bytes 2308
  (49 other events, 492.3 us)
Sparse Core Ops, SparseCore 0:
  10.9 62.8 all-gather.5
  76.7 52.8 all-gather.7
  132.5 62.7 all-gather.9
  198.1 62.4 all-gather.11
  448.2 95.1 reduce-scatter.7
  565.6 115.3 reduce-scatter.13
  687.4 134.7 reduce-scatter.11
  829.7 134.5 reduce-scatter.9
where the time goes:
time: 982 us; the launch traced here: 973 us
  matrix products  344 us (35%)
  waiting for transfers between devices  275 us (28%)
  blocking collectives  148 us (15%)
  other arithmetic  94 us (10%)
  local copies, waits for them, and re-layouts  88.4 us (9%)
  between operations  22.7 us (2%)
    reduce_scatter x1, waiting for transfers between devices, shards(): lax.psum_scatter(up_weight_grad, ('pb', 'col'), scatter_dimension=0, tile...  142 us
    reduce_scatter x1, waiting for transfers between devices, shards(): lax.psum_scatter(down_weight_grad, ('pb', 'col'), scatter_dimension=0, ti...  130 us
    unnamed x3, blocking collectives  83.2 us
    dot_general x4, matrix products, matmul(): return jnp.dot(left, right, preferred_element_type=jnp.float32)  55.7 us
    dot_general x1, local copies, waits for them, and re-layouts, shards(): jnp.einsum('bij,bh->hij', onehot, rel_bias, preferred_element_type=jnp.fl...  44.5 us
    all_gather x1, blocking collectives, shards(): lax.all_gather(qv_bias, ('pb', 'col'), axis=1, tiled=True)  43 us
    dot_general x4, matrix products, right_product(): jnp.einsum('ra,ba->rb', left, right, preferred_element_type=jnp.float32)  42 us
    dot_general x2, matrix products, shards(): jnp.einsum('hij,bij->bh', scores_low, onehot[:, offset:offset + block_row...  39.5 us
  transfers between devices with their start and end apart: 8, of which 2 were waited for; matrix products, arithmetic and copies ran while one was open for 43% of the time, Pallas kernels for 0%

commit v1 on v0

v1 whole, which is shorter than its diff:
```python
import functools

import jax
import jax.numpy as jnp
from jax import lax
from jax.experimental import pallas as pl
from jax.experimental.pallas import tpu as pltpu
from jax.sharding import PartitionSpec as P

f32=jnp.float32; bf=jnp.bfloat16
NT=(((1,),(1,)),((),())); NN=(((1,),(0,)),((),())); TN=(((0,),(0,)),((),()))
T=128
EDGES = (1, 2, 3, 4, 5, 6, 7, 8, 12, 16, 23, 32, 45, 64, 91)
def strip_ids():
    r=jnp.arange(3*T,dtype=jnp.int32)[None,:]-T-jnp.arange(T,dtype=jnp.int32)[:,None]
    m=jnp.abs(r); ids=jnp.where(r>0,16,0).astype(jnp.int32)
    for e in EDGES: ids=ids+(m>=e).astype(jnp.int32)
    return ids
def tables(rel_bias, length, S):
    ids=strip_ids()
    nb=rel_bias.shape[0]
    oh=(ids[None]==jnp.arange(nb,dtype=jnp.int32)[:,None,None]).astype(bf)
    strips=jnp.einsum("bac,bh->hac",oh,rel_bias,preferred_element_type=f32)
    j=jnp.arange(S,dtype=jnp.int32)[:,None]; lane=jnp.arange(128,dtype=jnp.int32)[None,:]
    jb=j//T; nblk=S//T
    low=(jb<=lane-2)&(lane<nblk); up=(jb>=lane+2)&(lane<nblk)
    mk=jnp.where((lane==nblk)&(j>=length),-1e30,0.0)
    rb=rel_bias.astype(f32)
    kx=jnp.where(low[None],rb[15][:,None,None],jnp.where(up[None],rb[31][:,None,None],mk[None])).astype(bf)
    return strips,kx
def fwd_kernel(BQ, S, q_ref,k_ref,v_ref,kx_ref,st_ref,mix_ref,linv_ref,mf_ref,p_ref):
    nblk=S//T
    lane=lax.broadcasted_iota(jnp.int32,(1,128),1)
    row=lax.broadcasted_iota(jnp.int32,(BQ,128),0)//T
    lane2=lax.broadcasted_iota(jnp.int32,(BQ,128),1)
    q=q_ref[...];k=k_ref[...];v=v_ref[...]
    masks=[lane<64,lane>=64]
    kaug=[jnp.concatenate([k,kx_ref[h]],axis=1) for h in (0,1)]
    vaug=[jnp.where(masks[h],v,jnp.ones_like(v)) for h in (0,1)]
    for i in range(S//BQ):
        outs=[]
        qi=q[i*BQ:(i+1)*BQ]
        qx=((lane2==nblk)|(lane2==row+i*(BQ//T))).astype(f32).astype(bf)
        for h in (0,1):
            qa=jnp.concatenate([jnp.where(masks[h],qi,jnp.zeros_like(qi)),qx],axis=1)
            s=dg(qa,kaug[h],NT)
            rows=[]
            for b in range(BQ//T):
                I=i*(BQ//T)+b
                lo=max(0,(I-1)*T);hi=min(S,(I+2)*T)
                sb=s[b*T:(b+1)*T]
                parts=[]
                if lo>0: parts.append(sb[:,:lo])
                parts.append(sb[:,lo:hi]+st_ref[h,:,lo-(I-1)*T:hi-(I-1)*T])
                if hi<S: parts.append(sb[:,hi:])
                rows.append(jnp.concatenate(parts,axis=1) if len(parts)>1 else parts[0])
            s=jnp.concatenate(rows,axis=0) if len(rows)>1 else rows[0]
            m=jnp.max(s,axis=1,keepdims=True)
            p=jnp.exp(s-m).astype(bf)
            p_ref[h,i*BQ:(i+1)*BQ,:]=p
            outs.append(dg(p,vaug[h],NN))
        o0,o1=outs
        num=jnp.where(masks[0],o0,o1)
        den=jnp.where(masks[0],o1,o0)
        den=pltpu.roll(den,64,1)
        linv=1.0/den
        mf=num*linv
        mf_ref[i*BQ:(i+1)*BQ,:]=mf
        mix_ref[i*BQ:(i+1)*BQ,:]=mf.astype(bf)
        linv_ref[i*BQ:(i+1)*BQ,:]=linv
def attn_fwd(qkv,kx,strips,BQ=128):
    S,W=qkv.shape; npair=W//3//128
    return pl.pallas_call(functools.partial(fwd_kernel,BQ,S),grid=(npair,),
        in_specs=[pl.BlockSpec((S,128),lambda p:(0,p)),pl.BlockSpec((S,128),lambda p:(0,npair+p)),pl.BlockSpec((S,128),lambda p:(0,2*npair+p)),
                  pl.BlockSpec((2,S,128),lambda p:(p,0,0)),pl.BlockSpec((2,T,3*T),lambda p:(p,0,0))],
        out_specs=[pl.BlockSpec((S,128),lambda p:(0,p))]*3+[pl.BlockSpec((2,S,S),lambda p:(p,0,0))],
        out_shape=[jax.ShapeDtypeStruct((S,W//3),bf),jax.ShapeDtypeStruct((S,W//3),f32),jax.ShapeDtypeStruct((S,W//3),f32),jax.ShapeDtypeStruct((2*npair,S,S),bf)],
        compiler_params=pltpu.CompilerParams(vmem_limit_bytes=56*2**20),
        )(qkv,qkv,qkv,kx,strips)
def bwd_kernel(BQ,S,form,scale,kscale,q_ref,k_ref,v_ref,gm_ref,mf_ref,linv_ref,p_ref,dq_ref,dk_ref,dv_ref,near_ref,far_ref,ds_ref):
    nblk=S//T
    lane=lax.broadcasted_iota(jnp.int32,(1,128),1)
    lanes=lax.broadcasted_iota(jnp.int32,(S,128),1)
    rows=lax.broadcasted_iota(jnp.int32,(S,128),0)
    masks=[lane<64,lane>=64]
    q=q_ref[...];k=k_ref[...];v=v_ref[...]
    gm=gm_ref[...].astype(f32);linv=linv_ref[...]
    do=(gm*linv).astype(bf)
    t=do.astype(f32)*mf_ref[...]
    kind=(lanes==rows//T).astype(f32).astype(bf)
    kaug=jnp.concatenate([k,kind],axis=1)
    vx=jnp.where(lanes<2,1.0,0.0).astype(bf)
    vaug=jnp.concatenate([v,vx],axis=1)
    dqs=[];dks=[];dvs=[]
    if form=="T":
        qT=q.T; doT=do.T
    for h in (0,1):
        delta=jnp.sum(jnp.where(masks[h],t,0.0),axis=1,keepdims=True)
        hi=delta.astype(bf).astype(f32); lo=delta-hi
        ex=jnp.where(lanes==0,-hi,jnp.where(lanes==1,-lo,0.0)).astype(bf)
        da=jnp.concatenate([jnp.where(masks[h],do,jnp.zeros_like(do)),ex],axis=1)
        near=[jnp.zeros((T,T),f32) for _ in range(3)]
        dq=[]
        for i in range(S//BQ):
            x=dg(da[i*BQ:(i+1)*BQ],vaug,NT)
            ds=p_ref[h,i*BQ:(i+1)*BQ,:]*x.astype(bf)
            ds_ref[i*BQ:(i+1)*BQ,:]=ds
            dq.append(dg(ds,kaug,NN))
            for b in range(BQ//T):
                I=i*(BQ//T)+b
                for n in (-1,0,1):
                    if 0<=I+n<nblk:
                        near[n+1]=near[n+1]+ds[b*T:(b+1)*T,(I+n)*T:(I+n+1)*T].astype(f32)
        for n in range(3): near_ref[h,:,n*T:(n+1)*T]=near[n]
        dq=jnp.concatenate(dq,axis=0)
        dqs.append(dq[:,:128])
        far=dq[:,128:]
        ib=rows//T
        far_ref[h,0:1,:]=jnp.sum(jnp.where(lanes<=ib-2,far,0.0),axis=0,keepdims=True)
        far_ref[h,1:2,:]=jnp.sum(jnp.where((lanes>=ib+2)&(lanes<nblk),far,0.0),axis=0,keepdims=True)
        far_ref[h,2:8,:]=jnp.zeros((6,128),f32)
        if form=="T":
            dks.append(dg(qT[h*64:(h+1)*64],ds_ref[...],NN))
            dvs.append(dg(doT[h*64:(h+1)*64],p_ref[h],NN))
        else:
            dks.append(dg(ds_ref[...],q,TN))
            dvs.append(dg(p_ref[h],do,TN))
    dq_ref[...]=(jnp.where(masks[0],dqs[0],dqs[1])*scale).astype(bf)
    if form=="T":
        dk_ref[...]=(jnp.concatenate(dks,axis=0)*kscale).T.astype(bf)
        dv_ref[...]=jnp.concatenate(dvs,axis=0).T.astype(bf)
    else:
        dk_ref[...]=(jnp.where(masks[0],dks[0],dks[1])*kscale).astype(bf)
        dv_ref[...]=jnp.where(masks[0],dvs[0],dvs[1]).astype(bf)
def attn_bwd(qkv,gm,mixed,linv,p,BQ=128,form="T",scale=0.125,kscale=1.0):
    S,W=qkv.shape; npair=W//3//128; D=W//3
    blk=lambda o: pl.BlockSpec((S,128),lambda i:(0,o*npair+i))
    return pl.pallas_call(functools.partial(bwd_kernel,BQ,S,form,scale,kscale),grid=(npair,),
        in_specs=[blk(0),blk(1),blk(2),blk(0),blk(0),blk(0),pl.BlockSpec((2,S,S),lambda i:(i,0,0))],
        out_specs=[blk(0),blk(0),blk(0),pl.BlockSpec((2,T,3*T),lambda i:(i,0,0)),pl.BlockSpec((2,8,128),lambda i:(i,0,0))],
        out_shape=[jax.ShapeDtypeStruct((S,D),bf)]*3+[jax.ShapeDtypeStruct((2*npair,T,3*T),f32),jax.ShapeDtypeStruct((2*npair,8,128),f32)],
        scratch_shapes=[pltpu.VMEM((S,S),bf)],
        compiler_params=pltpu.CompilerParams(vmem_limit_bytes=56*2**20),
        )(qkv,qkv,qkv,gm,mixed,linv,p)
def dg(a,b,d=NN): return lax.dot_general(a,b,d,preferred_element_type=f32)
QB,VB,OB,G1,S1,DB,G2,S2,SW,UB=0,1,2,3,4,5,6,7,8,9
def gelu_both(x,mode="poly"):
    e=jnp.exp(x*x*-0.5)
    if mode=="erf":
        cdf=0.5*(1.0+lax.erf(x*0.7071067811865476))
    else:
        t=1.0/(1.0+(0.3275911*0.7071067811865476)*jnp.abs(x))
        q=t*(0.127414796+t*(-0.142248368+t*(0.7107068705+t*(-0.7265760135+t*0.5307027145))))*e
        cdf=jnp.where(x>=0,1.0-q,q)
    return x*cdf, cdf+x*e*0.3989422804014327
def norm(r):
    c=r-jnp.mean(r,axis=-1,keepdims=True)
    s=lax.rsqrt(jnp.mean(c*c,axis=-1,keepdims=True)+1e-05)
    return c*s,s
def norm_bwd(up,u,s,g):
    p=up*g
    return (p-jnp.mean(p,axis=-1,keepdims=True)-u*jnp.mean(p*u,axis=-1,keepdims=True))*s
def whole(a): return pl.BlockSpec(memory_space=pltpu.VMEM)
def qkv_kernel(TR,hid_ref,w_ref,vec_ref,o_ref):
    D=hid_ref.shape[1]
    x=hid_ref[...]
    o_ref[:,:D]=((dg(x,w_ref[:,:D])+vec_ref[QB:QB+1,:])*0.125).astype(bf)
    o_ref[:,D:2*D]=dg(x,w_ref[:,D:2*D]).astype(bf)
    o_ref[:,2*D:]=(dg(x,w_ref[:,2*D:])+vec_ref[VB:VB+1,:]).astype(bf)
def qkv_fwd(hid,w,vec,TR=256):
    R,D=hid.shape;N=w.shape[1]
    return pl.pallas_call(functools.partial(qkv_kernel,TR),grid=(R//TR,),
        in_specs=[pl.BlockSpec((TR,D),lambda i:(i,0)),pl.BlockSpec((D,N),lambda i:(0,0)),pl.BlockSpec(vec.shape,lambda i:(0,0))],
        out_specs=pl.BlockSpec((TR,N),lambda i:(i,0)),out_shape=jax.ShapeDtypeStruct((R,N),bf),
        compiler_params=pltpu.CompilerParams(vmem_limit_bytes=56*2**20))(hid,w,vec)
def post_kernel(TR,mode,len_ref,mix_ref,hid_ref,ow_ref,uw_ref,dw_ref,vec_ref,lo_ref,u1_ref,u2_ref,sc_ref,nl_ref,act_ref,gp_ref,fr_ref):
    D=hid_ref.shape[1];F=uw_ref.shape[1]
    i=pl.program_id(0)
    vec=lambda n: vec_ref[n:n+1,:]
    r=hid_ref[...].astype(f32)+(dg(mix_ref[...],ow_ref[...])+vec(OB))
    u1,s1=norm(r)
    u1_ref[...]=u1
    n=u1*vec(G1)+vec(S1)
    nl=n.astype(bf)
    nl_ref[...]=nl
    br=None
    for c in range(F//D):
        x=dg(nl,uw_ref[:,c*D:(c+1)*D])+vec(UB+c)
        a,gp=gelu_both(x,mode)
        a=a.astype(bf)
        act_ref[:,c*D:(c+1)*D]=a
        gp_ref[:,c*D:(c+1)*D]=gp.astype(bf)
        b=dg(a,dw_ref[c*D:(c+1)*D,:])
        br=b if br is None else br+b
    u2,s2=norm(n+(br+vec(DB)))
    u2_ref[...]=u2
    fin=u2*vec(G2)+vec(S2)
    row=lax.broadcasted_iota(jnp.int32,(TR,D),0)+i*TR
    lo_ref[...]=jnp.where(row<len_ref[0],fin,0.0).astype(bf)
    lane=lax.broadcasted_iota(jnp.int32,(TR,128),1)
    sc_ref[...]=jnp.where(lane==0,s1,s2)
    @pl.when(i==0)
    def _():
        fr_ref[...]=fin[:8]
def post_fwd(length,mixed,hid,ow,uw,dw,vec,TR=256,mode="poly"):
    R,D=hid.shape;F=uw.shape[1]
    rb=lambda n: pl.BlockSpec((TR,n),lambda i:(i,0))
    cb=lambda a: pl.BlockSpec(a.shape,lambda i:(0,0))
    sd=jax.ShapeDtypeStruct
    return pl.pallas_call(functools.partial(post_kernel,TR,mode),grid=(R//TR,),
        in_specs=[pl.BlockSpec(memory_space=pltpu.SMEM),rb(D),rb(D),cb(ow),cb(uw),cb(dw),cb(vec)],
        out_specs=[rb(D),rb(D),rb(D),rb(128),rb(D),rb(F),rb(F),pl.BlockSpec((8,D),lambda i:(0,0))],
        out_shape=[sd((R,D),bf),sd((R,D),f32),sd((R,D),f32),sd((R,128),f32),sd((R,D),bf),sd((R,F),bf),sd((R,F),bf),sd((8,D),f32)],
        compiler_params=pltpu.CompilerParams(vmem_limit_bytes=60*2**20))(length,mixed,hid,ow,uw,dw,vec)
def pbwd_kernel(TR,len_ref,gs_ref,og_ref,u1_ref,u2_ref,sc_ref,mix_ref,nl_ref,act_ref,gp_ref,ow_ref,uw_ref,dw_ref,vec_ref,
                gr1_ref,gm_ref,vg_ref,ddw_ref,duw_ref,dow_ref, gb_s,gi_s,ga_s,mix_s,nl_s,act_s):
    D=og_ref.shape[1];F=uw_ref.shape[1]
    i=pl.program_id(0);n=pl.num_programs(0)
    vec=lambda k: vec_ref[k:k+1,:]
    row=lax.broadcasted_iota(jnp.int32,(TR,D),0)+i*TR
    gf=og_ref[...].astype(f32)
    gf=gf+jnp.where(row==0,gs_ref[0]*vec(SW),0.0)
    gf=jnp.where(row<len_ref[0],gf,0.0)
    @pl.when(i==0)
    def _(): vg_ref[...]=jnp.zeros_like(vg_ref)
    def add(k,v): vg_ref[k:k+1,:]+=jnp.sum(v,axis=0,keepdims=True)
    u2=u2_ref[...]; s1=sc_ref[:,0:1]; s2=sc_ref[:,1:2]
    add(G2,gf*u2); add(S2,gf)
    gr2=norm_bwd(gf,u2,s2,vec(G2))
    gb=gr2.astype(bf)
    here=pl.ds(pl.multiple_of(i*TR,TR),TR)
    gb_s[here,:]=gb; mix_s[here,:]=mix_ref[...]; nl_s[here,:]=nl_ref[...]; act_s[here,:]=act_ref[...]
    add(DB,gb.astype(f32))
    gn=gr2
    for c in range(F//D):
        ga=dg(gb,dw_ref[c*D:(c+1)*D,:],NT)
        gi=(ga*gp_ref[:,c*D:(c+1)*D].astype(f32)).astype(bf)
        gi_s[here,c*D:(c+1)*D]=gi
        add(UB+c,gi.astype(f32))
        gn=gn+dg(gi,uw_ref[:,c*D:(c+1)*D],NT)
    u1=u1_ref[...]
    add(G1,gn*u1); add(S1,gn)
    gr1=norm_bwd(gn,u1,s1,vec(G1))
    gr1_ref[...]=gr1
    ga=gr1.astype(bf)
    ga_s[here,:]=ga
    add(OB,ga.astype(f32))
    gm_ref[...]=dg(ga,ow_ref[...],NT).astype(bf)
    @pl.when(i==n-1)
    def _():
        gball=gb_s[...]
        for c in range(F//D):
            ddw_ref[c*D:(c+1)*D,:]=dg(act_s[:,c*D:(c+1)*D],gball,TN).astype(ddw_ref.dtype)
        nlall=nl_s[...]
        for c in range(F//D):
            duw_ref[:,c*D:(c+1)*D]=dg(nlall,gi_s[:,c*D:(c+1)*D],TN).astype(duw_ref.dtype)
        dow_ref[...]=dg(mix_s[...],ga_s[...],TN).astype(dow_ref.dtype)
def post_bwd(length,gs,og,u1,u2,sc,mixed,nl,act,gp,ow,uw,dw,vec,TR=256):
    R,D=og.shape;F=uw.shape[1]
    rb=lambda n: pl.BlockSpec((TR,n),lambda i:(i,0))
    cb=lambda a: pl.BlockSpec(a.shape,lambda i:(0,0),pipeline_mode=pl.Buffered(1))
    sd=jax.ShapeDtypeStruct
    sm=pl.BlockSpec(memory_space=pltpu.SMEM)
    return pl.pallas_call(functools.partial(pbwd_kernel,TR),grid=(R//TR,),
        in_specs=[sm,sm,rb(D),rb(D),rb(D),rb(128),rb(D),rb(D),rb(F),rb(F),cb(ow),cb(uw),cb(dw),cb(vec)],
        out_specs=[rb(D),rb(D),cb(sd((16,D),f32)),cb(sd((F,D),f32)),cb(sd((D,F),f32)),cb(sd((D,D),f32))],
        out_shape=[sd((R,D),f32),sd((R,D),bf),sd((16,D),f32),sd((F,D),bf),sd((D,F),bf),sd((D,D),bf)],
        scratch_shapes=[pltpu.VMEM((R,D),bf),pltpu.VMEM((R,F),bf),pltpu.VMEM((R,D),bf),pltpu.VMEM((R,D),bf),pltpu.VMEM((R,D),bf),pltpu.VMEM((R,F),bf)],
        compiler_params=pltpu.CompilerParams(vmem_limit_bytes=62*2**20))(length,gs,og,u1,u2,sc,mixed,nl,act,gp,ow,uw,dw,vec)
def dqkv_kernel(TR,hid_ref,gq_ref,gk_ref,gv_ref,gr1_ref,w_ref,hg_ref,dw_ref,vb_ref,x_s,g_s):
    D=hid_ref.shape[1]
    i=pl.program_id(0);n=pl.num_programs(0)
    here=pl.ds(pl.multiple_of(i*TR,TR),TR)
    x_s[here,:]=hid_ref[...]
    acc=gr1_ref[...]
    @pl.when(i==0)
    def _(): vb_ref[...]=jnp.zeros_like(vb_ref)
    for c,r in enumerate((gq_ref,gk_ref,gv_ref)):
        g=r[...]
        g_s[here,c*D:(c+1)*D]=g
        acc=acc+dg(g,w_ref[:,c*D:(c+1)*D],NT)
        if c!=1: vb_ref[c//2:c//2+1,:]+=jnp.sum(g.astype(f32),axis=0,keepdims=True)
    hg_ref[...]=acc.astype(bf)
    @pl.when(i==n-1)
    def _():
        x=x_s[...]
        for c in range(3):
            dw_ref[:,c*D:(c+1)*D]=dg(x,g_s[:,c*D:(c+1)*D],TN).astype(bf)
def dqkv(hid,gq,gk,gv,gr1,w,TR=256):
    R,D=hid.shape;N=w.shape[1]
    rb=lambda n: pl.BlockSpec((TR,n),lambda i:(i,0))
    sd=jax.ShapeDtypeStruct
    return pl.pallas_call(functools.partial(dqkv_kernel,TR),grid=(R//TR,),
        in_specs=[rb(D)]*5+[pl.BlockSpec((D,N),lambda i:(0,0))],
        out_specs=[rb(D),pl.BlockSpec((D,N),lambda i:(0,0)),pl.BlockSpec((8,D),lambda i:(0,0))],
        out_shape=[sd((R,D),bf),sd((D,N),bf),sd((8,D),f32)],
        scratch_shapes=[pltpu.VMEM((R,D),bf),pltpu.VMEM((R,N),bf)],
        compiler_params=pltpu.CompilerParams(vmem_limit_bytes=60*2**20))(hid,gq,gk,gv,gr1,w)

def listwise(scores, weights, counts):
    slots = scores.shape[1]
    live = jnp.arange(slots, dtype=jnp.float32)[None, :] < counts[:, None]
    share = jnp.where(live, weights, 0.0)
    target = share / jnp.sum(share, axis=1, keepdims=True)
    masked = jnp.where(live, scores, -1e30)
    top = jnp.max(masked, axis=1, keepdims=True)
    lognorm = top + jnp.log(jnp.sum(jnp.exp(masked - top), axis=1, keepdims=True))
    entropy = lognorm[:, 0] - jnp.sum(target * scores, axis=1)
    probs = jnp.where(live, jnp.exp(masked - lognorm), 0.0)
    return (entropy, probs - target)


def shards(hidden, lengths, counts, targets, out_grad, qkv_weight, qv_bias, out_weight, out_bias,
           norm1_gain, norm1_bias, up_weight, up_bias, down_weight, down_bias, norm2_gain,
           norm2_bias, rel_bias, score_weight):
    ALL = ("pb", "col")
    _, _, S, D = hidden.shape
    n_dev = lax.axis_size(ALL)
    dev = lax.axis_index(ALL)
    d1 = D // n_dev
    tokens = hidden.reshape(S, D)
    length = lengths.reshape(1)
    small = jnp.concatenate([qv_bias.reshape(-1), out_bias, norm1_gain, norm1_bias, down_bias, norm2_gain, norm2_bias, score_weight, up_bias])
    small = lax.all_gather(small, ALL, axis=0)
    body = small[:, : 9 * d1].reshape(n_dev, 9, d1).transpose(1, 0, 2).reshape(9, D)
    ups = small[:, 9 * d1 :].reshape(-1, D)
    vec = jnp.concatenate([body, ups, jnp.zeros((16 - 9 - ups.shape[0], D), body.dtype)], axis=0).astype(f32)
    gather = lambda w: lax.all_gather(w, ALL, axis=0, tiled=True)
    qkv_w, out_w, up_w, down_w = map(gather, (qkv_weight, out_weight, up_weight, down_weight))
    strips, kx = tables(rel_bias, length[0], S)
    qkv = qkv_fwd(tokens, qkv_w, vec)
    mixed, linv, mixed_f, probs = attn_fwd(qkv, kx, strips, BQ=512)
    layer_out, u1, u2, sc, nl, act, gp, first = post_fwd(length, mixed, tokens, out_w, up_w, down_w, vec, mode="erf")
    own_score = jnp.sum(first[0] * vec[SW])
    count_f = counts.astype(f32)
    near_scores = lax.all_gather(own_score.reshape(1, 1), "col", axis=1, tiled=True)
    near_targets = lax.all_gather(targets, "col", axis=1, tiled=True)
    entropy, difference = listwise(near_scores, near_targets, count_f)
    weighted, total_count = lax.psum((count_f[0] * entropy[0], count_f[0]), "pb")
    loss = weighted / total_count
    gs = lax.dynamic_slice_in_dim(count_f[0] / total_count * difference[0], lax.axis_index("col"), 1)
    gr1, gm, vg, d_down, d_up, d_out = post_bwd(length, gs, out_grad.reshape(S, D), u1, u2, sc, mixed, nl, act, gp, out_w, up_w, down_w, vec)
    dq, dk, dv, near, far = attn_bwd(qkv, gm, mixed_f, linv, probs, BQ=512)
    hidden_grad, d_qkv, vb = dqkv(tokens, dq, dk, dv, gr1, qkv_w)
    ids = strip_ids()
    onehot = (ids[:, :, None] == jnp.arange(rel_bias.shape[0], dtype=jnp.int32)).astype(f32)
    bucket = jnp.einsum("hac,acb->bh", near, onehot, precision=lax.Precision.HIGHEST)
    far = jnp.sum(far, axis=2)
    bucket = bucket.at[15].add(far[:, 0]).at[31].add(far[:, 1])
    scatter = lambda w: lax.psum_scatter(w, ALL, scatter_dimension=0, tiled=True).astype(f32)
    d_down, d_up, d_out, d_qkv = map(scatter, (d_down, d_up, d_out, d_qkv))
    score_grad = gs[0] * first[:1]
    smalls = lax.psum(jnp.concatenate([vg, vb[:2], score_grad], axis=0), ALL)
    bucket = lax.psum(bucket, ALL)
    part = lax.dynamic_slice_in_dim(smalls, dev * d1, d1, axis=1)
    f1 = up_bias.shape[0]
    up_bias_grad = lax.dynamic_slice_in_dim(smalls[UB : UB + 4].reshape(-1), dev * f1, f1)
    return (layer_out.reshape(hidden.shape), loss, hidden_grad.reshape(hidden.shape), d_qkv, part[16:18],
            d_out, part[OB], part[G1], part[S1], d_up, up_bias_grad, d_down, part[DB], part[G2], part[S2],
            bucket, part[18])


def solution(mesh):
    lead = P(("pb", "col"))
    row = P(("pb", "col"), None)
    act = P("pb", "col", None, None)
    side = P(None, ("pb", "col"))
    return jax.shard_map(
        shards,
        mesh=mesh,
        in_specs=(act, P("pb", "col"), P("pb"), P("pb", "col"), act, row, side, row, lead, lead, lead, row, lead, row, lead, lead, lead, P(), lead),
        out_specs=(act, P(), act, row, side, row, lead, lead, lead, row, lead, row, lead, lead, lead, P(), lead),
        check_vma=False,
    )
```

time: 982 us -> 801 us (0.82)
  matrix products: 344 us -> 5.7 us
  waiting for transfers between devices: 275 us -> 489 us
  Pallas kernels: 0 us -> 138 us
  other arithmetic: 94 us -> 18 us
  local copies, waits for them, and re-layouts: 88.4 us -> 15.8 us
  blocking collectives: 148 us -> 108 us
    dot_general x27 -> x2, matrix products: 344 us -> 5.7 us  [the longest x1 3.98 us: shards(): jnp.einsum('hac,acb->bh', near, onehot, precision=lax.Precision.HIGHEST)]
    all_gather x4, waiting for transfers between devices: 0.05 us -> 156 us  [shards(): gather = lambda w: lax.all_gather(w, ALL, axis=0, tiled=True)]
    pallas_call x0 -> x6, Pallas kernels: none -> 138 us  [the longest x1 39.2 us: post_bwd(): pl.pallas_call(functools.partial(pbwd_kernel, TR), grid=(R // TR,), in_sp...]
    reduce_scatter x3 -> x4, waiting for transfers between devices: 272 us -> 328 us  [shards(): lax.psum_scatter(w, ALL, scatter_dimension=0, tiled=True).astype(f32)]
    all_gather x1 -> x0, blocking collectives: 43 us -> none  [shards(): lax.all_gather(qv_bias, ('pb', 'col'), axis=1, tiled=True)]
    dot_general x1, local copies, waits for them, and re-layouts: 44.5 us -> 2.25 us  [tables(): strips = jnp.einsum('bac,bh->hac', oh, rel_bias, preferred_element_type=f32)]
    psum x0 -> x1, blocking collectives: none -> 37.8 us  [shards(): smalls = lax.psum(jnp.concatenate([vg, vb[:2], score_grad], axis=0), ALL)]
    convert_element_type x12 -> x7, other arithmetic: 45.1 us -> 10.4 us  [the longest x4 6.29 us: shards(): lax.psum_scatter(w, ALL, scatter_dimension=0, tiled=True).astype(f32)]
  transfers between devices with their start and end apart: 8 -> 8, of which waited for: 2 -> 8; matrix products, arithmetic and copies ran while one was open for 43% -> 4% of each run, Pallas kernels for 0% -> 9%
where the time goes in v1:
time: 801 us; the launch traced here: 796 us
  waiting for transfers between devices  489 us (61%)
  Pallas kernels  138 us (17%)
  blocking collectives  108 us (13%)
  between operations  22 us (3%)
  other arithmetic  18 us (2%)
  local copies, waits for them, and re-layouts  15.8 us (2%)
    reduce_scatter x4, waiting for transfers between devices, shards(): lax.psum_scatter(w, ALL, scatter_dimension=0, tiled=True).astype(f32)  328 us
    all_gather x4, waiting for transfers between devices, shards(): gather = lambda w: lax.all_gather(w, ALL, axis=0, tiled=True)  156 us
    unnamed x2, blocking collectives  49.4 us
    pallas_call x1, Pallas kernels, post_bwd(): pl.pallas_call(functools.partial(pbwd_kernel, TR), grid=(R // TR,), in_sp...  39.2 us
    psum x1, blocking collectives, shards(): smalls = lax.psum(jnp.concatenate([vg, vb[:2], score_grad], axis=0), ALL)  37.8 us
    pallas_call x1, Pallas kernels, attn_bwd(): pl.pallas_call(functools.partial(bwd_kernel, BQ, S, form, scale, kscale),...  28.5 us
    pallas_call x1, Pallas kernels, post_fwd(): pl.pallas_call(functools.partial(post_kernel, TR, mode), grid=(R // TR,),...  24.2 us
    pallas_call x1, Pallas kernels, attn_fwd(): pl.pallas_call(functools.partial(fwd_kernel, BQ, S), grid=(npair,), in_sp...  24.1 us
  transfers between devices with their start and end apart: 8, of which 8 were waited for; matrix products, arithmetic and copies ran while one was open for 4% of the time, Pallas kernels for 9%

profile of v1, /device:TPU:0, one launch (start us, length us, event | category | flops | bytes accessed | tf_op | source)
XLA Modules:
  0.0 796.3 jit_solution(12232573689035450399)
XLA Ops:
  10.8 5.4 concatenate.13
  16.5 42.5 %all-reduce = bf16[9984]{0:T(1024)(128)(2,1)S(1)} all-reduce(bf16[9984]{0:T(1024)(128)(2,1)S(1)} %dynamic-update-slice.6), channel_id=2, replica_groups=mesh['pb'=8,'col'=4] {'pb','col'}, use_global_device_ids=true, to_apply=%add | all-reduce | flops 9984 | bytes 39936
  61.3 1.7 fusion
  63.0 2.3 copy.70
  69.5 2.7 select_convert_fusion.kx_ref
  72.2 1.7 all-gather.6.cloned.1.call-done.w_ref
  73.9 7.8 shard_map.314.q_ref.k_ref.v_ref
  81.7 24.1 %shard_map.315 = (bf16[1024,768]{1,0:T(8,128)(2,1)}, f32[1024,768]{1,0:T(8,128)}, f32[1024,768]{1,0:T(8,128)}, bf16[12,1024,1024]{2,1,0:T(8,128)(2,1)}) custom-call(bf16[1024,2304]{1,0:T(8,128)(2,1)} %shard_map.314.q_ref.k_ref.v_ref, bf16[1024,2304]{1,0:T(8,128)(2,1)} %shard_map.314.q_ref.k_ref.v_ref, bf16[1024,2304]{1,0:T(8,128)(2,1)} %shard_map.314.q_ref.k_ref.v_ref, ...), custom_call_target="tpu_custom_call" | custom-call | tf_op jit(solution)/shard_map/pallas_call | solution.py:73
  105.8 23.8 %all-gather.8.cloned.1.call-done.ow_ref = bf16[768,768]{1,0:T(8,128)(2,1)} async-done(((bf16[24,768]{1,0:T(8,128)(2,1)}), bf16[768,768]{1,0:T(8,128)(2,1)}) %all-gather.8.cloned.1.call-update) | async-done | bytes 1179664 | tf_op jit(solution)/shard_map/all_gather | solution.py:328
  129.6 65.5 %all-gather.10.cloned.1.call-done.uw_ref = bf16[768,3072]{1,0:T(8,128)(2,1)} async-done(((bf16[24,3072]{1,0:T(8,128)(2,1)}), bf16[768,3072]{1,0:T(8,128)(2,1)}) %all-gather.10.cloned.1.call-update) | async-done | bytes 4718608 | tf_op jit(solution)/shard_map/all_gather | solution.py:328
  195.2 65.2 %all-gather.12.cloned.1.call-done.dw_ref = bf16[3072,768]{1,0:T(8,128)(2,1)} async-done(((bf16[96,768]{1,0:T(8,128)(2,1)}), bf16[3072,768]{1,0:T(8,128)(2,1)}) %all-gather.12.cloned.1.call-update) | async-done | bytes 4718608 | tf_op jit(solution)/shard_map/all_gather | solution.py:328
  260.4 24.2 %shard_map.316 = (bf16[1024,768]{1,0:T(8,128)(2,1)}, f32[1024,768]{1,0:T(8,128)}, f32[1024,768]{1,0:T(8,128)}, f32[1024,128]{1,0:T(8,128)}, bf16[1024,768]{1,0:T...) custom-call(s32[1]{0:T(128)} %bitcast.67.len_ref, ...), custom_call_target="tpu_custom_call" | custom-call | tf_op jit(solution)/shard_map/pallas_call | solution.py:210
  287.4 6.9 all-reduce.5
  295.5 1.9 fusion.32
  299.4 20.6 %all-reduce.4 = (f32[]{:T(128)}, f32[]{:T(128)}) all-reduce(f32[]{:T(128)S(6)} %mul.34, f32[]{:T(128)} %bitcast.8), channel_id=1, replica_groups=mesh['pb'=8,'col'=4] {'pb'}, use_global_device_ids=true, to_apply=%region_5.6 | all-reduce | flops 2 | bytes 16 | tf_op jit(solution)/shard_map/psum | solution.py:339
  321.9 39.2 %shard_map.317 = (f32[1024,768]{1,0:T(8,128)}, bf16[1024,768]{1,0:T(8,128)(2,1)}, f32[16,768]{1,0:T(8,128)}, bf16[3072,768]{1,0:T(8,128)(2,1)}, bf16[768,3072]{1,0:T(8,128)(2,1)}, /*index=5*/bf16[768,768]{1,0:T(8,128)(2,1)}) custom-call(s32[1]{0:T(128)} %bitcast.68.len_ref, f32[1]{0:T(128)} %bitcast.14.gs_ref, bf16[1024,768]{1,0:T(8,128)(2,1)} %bitcast.74, ...), custom_call_target="tpu_custom_call" | custom-call | tf_op jit(solution)/shard_map/pallas_call | solution.py:264
  361.2 28.5 %shard_map.318 = (bf16[1024,768]{1,0:T(8,128)(2,1)}, bf16[1024,768]{1,0:T(8,128)(2,1)}, bf16[1024,768]{1,0:T(8,128)(2,1)}, f32[12,128,384]{2,1,0:T(8,128)}, f32[12,8,128]{2,1,0:T(8,128)}) custom-call(bf16[1024,2304]{1,0:T(8,128)(2,1)} %shard_map.314.q_ref.k_ref.v_ref, bf16[1024,2304]{1,0:T(8,128)(2,1)} %shard_map.314.q_ref.k_ref.v_ref, ...), custom_call_target="tpu_custom_call" | custom-call | tf_op jit(solution)/shard_map/pallas_call | solution.py:138
  389.7 14.4 %shard_map.319 = (bf16[1024,768]{1,0:T(8,128)(2,1)}, bf16[768,2304]{1,0:T(8,128)(2,1)}, f32[8,768]{1,0:T(8,128)}) custom-call(bf16[1024,768]{1,0:T(8,128)(2,1)} %bitcast.72, bf16[1024,768]{1,0:T(8,128)(2,1)} %get-tuple-element.80.gq_ref, bf16[1024,768]{1,0:T(8,128)(2,1)} %get-tuple-element.81.gk_ref, bf16[1024,768]{1,0:T(8,128)(2,1)} %get-tuple-element.82.gv_ref, ...), custom_call_target="tpu_custom_call" | custom-call | tf_op jit(solution)/shard_map/pallas_call | solution.py:293
  407.8 4.0 fusion.5
  413.6 37.8 %all-reduce.3 = (f32[19,768]{1,0:T(8,128)S(1)}, f32[32,12]{0,1:T(8,128)}) all-reduce(f32[19,768]{1,0:T(8,128)S(1)} %pad_maximum_fusion, f32[32,12]{0,1:T(8,128)S(1)} %scatter-add.9), channel_id=1, replica_groups=mesh['pb'=8,'col'=4] {'pb','col'}, use_global_device_ids=true, to_apply=%region_8.9 | all-reduce | flops 14976 | bytes 119808 | tf_op jit(solution)/shard_map/psum | solution.py:353
  456.2 106.2 %reduce-scatter.5.cloned.1.call-done = bf16[24,2304]{1,0:T(8,128)(2,1)} async-done(((bf16[768,2304]{1,0:T(8,128)(2,1)}), bf16[24,2304]{1,0:T(8,128)(2,1)}) %reduce-scatter.5.cloned.1.call-update) | async-done | bytes 110608 | tf_op jit(solution)/shard_map/reduce_scatter | solution.py:350
  564.0 109.8 %reduce-scatter.9.cloned.1.call-done = bf16[24,3072]{1,0:T(8,128)(2,1)} async-done(((bf16[768,3072]{1,0:T(8,128)(2,1)}), bf16[24,3072]{1,0:T(8,128)(2,1)}) %reduce-scatter.9.cloned.1.call-update) | async-done | bytes 147472 | tf_op jit(solution)/shard_map/reduce_scatter | solution.py:350
  673.8 1.6 convert_element_type.257
  675.4 110.8 %reduce-scatter.11.cloned.1.call-done = bf16[96,768]{1,0:T(8,128)(2,1)} async-done(((bf16[3072,768]{1,0:T(8,128)(2,1)}), bf16[96,768]{1,0:T(8,128)(2,1)}) %reduce-scatter.11.cloned.1.call-update) | async-done | bytes 147472 | tf_op jit(solution)/shard_map/reduce_scatter | solution.py:350
  (75 shorter events, 25.7 us)
Async XLA Ops:
  7.2 66.7 %all-gather.6.cloned.1.call-start = ((), (), s32[]{:S(2)}) async-start(), calls=%async_computation.4 | async-start | bytes 3649536 | tf_op jit(solution)/shard_map/all_gather | solution.py:328
  7.9 121.7 %all-gather.8.cloned.1.call-start = ((), (), s32[]{:S(2)}) async-start(), calls=%async_computation.5 | async-start | bytes 1216512 | tf_op jit(solution)/shard_map/all_gather | solution.py:328
  8.7 186.5 %all-gather.10.cloned.1.call-start = ((), (), s32[]{:S(2)}) async-start(), calls=%async_computation.6 | async-start | bytes 4866048 | tf_op jit(solution)/shard_map/all_gather | solution.py:328
  9.4 251.0 %all-gather.12.cloned.1.call-start = ((), (), s32[]{:S(2)}) async-start(), calls=%async_computation.7 | async-start | bytes 4866048 | tf_op jit(solution)/shard_map/all_gather | solution.py:328
  10.0 444.8 %reduce-scatter.7.cloned.1.call-start = ((), (), s32[]{:S(2)}) async-start(), calls=%async_computation.9 | async-start | bytes 1216512 | tf_op jit(solution)/shard_map/reduce_scatter | solution.py:350
  63.0 2.9 copy-start.3
  361.2 201.3 %reduce-scatter.5.cloned.1.call-start = ((), (), s32[]{:S(2)}) async-start(), calls=%async_computation.8 | async-start | bytes 3649536 | tf_op jit(solution)/shard_map/reduce_scatter | solution.py:350
  404.1 269.7 %reduce-scatter.9.cloned.1.call-start = ((), (), s32[]{:S(2)}) async-start(), calls=%async_computation.10 | async-start | bytes 4866048 | tf_op jit(solution)/shard_map/reduce_scatter | solution.py:350
  404.9 2.9 copy-start.2
  404.9 3.0 copy-start
  404.9 381.4 %reduce-scatter.11.cloned.1.call-start = ((), (), s32[]{:S(2)}) async-start(), calls=%async_computation.11 | async-start | bytes 4866048 | tf_op jit(solution)/shard_map/reduce_scatter | solution.py:350
  404.9 8.7 %copy-start.1 = (f32[16,768]{1,0:T(8,128)S(1)}, f32[16,768]{1,0:T(8,128)}, u32[]{:S(2)}) copy-start(f32[16,768]{1,0:T(8,128)} %get-tuple-element.86) | copy-start | bytes 147460
Sparse Core Ops, SparseCore 0:
  10.9 62.8 all-gather.5
  76.8 52.8 all-gather.7
  132.6 62.5 all-gather.9
  197.9 62.4 all-gather.11
  361.3 93.4 reduce-scatter.6
  460.1 102.2 reduce-scatter.4
  567.9 105.8 reduce-scatter.8
  680.2 106.0 reduce-scatter.10

commit v2 on v1

v2 whole, which is shorter than its diff:
```python
import functools

import jax
import jax.numpy as jnp
from jax import lax
from jax.experimental import pallas as pl
from jax.experimental.pallas import tpu as pltpu
from jax.sharding import PartitionSpec as P

f32=jnp.float32; bf=jnp.bfloat16
NT=(((1,),(1,)),((),())); NN=(((1,),(0,)),((),())); TN=(((0,),(0,)),((),()))
T=128
EDGES = (1, 2, 3, 4, 5, 6, 7, 8, 12, 16, 23, 32, 45, 64, 91)
def strip_ids():
    r=jnp.arange(3*T,dtype=jnp.int32)[None,:]-T-jnp.arange(T,dtype=jnp.int32)[:,None]
    m=jnp.abs(r); ids=jnp.where(r>0,16,0).astype(jnp.int32)
    for e in EDGES: ids=ids+(m>=e).astype(jnp.int32)
    return ids
def tables(rel_bias, length, S):
    ids=strip_ids()
    nb=rel_bias.shape[0]
    oh=(ids[None]==jnp.arange(nb,dtype=jnp.int32)[:,None,None]).astype(bf)
    strips=jnp.einsum("bac,bh->hac",oh,rel_bias,preferred_element_type=f32)
    j=jnp.arange(S,dtype=jnp.int32)[:,None]; lane=jnp.arange(128,dtype=jnp.int32)[None,:]
    jb=j//T; nblk=S//T
    low=(jb<=lane-2)&(lane<nblk); up=(jb>=lane+2)&(lane<nblk)
    mk=jnp.where((lane==nblk)&(j>=length),-1e30,0.0)
    rb=rel_bias.astype(f32)
    kx=jnp.where(low[None],rb[15][:,None,None],jnp.where(up[None],rb[31][:,None,None],mk[None])).astype(bf)
    return strips,kx
def fwd_kernel(BQ, S, q_ref,k_ref,v_ref,kx_ref,st_ref,mix_ref,linv_ref,mf_ref,p_ref):
    nblk=S//T
    lane=lax.broadcasted_iota(jnp.int32,(1,128),1)
    row=lax.broadcasted_iota(jnp.int32,(BQ,128),0)//T
    lane2=lax.broadcasted_iota(jnp.int32,(BQ,128),1)
    q=q_ref[...];k=k_ref[...];v=v_ref[...]
    masks=[lane<64,lane>=64]
    kaug=[jnp.concatenate([k,kx_ref[h]],axis=1) for h in (0,1)]
    vaug=[jnp.where(masks[h],v,jnp.ones_like(v)) for h in (0,1)]
    for i in range(S//BQ):
        outs=[]
        qi=q[i*BQ:(i+1)*BQ]
        qx=((lane2==nblk)|(lane2==row+i*(BQ//T))).astype(f32).astype(bf)
        for h in (0,1):
            qa=jnp.concatenate([jnp.where(masks[h],qi,jnp.zeros_like(qi)),qx],axis=1)
            s=dg(qa,kaug[h],NT)
            rows=[]
            for b in range(BQ//T):
                I=i*(BQ//T)+b
                lo=max(0,(I-1)*T);hi=min(S,(I+2)*T)
                sb=s[b*T:(b+1)*T]
                parts=[]
                if lo>0: parts.append(sb[:,:lo])
                parts.append(sb[:,lo:hi]+st_ref[h,:,lo-(I-1)*T:hi-(I-1)*T])
                if hi<S: parts.append(sb[:,hi:])
                rows.append(jnp.concatenate(parts,axis=1) if len(parts)>1 else parts[0])
            s=jnp.concatenate(rows,axis=0) if len(rows)>1 else rows[0]
            m=jnp.max(s,axis=1,keepdims=True)
            p=jnp.exp(s-m).astype(bf)
            p_ref[h,i*BQ:(i+1)*BQ,:]=p
            outs.append(dg(p,vaug[h],NN))
        o0,o1=outs
        num=jnp.where(masks[0],o0,o1)
        den=jnp.where(masks[0],o1,o0)
        den=pltpu.roll(den,64,1)
        linv=1.0/den
        mf=num*linv
        mf_ref[i*BQ:(i+1)*BQ,:]=mf
        mix_ref[i*BQ:(i+1)*BQ,:]=mf.astype(bf)
        linv_ref[i*BQ:(i+1)*BQ,:]=linv
def attn_fwd(qkv,kx,strips,p0,n,BQ=512):
    S,W=qkv.shape; npair=W//3//128
    blk=lambda o: pl.BlockSpec((S,128),lambda p:(0,o*npair+p0+p))
    out=pl.BlockSpec((S,128),lambda p:(0,p))
    return pl.pallas_call(functools.partial(fwd_kernel,BQ,S),cost_estimate=takes(n*FAST),grid=(n,),
        in_specs=[blk(0),blk(1),blk(2),pl.BlockSpec((2,S,128),lambda p:(p0+p,0,0)),pl.BlockSpec((2,T,3*T),lambda p:(p0+p,0,0))],
        out_specs=[out]*3+[pl.BlockSpec((2,S,S),lambda p:(p,0,0))],
        out_shape=[sd((S,n*128),bf),sd((S,n*128),f32),sd((S,n*128),f32),sd((2*n,S,S),bf)],
        compiler_params=pltpu.CompilerParams(vmem_limit_bytes=56*2**20),
        )(qkv,qkv,qkv,kx,strips)
def bwd_kernel(BQ,S,form,scale,kscale,q_ref,k_ref,v_ref,gm_ref,mf_ref,linv_ref,p_ref,dq_ref,dk_ref,dv_ref,near_ref,far_ref,ds_ref):
    nblk=S//T
    lane=lax.broadcasted_iota(jnp.int32,(1,128),1)
    lanes=lax.broadcasted_iota(jnp.int32,(S,128),1)
    rows=lax.broadcasted_iota(jnp.int32,(S,128),0)
    masks=[lane<64,lane>=64]
    q=q_ref[...];k=k_ref[...];v=v_ref[...]
    gm=gm_ref[...].astype(f32);linv=linv_ref[...]
    do=(gm*linv).astype(bf)
    t=do.astype(f32)*mf_ref[...]
    kind=(lanes==rows//T).astype(f32).astype(bf)
    kaug=jnp.concatenate([k,kind],axis=1)
    vx=jnp.where(lanes<2,1.0,0.0).astype(bf)
    vaug=jnp.concatenate([v,vx],axis=1)
    dqs=[];dks=[];dvs=[]
    if form=="T":
        qT=q.T; doT=do.T
    for h in (0,1):
        delta=jnp.sum(jnp.where(masks[h],t,0.0),axis=1,keepdims=True)
        hi=delta.astype(bf).astype(f32); lo=delta-hi
        ex=jnp.where(lanes==0,-hi,jnp.where(lanes==1,-lo,0.0)).astype(bf)
        da=jnp.concatenate([jnp.where(masks[h],do,jnp.zeros_like(do)),ex],axis=1)
        near=[jnp.zeros((T,T),f32) for _ in range(3)]
        dq=[]
        for i in range(S//BQ):
            x=dg(da[i*BQ:(i+1)*BQ],vaug,NT)
            ds=p_ref[h,i*BQ:(i+1)*BQ,:]*x.astype(bf)
            ds_ref[i*BQ:(i+1)*BQ,:]=ds
            dq.append(dg(ds,kaug,NN))
            for b in range(BQ//T):
                I=i*(BQ//T)+b
                for n in (-1,0,1):
                    if 0<=I+n<nblk:
                        near[n+1]=near[n+1]+ds[b*T:(b+1)*T,(I+n)*T:(I+n+1)*T].astype(f32)
        for n in range(3): near_ref[h,:,n*T:(n+1)*T]=near[n]
        dq=jnp.concatenate(dq,axis=0)
        dqs.append(dq[:,:128])
        far=dq[:,128:]
        ib=rows//T
        far_ref[h,0:1,:]=jnp.sum(jnp.where(lanes<=ib-2,far,0.0),axis=0,keepdims=True)
        far_ref[h,1:2,:]=jnp.sum(jnp.where((lanes>=ib+2)&(lanes<nblk),far,0.0),axis=0,keepdims=True)
        far_ref[h,2:8,:]=jnp.zeros((6,128),f32)
        if form=="T":
            dks.append(dg(qT[h*64:(h+1)*64],ds_ref[...],NN))
            dvs.append(dg(doT[h*64:(h+1)*64],p_ref[h],NN))
        else:
            dks.append(dg(ds_ref[...],q,TN))
            dvs.append(dg(p_ref[h],do,TN))
    dq_ref[...]=(jnp.where(masks[0],dqs[0],dqs[1])*scale).astype(bf)
    if form=="T":
        dk_ref[...]=(jnp.concatenate(dks,axis=0)*kscale).T.astype(bf)
        dv_ref[...]=jnp.concatenate(dvs,axis=0).T.astype(bf)
    else:
        dk_ref[...]=(jnp.where(masks[0],dks[0],dks[1])*kscale).astype(bf)
        dv_ref[...]=jnp.where(masks[0],dvs[0],dvs[1]).astype(bf)
def attn_bwd(qkv,gm,mixed,linv,p,p0,n,BQ=512,form="T",scale=0.125,kscale=1.0):
    S,W=qkv.shape; npair=W//3//128
    blk=lambda o: pl.BlockSpec((S,128),lambda i:(0,o*npair+p0+i))
    own=pl.BlockSpec((S,128),lambda i:(0,i))
    return pl.pallas_call(functools.partial(bwd_kernel,BQ,S,form,scale,kscale),cost_estimate=takes(n*FAST),grid=(n,),
        in_specs=[blk(0),blk(1),blk(2),blk(0),own,own,pl.BlockSpec((2,S,S),lambda i:(i,0,0))],
        out_specs=[own]*3+[pl.BlockSpec((2,T,3*T),lambda i:(i,0,0)),pl.BlockSpec((2,8,128),lambda i:(i,0,0))],
        out_shape=[sd((S,n*128),bf)]*3+[sd((2*n,T,3*T),f32),sd((2*n,8,128),f32)],
        scratch_shapes=[pltpu.VMEM((S,S),bf)],
        compiler_params=pltpu.CompilerParams(vmem_limit_bytes=56*2**20),
        )(qkv,qkv,qkv,gm,mixed,linv,p)
sd=jax.ShapeDtypeStruct
FAST=1.0
def takes(us): return pl.CostEstimate(flops=int(us*1.15e9),bytes_accessed=int(us*1e6),transcendentals=0)
def dg(a,b,d=NN): return lax.dot_general(a,b,d,preferred_element_type=f32)
QB,VB,OB,G1,S1,DB,G2,S2,SW,UB,CT,TG,NV=0,1,2,3,4,5,6,7,8,9,13,14,24
def gelu_both(x,mode="poly"):
    e=jnp.exp(x*x*-0.5)
    if mode=="erf":
        cdf=0.5*(1.0+lax.erf(x*0.7071067811865476))
    else:
        t=1.0/(1.0+(0.3275911*0.7071067811865476)*jnp.abs(x))
        q=t*(0.127414796+t*(-0.142248368+t*(0.7107068705+t*(-0.7265760135+t*0.5307027145))))*e
        cdf=jnp.where(x>=0,1.0-q,q)
    return x*cdf, cdf+x*e*0.3989422804014327
def norm(r):
    c=r-jnp.mean(r,axis=-1,keepdims=True)
    s=lax.rsqrt(jnp.mean(c*c,axis=-1,keepdims=True)+1e-05)
    return c*s,s
def norm_bwd(up,u,s,g):
    p=up*g
    return (p-jnp.mean(p,axis=-1,keepdims=True)-u*jnp.mean(p*u,axis=-1,keepdims=True))*s
def whole(a): return pl.BlockSpec(memory_space=pltpu.VMEM)

BLK=16
RELA=((0,0,0),(0,0,1),(0,1,0),(0,1,1))
RELB=((0,0,2),(0,0,3),(1,0,2),(1,0,3))
RELXA=((1,0,0),(1,0,1),(1,1,0),(1,1,1))
RELYB=((0,1,2),(0,1,3),(1,1,2),(1,1,3))
RELS=(RELA,RELB,RELXA,RELYB)
X_,Y_,Z_,C_=0,1,2,3
def place(pos,rel):
    xr,yr,zr=rel
    return (((pos[Z_]-zr)&3)*2+(pos[Y_]^yr))*2+(pos[X_]^xr)
def slot(pos,k):
    x,y,z=k&1,(k>>1)&1,k>>2
    xr,yr,zr=pos[X_]^x,pos[Y_]^y,(pos[Z_]-z)&3
    return jnp.where(zr<2,(1-xr)*8+yr*2+zr,2+(1-yr)*8+xr*2+zr)
def load(pos,pieces,parts,sem):
    for s in range(8):
        half=pos[C_] if s<4 else 1-pos[C_]
        for b,rel in enumerate(RELS[s%4]):
            k=place(pos,rel)
            R=pieces[s].shape[1]
            rows=pl.ds(pl.multiple_of(k*R,R),R)
            for off,w,dst in parts:
                cols=pl.ds(pl.multiple_of(half*w,w),w)
                pltpu.make_async_copy(pieces[s].at[b,:,pl.ds(off,w)],dst.at[rows,cols],sem).start()
def arrived(dst,sem):
    pltpu.make_async_copy(dst,dst,sem).wait()
ANYS=pl.BlockSpec(memory_space=pltpu.HBM)
SMEM=pl.BlockSpec(memory_space=pltpu.SMEM)
def qkv_kernel(pos,*refs):
    pieces=refs[:8]; hid_ref,o_ref,vec_ref,w_s,sm_s,sems=refs[8:]
    D=hid_ref.shape[1]; N=3*D
    @pl.when(pl.program_id(0)==0)
    def _():
        for s in range(4):
            for b,rel in enumerate(RELS[s]):
                R=pieces[s].shape[1]
                rows=pl.ds(pl.multiple_of(place(pos,rel)*R,R),R)
                pltpu.make_async_copy(pieces[s].at[b,:,pl.ds(N//2,128)],sm_s.at[rows,:],sems.at[1]).start()
        load(pos,pieces,[(0,N//2,w_s)],sems.at[0])
        arrived(sm_s,sems.at[1])
        vec_ref[...]=sm_s[...].astype(f32).T[:NV]
        arrived(w_s,sems.at[0])
    x=hid_ref[...]
    o_ref[:,:D]=((dg(x,w_s[:,:D])+vec_ref[QB:QB+1,:])*0.125).astype(bf)
    o_ref[:,D:2*D]=dg(x,w_s[:,D:2*D]).astype(bf)
    o_ref[:,2*D:]=(dg(x,w_s[:,2*D:])+vec_ref[VB:VB+1,:]).astype(bf)
def qkv_fwd(pos,pieces,hid,TR=256):
    R,D=hid.shape;N=3*D
    return pl.pallas_call(qkv_kernel,cost_estimate=takes(FAST),grid=(R//TR,),
        in_specs=[SMEM]+[ANYS]*8+[pl.BlockSpec((TR,D),lambda i:(i,0))],
        out_specs=[pl.BlockSpec((TR,N),lambda i:(i,0)),pl.BlockSpec((NV,D),lambda i:(0,0))],
        out_shape=[sd((R,N),bf),sd((NV,D),f32)],
        scratch_shapes=[pltpu.VMEM((D,N),bf),pltpu.VMEM((D,128),bf),pltpu.SemaphoreType.DMA((2,))],
        compiler_params=pltpu.CompilerParams(vmem_limit_bytes=56*2**20))(pos,*pieces,hid)
def fetch(w,off,dst,sem):
    pltpu.make_async_copy(w.at[:,pl.ds(off,dst.shape[1])],dst,sem).start()
def fetch_down(w,off,dst,sems):
    D=dst.shape[1]
    for j in range(dst.shape[0]//D):
        pltpu.make_async_copy(w.at[:,pl.ds(off+j*D,D)],dst.at[pl.ds(j*D,D),:],sems.at[j]).start()
def arrived_down(dst,sems):
    D=dst.shape[1]
    for j in range(dst.shape[0]//D):
        arrived(dst.at[pl.ds(j*D,D),:],sems.at[j])
def post_kernel(TR,mode,len_ref,*refs):
    w,m0,m1,m2,hid_ref,vec_ref,lo_ref,u1_ref,u2_ref,sc_ref,nl_ref,act_ref,gp_ref,fr_ref,os_ref,ow_ref,uw_ref,dw_ref,sems=refs
    D=hid_ref.shape[1];F=uw_ref.shape[1]
    i=pl.program_id(0)
    @pl.when(i==0)
    def _():
        fetch(w,0,ow_ref,sems.at[4])
        fetch(w,D,uw_ref,sems.at[5])
        fetch_down(w,D+F,dw_ref,sems)
        arrived(ow_ref,sems.at[4])
        arrived(uw_ref,sems.at[5])
        arrived_down(dw_ref,sems)
    vec=lambda n: vec_ref[n:n+1,:]
    r=hid_ref[...].astype(f32)+(dg(jnp.concatenate([m0[...],m1[...],m2[...]],axis=1),ow_ref[...])+vec(OB))
    u1,s1=norm(r)
    u1_ref[...]=u1
    n=u1*vec(G1)+vec(S1)
    nl=n.astype(bf)
    nl_ref[...]=nl
    br=None
    for c in range(F//D):
        x=dg(nl,uw_ref[:,c*D:(c+1)*D])+vec(UB+c)
        a,gp=gelu_both(x,mode)
        a=a.astype(bf)
        act_ref[:,c*D:(c+1)*D]=a
        gp_ref[:,c*D:(c+1)*D]=gp.astype(bf)
        b=dg(a,dw_ref[c*D:(c+1)*D,:])
        br=b if br is None else br+b
    u2,s2=norm(n+(br+vec(DB)))
    u2_ref[...]=u2
    fin=u2*vec(G2)+vec(S2)
    row=lax.broadcasted_iota(jnp.int32,(TR,D),0)+i*TR
    lo_ref[...]=jnp.where(row<len_ref[0],fin,0.0).astype(bf)
    lane=lax.broadcasted_iota(jnp.int32,(TR,128),1)
    sc_ref[...]=jnp.where(lane==0,s1,s2)
    @pl.when(i==0)
    def _():
        fr_ref[...]=fin[:8]
        own=jnp.sum(fin[:1]*vec(SW),axis=1,keepdims=True)
        os_ref[...]=jnp.broadcast_to(own,(8,128))
def post_fwd(length,w,mixed,hid,vec,TR=256,mode="erf"):
    R,D=hid.shape;F=4*D
    rb=lambda n: pl.BlockSpec((TR,n),lambda i:(i,0))
    cb=lambda a: pl.BlockSpec(a.shape,lambda i:(0,0))
    return pl.pallas_call(functools.partial(post_kernel,TR,mode),cost_estimate=takes(FAST),grid=(R//TR,),
        in_specs=[SMEM,ANYS]+[rb(m.shape[1]) for m in mixed]+[rb(D),cb(vec)],
        out_specs=[rb(D),rb(D),rb(D),rb(128),rb(D),rb(F),rb(F),pl.BlockSpec((8,D),lambda i:(0,0)),pl.BlockSpec((8,128),lambda i:(0,0))],
        out_shape=[sd((R,D),bf),sd((R,D),f32),sd((R,D),f32),sd((R,128),f32),sd((R,D),bf),sd((R,F),bf),sd((R,F),bf),sd((8,D),f32),sd((8,128),f32)],
        scratch_shapes=[pltpu.VMEM((D,D),bf),pltpu.VMEM((D,F),bf),pltpu.VMEM((F,D),bf),pltpu.SemaphoreType.DMA((6,))],
        compiler_params=pltpu.CompilerParams(vmem_limit_bytes=60*2**20))(length,w,*mixed,hid,vec)
def listwise(pos,ncol,d1,scores,vec_ref,info_ref):
    lane=lax.broadcasted_iota(jnp.int32,(1,vec_ref.shape[1]),1)
    pb,col=pos[4],pos[5]
    counts=vec_ref[CT:CT+1,:]
    targets=vec_ref[TG:TG+1,:]+vec_ref[TG+1:TG+2,:]+vec_ref[TG+2:TG+3,:]
    pick=lambda row,dev: jnp.sum(jnp.where(lane==dev*d1,row,0.0),axis=1,keepdims=True)
    total=jnp.sum(counts,axis=1,keepdims=True)*(1.0/ncol)
    mine=pick(counts,pb*ncol)
    n=len(scores)
    live=[(col^r).astype(f32)<mine for r in range(n)]
    share=[jnp.where(live[r],pick(targets,pb*ncol+(col^r)),0.0) for r in range(n)]
    def pairs(f,v):
        while len(v)>1: v=[f(v[i],v[i+1]) for i in range(0,len(v),2)]
        return v[0]
    add=lambda a,b: a+b
    whole=pairs(add,share)
    masked=[jnp.where(live[r],scores[r],-1e30) for r in range(n)]
    top=pairs(jnp.maximum,masked)
    log=top+jnp.log(pairs(add,[jnp.exp(m-top) for m in masked]))
    entropy=log-pairs(add,[share[r]/whole*scores[r] for r in range(n)])
    prob=jnp.where(live[0],jnp.exp(masked[0]-log),0.0)
    gs=mine/total*(prob-share[0]/whole)
    weighted=jnp.where(col==0,mine*entropy,0.0)
    row=lax.broadcasted_iota(jnp.int32,(8,128),0)
    info_ref[...]=jnp.where(row==0,gs,jnp.where(row==1,weighted,total))
def back1_kernel(TR,ncol,d1,pos,len_ref,*refs):
    s_refs=refs[:ncol]
    (w,og_ref,u2_ref,sc_ref,act_ref,gp_ref,vec_ref,gr2_ref,gi_ref,vg_ref,kb_ref,sb_ref,info_ref,
     dw_ref,gb_s,act_s,sems)=refs[ncol:]
    D=og_ref.shape[1];F=act_ref.shape[1];H=D//2
    i=pl.program_id(0);n=pl.num_programs(0)
    @pl.when(i==0)
    def _():
        fetch_down(w,D+F,dw_ref,sems)
        listwise(pos,ncol,d1,[r[0:1,0:1] for r in s_refs],vec_ref,info_ref)
        vg_ref[...]=jnp.zeros_like(vg_ref)
        arrived_down(dw_ref,sems)
    vec=lambda k: vec_ref[k:k+1,:]
    row=lax.broadcasted_iota(jnp.int32,(TR,D),0)+i*TR
    gf=og_ref[...].astype(f32)
    gf=gf+jnp.where(row==0,info_ref[0:1,0:1]*vec(SW),0.0)
    gf=jnp.where(row<len_ref[0],gf,0.0)
    def add(k,v): vg_ref[k:k+1,:]+=jnp.sum(v,axis=0,keepdims=True)
    u2=u2_ref[...]; s2=sc_ref[:,1:2]
    add(G2,gf*u2); add(S2,gf)
    gr2=norm_bwd(gf,u2,s2,vec(G2))
    gr2_ref[...]=gr2
    gb=gr2.astype(bf)
    here=pl.ds(pl.multiple_of(i*TR,TR),TR)
    gb_s[here,:]=gb; act_s[here,:]=act_ref[...]
    add(DB,gb.astype(f32))
    for c in range(F//D):
        ga=dg(gb,dw_ref[c*D:(c+1)*D,:],NT)
        gi=(ga*gp_ref[:,c*D:(c+1)*D].astype(f32)).astype(bf)
        gi_ref[:,c*D:(c+1)*D]=gi
        add(UB+c,gi.astype(f32))
    @pl.when(i==n-1)
    def _():
        gball=gb_s[...]
        core=pos[C_]
        slots=[slot(pos,k) for k in range(BLK)]
        for ref,h in ((sb_ref,1-core),(kb_ref,core)):
            for c in range(F//D//2):
                cols=pl.ds(pl.multiple_of(h*(F//2)+c*D,D),D)
                t=dg(act_s[:,cols],gball,TN).astype(bf)
                for k in range(BLK):
                    ref[slots[k],:,c*D:(c+1)*D]=t[k*(D//BLK):(k+1)*(D//BLK)]
def whole1(a): return pl.BlockSpec(a.shape,lambda i:(0,)*len(a.shape),pipeline_mode=pl.Buffered(1))
def back1(pos,length,scores,d1,w,og,u2,sc,act,gp,vec,TR=256):
    R,D=og.shape;F=act.shape[1]
    rb=lambda n: pl.BlockSpec((TR,n),lambda i:(i,0))
    gb=sd((BLK,D//BLK,F//2),bf)
    return pl.pallas_call(functools.partial(back1_kernel,TR,len(scores),d1),cost_estimate=takes(FAST),grid=(R//TR,),
        in_specs=[SMEM]*2+[whole1(v) for v in scores]+[ANYS]+[rb(D),rb(D),rb(128),rb(F),rb(F),whole1(vec)],
        out_specs=[rb(D),rb(F),whole1(vec),whole1(gb),whole1(gb),whole1(scores[0])],
        out_shape=[sd((R,D),f32),sd((R,F),bf),vec,gb,gb,sd((8,128),f32)],
        scratch_shapes=[pltpu.VMEM((F,D),bf),pltpu.VMEM((R,D),bf),pltpu.VMEM((R,F),bf),pltpu.SemaphoreType.DMA((4,))],
        compiler_params=pltpu.CompilerParams(vmem_limit_bytes=62*2**20))(pos,length,*scores,w,og,u2,sc,act,gp,vec)
def back2_kernel(TR,*refs):
    (w,gr2_ref,u1_ref,sc_ref,gi_ref,vec_ref,gr1_ref,ga_ref,gm_ref,vg_ref,ow_ref,uw_ref,sems)=refs
    D=gr2_ref.shape[1]
    i=pl.program_id(0)
    @pl.when(i==0)
    def _():
        fetch(w,D,uw_ref,sems.at[0])
        fetch(w,0,ow_ref,sems.at[1])
        vg_ref[...]=jnp.zeros_like(vg_ref)
        arrived(uw_ref,sems.at[0])
        arrived(ow_ref,sems.at[1])
    vec=lambda k: vec_ref[k:k+1,:]
    def add(k,v): vg_ref[k:k+1,:]+=jnp.sum(v,axis=0,keepdims=True)
    gn=gr2_ref[...]+dg(gi_ref[...],uw_ref[...],NT)
    u1=u1_ref[...]
    add(G1,gn*u1); add(S1,gn)
    gr1=norm_bwd(gn,u1,sc_ref[:,0:1],vec(G1))
    gr1_ref[...]=gr1
    ga=gr1.astype(bf)
    ga_ref[...]=ga
    add(OB,ga.astype(f32))
    gm_ref[...]=dg(ga,ow_ref[...],NT).astype(bf)
def back2(w,gr2,u1,sc,gi,vec,TR=256):
    R,D=gr2.shape;F=gi.shape[1]
    rb=lambda n: pl.BlockSpec((TR,n),lambda i:(i,0))
    return pl.pallas_call(functools.partial(back2_kernel,TR),cost_estimate=takes(FAST),grid=(R//TR,),
        in_specs=[ANYS,rb(D),rb(D),rb(128),rb(F),whole1(vec)],
        out_specs=[rb(D),rb(D),rb(D),whole1(vec)],
        out_shape=[sd((R,D),f32),sd((R,D),bf),sd((R,D),bf),vec],
        scratch_shapes=[pltpu.VMEM((D,D),bf),pltpu.VMEM((D,F),bf),pltpu.SemaphoreType.DMA((2,))],
        compiler_params=pltpu.CompilerParams(vmem_limit_bytes=56*2**20))(w,gr2,u1,sc,gi,vec)
def wup_kernel(pos,m0,m1,m2,ga_ref,nl_ref,gi_ref,ka_ref,sa_ref,tmp_s):
    D=ga_ref.shape[1];F=gi_ref.shape[1];H=D//2
    core=pos[C_]
    slots=[slot(pos,k) for k in range(BLK)]
    mine,other=[pl.ds(pl.multiple_of(h*H,H),H) for h in (core,1-core)]
    nlall=nl_ref[...]
    for ref,h in ((sa_ref,1-core),(ka_ref,core)):
        for c in range(F//D//2):
            cols=pl.ds(pl.multiple_of(h*(F//2)+c*D,D),D)
            t=dg(nlall,gi_ref[:,cols],TN).astype(bf)
            for k in range(BLK):
                ref[slots[k],:,H+c*D:H+(c+1)*D]=t[k*(D//BLK):(k+1)*(D//BLK)]
    tmp_s[...]=dg(jnp.concatenate([m0[...],m1[...],m2[...]],axis=1),ga_ref[...],TN).astype(bf)
    for k in range(BLK):
        rows=slice(k*(D//BLK),(k+1)*(D//BLK))
        ka_ref[slots[k],:,:H]=tmp_s[rows,mine]
        sa_ref[slots[k],:,:H]=tmp_s[rows,other]
VM=pl.BlockSpec(memory_space=pltpu.VMEM)
def wup(pos,mixed,ga,nl,gi):
    R,D=ga.shape;F=gi.shape[1]
    o=sd((BLK,D//BLK,(D+F)//2),bf)
    return pl.pallas_call(wup_kernel,cost_estimate=takes(FAST),in_specs=[SMEM]+[VM]*6,out_specs=[VM]*2,out_shape=[o,o],
        scratch_shapes=[pltpu.VMEM((D,D),bf)],
        compiler_params=pltpu.CompilerParams(vmem_limit_bytes=56*2**20))(pos,*mixed,ga,nl,gi)
def wqkv_kernel(pos,hid_ref,*refs):
    parts=refs[:9]; k_ref,s_ref,vb_ref,g_s=refs[9:]
    D=hid_ref.shape[1];N=3*D
    vb_ref[...]=jnp.zeros_like(vb_ref)
    w=parts[0].shape[1]
    for j,r in enumerate(parts):
        g=r[...]
        g_s[:,j*w:(j+1)*w]=g
        row,lane=j//3,(j%3)*w
        if row!=1: vb_ref[row//2:row//2+1,lane:lane+w]=jnp.sum(g.astype(f32),axis=0,keepdims=True)
    x=hid_ref[...]
    core=pos[C_]
    slots=[slot(pos,k) for k in range(BLK)]
    for ref,h in ((s_ref,1-core),(k_ref,core)):
        t=dg(x,g_s[:,pl.ds(pl.multiple_of(h*(N//2),N//2),N//2)],TN).astype(bf)
        for k in range(BLK):
            ref[slots[k]]=t[k*(D//BLK):(k+1)*(D//BLK)]
def wqkv(pos,hid,parts):
    R,D=hid.shape;N=3*D
    g=sd((BLK,D//BLK,N//2),bf)
    return pl.pallas_call(wqkv_kernel,cost_estimate=takes(FAST),
        in_specs=[SMEM]+[VM]*10,out_specs=[VM]*3,out_shape=[g,g,sd((8,D),f32)],
        scratch_shapes=[pltpu.VMEM((R,N),bf)],
        compiler_params=pltpu.CompilerParams(vmem_limit_bytes=60*2**20))(pos,hid,*parts)
def hgrad_kernel(pos,*refs):
    pieces=refs[:8]
    parts=refs[8:17]; gr1_ref,hg_ref,w_s,sems=refs[17:]
    D=gr1_ref.shape[1];N=3*D
    @pl.when(pl.program_id(0)==0)
    def _():
        load(pos,pieces,[(0,N//2,w_s)],sems.at[0])
        arrived(w_s,sems.at[0])
    g=jnp.concatenate([r[...] for r in parts],axis=1)
    hg_ref[...]=(gr1_ref[...]+dg(g,w_s[...],NT)).astype(bf)
def hgrad(pos,pieces,parts,gr1,TR=256):
    R,D=gr1.shape;N=3*D
    rb=lambda n: pl.BlockSpec((TR,n),lambda i:(i,0))
    return pl.pallas_call(hgrad_kernel,cost_estimate=takes(FAST),grid=(R//TR,),
        in_specs=[SMEM]+[ANYS]*8+[rb(p.shape[1]) for p in parts]+[rb(D)],
        out_specs=rb(D),out_shape=sd((R,D),bf),
        scratch_shapes=[pltpu.VMEM((D,N),bf),pltpu.SemaphoreType.DMA((1,))],
        compiler_params=pltpu.CompilerParams(vmem_limit_bytes=60*2**20))(pos,*pieces,*parts,gr1)

ALL=("pb","col")
def staged():
    return lax.axis_size("pb")==8 and lax.axis_size("col")==4
def swap_core(v): return lax.ppermute(v,"col",[(i,i^1) for i in range(4)])
def swap_col(v,k): return lax.ppermute(v,"col",[(i,i^k) for i in range(lax.axis_size("col"))])
def swap_x(v): return lax.ppermute(v,"col",[(i,i^2) for i in range(4)])
def swap_y(v): return lax.ppermute(v,"pb",[(i,i^1) for i in range(8)])
def flip_z(v,m): return lax.ppermute(v,"pb",[(i,i^(2*m)) for i in range(8)])
def shift_z(v,k): return lax.ppermute(v,"pb",[(i,(i+2*k)%8) for i in range(8)])
def cat(a): return jnp.concatenate(a,axis=0)
def after(v,*first):
    return lax.optimization_barrier((v,)+first)[0]
def spread1(block):
    o=block[None]
    return [o,shift_z(o,1),shift_z(o,2),shift_z(o,3)]
def spread2(v):
    a=cat(v[:2]);b=cat(v[2:])
    return [cat([a,swap_y(a)]),cat([b,swap_x(b)])]
def spread3(v):
    a,b=v
    return [a,b,swap_x(a),swap_y(b)]
def spread4(own):
    return own+[swap_core(v) for v in own]
def own_order():
    zero=(0,0,0,0)
    return [[place(zero,rel) for rel in rels] for rels in RELS]
def spread_plain(full):
    out=[]
    for half in (0,1):
        cols=jnp.concatenate([w.reshape(BLK,w.shape[0]//BLK,2,w.shape[1]//2)[:,:,half] for w in full],axis=2)
        for order in own_order():
            out.append(jnp.stack([cols[k] for k in order]))
    return out
def add2(a,b): return (a.astype(f32)+b.astype(f32)).astype(bf)
def collect1(keep,r):
    sa,sb,ka,kb=[add2(keep[4*s:4*s+4],r[4*s:4*s+4]) for s in range(4)]
    return ka,kb,swap_x(sa),swap_y(sb)
def collect2(ka,kb,ra,rb):
    ka2,sa2=add2(ka[:2],ra[:2]),add2(ka[2:],ra[2:])
    kb2,sb2=add2(kb[:2],rb[:2]),add2(kb[2:],rb[2:])
    return ka2,kb2,swap_y(sa2),swap_x(sb2)
def collect3(ka2,kb2,ra,rb):
    t0=ka2[0].astype(f32)+ra[0].astype(f32)
    t1=add2(ka2[1],ra[1])
    t2=add2(kb2[0],rb[0]);t3=add2(kb2[1],rb[1])
    return t0,shift_z(t1,3),shift_z(t2,2),shift_z(t3,1)
def collect4(t0,t1,t2,t3):
    t=t0+t1.astype(f32)+t2.astype(f32)+t3.astype(f32)
    c=lax.axis_index("col")&1
    h=t.shape[0]//2
    mine=lax.dynamic_slice_in_dim(t,c*h,h,0)
    other=swap_core(lax.dynamic_slice_in_dim(t,(1-c)*h,h,0).astype(bf)).astype(f32)
    return mine,other,c
def afters(vs,*first):
    return list(lax.optimization_barrier(tuple(vs)+tuple(first))[:len(vs)])
def sides(mine,other,c):
    return jnp.where(c==0,jnp.concatenate([mine,other],axis=1),jnp.concatenate([other,mine],axis=1))
def natural(keep,send):
    order=[int(v) for v in NATURAL]
    keep,send=[jnp.concatenate([v[k] for k in order],axis=0) for v in (keep,send)]
    return jnp.concatenate([keep,send],axis=1)
def slot0(k):
    xr,yr,zr=k&1,(k>>1)&1,(-(k>>2))&3
    return (1-xr)*8+yr*2+zr if zr<2 else 2+(1-yr)*8+xr*2+zr
NATURAL=[slot0(k) for k in range(BLK)]

def shards(hidden, lengths, counts, targets, out_grad, qkv_weight, qv_bias, out_weight, out_bias,
           norm1_gain, norm1_bias, up_weight, up_bias, down_weight, down_bias, norm2_gain,
           norm2_bias, rel_bias, score_weight):
    _, _, S, D = hidden.shape
    F = down_weight.shape[0] * lax.axis_size(ALL)
    n_dev = lax.axis_size(ALL)
    dev = lax.axis_index(ALL)
    d1, f1 = D // n_dev, F // n_dev
    tokens = hidden.reshape(S, D)
    length = lengths.reshape(1)
    fast = staged()
    count_f = counts.astype(f32)
    npb, ncol = lax.axis_size("pb"), lax.axis_size("col")
    pb, col = lax.axis_index("pb"), lax.axis_index("col")
    t1 = targets.astype(bf)
    t2 = (targets - t1.astype(f32)).astype(bf)
    t3 = (targets - t1.astype(f32) - t2.astype(f32)).astype(bf)
    columns = [qv_bias[0], qv_bias[1], out_bias, norm1_gain, norm1_bias, down_bias, norm2_gain, norm2_bias, score_weight]
    columns += [up_bias[j * d1 : (j + 1) * d1] for j in range(4)]
    lane = lax.broadcasted_iota(jnp.int32, (d1, 128), 1)
    panel = jnp.zeros((d1, 128), bf)
    for j, v in enumerate(columns):
        panel = jnp.where(lane == j, v[:, None], panel)
    place0 = lax.broadcasted_iota(jnp.int32, (d1, 128), 0) == 0
    for j, v in enumerate((count_f.reshape(1, 1).astype(bf), t1, t2, t3)):
        panel = jnp.where((lane == CT + j) & place0, v, panel)
    ups = up_weight.reshape(d1, n_dev, 4, d1).transpose(0, 2, 1, 3).reshape(d1, F)
    rest = jnp.concatenate([out_weight, ups] + [down_weight[j * d1 : (j + 1) * d1] for j in range(4)], axis=1)
    w_rest = lax.all_gather(rest, ALL, axis=0, tiled=True)
    if fast:
        c = col & 1
        pos = jnp.stack([col >> 1, pb & 1, pb >> 1, c, pb, col]).astype(jnp.int32)
        half = lambda h: jnp.concatenate([lax.dynamic_slice_in_dim(qkv_weight, h * (3 * D // 2), 3 * D // 2, 1), panel], axis=1)
        got, mine = swap_core(half(1 - c)), half(c)
        q1 = spread1(jnp.where(c == 0, cat([mine, got]), cat([got, mine])))
        p_qkv = spread4(spread3(spread2(q1)))
    else:
        pos = jnp.stack([0 * pb, 0 * pb, 0 * pb, 0 * pb, pb, col]).astype(jnp.int32)
        both = lax.all_gather(jnp.concatenate([qkv_weight, panel], axis=1), ALL, axis=0, tiled=True)
        panel = both[:, 3 * D :]
        p_qkv = spread_plain([both[:, : 3 * D], jnp.concatenate([panel, panel], axis=1)])
    strips, kx = tables(rel_bias, length[0], S)
    qkv, vec = qkv_fwd(pos, p_qkv, tokens)
    attn = [attn_fwd(qkv, kx, strips, 2 * i, 2) for i in range(3)]
    mixed = [v[0] for v in attn]
    layer_out, u1, u2, sc, nl, act, gp, first, own_score = post_fwd(length, w_rest, mixed, tokens, vec)
    scores = [own_score] + [swap_col(own_score, r) for r in range(1, ncol)]
    gr2, gi, vg1, kb, sb, info = back1(pos, length, scores, d1, w_rest, out_grad.reshape(S, D), u2, sc, act, gp, vec)
    if fast:
        rb0 = swap_core(sb)
    gr1, ga, gm, vg2 = back2(w_rest, gr2, u1, sc, gi, vec)
    if fast:
        cb1 = collect1(*afters([kb, rb0], gm))
        nl = afters([nl], cb1[0])[0]
    ka, sa = wup(pos, mixed, ga, nl, gi)
    gm_1 = afters([gm], ka)[0]
    if fast:
        ra0 = swap_core(sa)
    back = lambda i, g: attn_bwd(qkv, g, attn[i][2], attn[i][1], attn[i][3], 2 * i, 2)
    grads = [back(0, gm_1)]
    gm_2 = afters([gm], grads[0][0])[0]
    if fast:
        ca1 = collect1(*afters([ka, ra0], grads[0][0]))
        cb2 = collect2(*afters(cb1, ca1[0], ca1[1]))
        gm_2 = afters([gm], cb2[0], cb2[1])[0]
    grads.append(back(1, gm_2))
    gm_3 = afters([gm], grads[1][0])[0]
    if fast:
        ca2 = collect2(*afters(ca1, grads[1][0]))
        cb3 = collect3(*afters(cb2, ca2[0], ca2[1]))
        gm_3 = afters([gm], ca2[0], ca2[1], cb3[0])[0]
    grads.append(back(2, gm_3))
    parts = [g[j] for j in range(3) for g in grads]
    if fast:
        ca3 = collect3(*afters(ca2, grads[2][0]))
        parts = afters(parts, ca3[0])
    kq, sq, vb = wqkv(pos, tokens, parts)
    if fast:
        rq0 = swap_core(sq)
        mb, ob, _ = collect4(*afters(cb3, kq))
        cq1 = collect1(kq, rq0)
        parts = afters(parts, cq1[0], cq1[1])
    hidden_grad = hgrad(pos, p_qkv, parts, gr1)
    near = cat([g[3] for g in grads])
    far = cat([g[4] for g in grads])
    ids = strip_ids()
    onehot = (ids[:, :, None] == jnp.arange(rel_bias.shape[0], dtype=jnp.int32)).astype(f32)
    bucket = jnp.einsum("hac,acb->bh", near, onehot, precision=lax.Precision.HIGHEST)
    far = jnp.sum(far, axis=2)
    bucket = bucket.at[15].add(far[:, 0]).at[31].add(far[:, 1])
    weighted = info[1, :1]
    last = jnp.concatenate([bucket.reshape(-1), weighted, jnp.zeros((D - bucket.size - 1,), f32)])
    smalls = jnp.concatenate([(vg1 + vg2)[:CT], vb[:2], info[0, 0] * first[:1], last[None]], axis=0)
    h = D // 2
    if fast:
        smalls = smalls + swap_core(smalls)
        smalls = smalls + swap_x(smalls)
        cq2 = collect2(*afters(cq1, hidden_grad))
        smalls = smalls + swap_y(afters([smalls], hidden_grad)[0])
        ma, oa, _ = collect4(*afters(ca3, cq2[0], cq2[1]))
        d_down = sides(mb, ob, c)
        cq3 = collect3(*cq2)
        smalls = smalls + flip_z(afters([smalls], cq3[0])[0], 1)
        d_qkv = sides(*collect4(*cq3))
        smalls = smalls + flip_z(smalls, 2)
        d_out = sides(ma[:, :h], oa[:, :h], c)
        d_up = sides(ma[:, h:], oa[:, h:], c)
    else:
        scatter = lambda w: lax.psum_scatter(w, ALL, scatter_dimension=0, tiled=True).astype(f32)
        d_down, d_qkv = scatter(natural(kb, sb)), scatter(natural(kq, sq))
        d_out = scatter(natural(ka[:, :, :h], sa[:, :, :h]))
        d_up = scatter(natural(ka[:, :, h:], sa[:, :, h:]))
        smalls = lax.psum(smalls, ALL)
    d_down = cat([d_down[:, j * D : (j + 1) * D] for j in range(4)])
    d_up = d_up.reshape(d1, 4, n_dev, d1).transpose(0, 2, 1, 3).reshape(d1, F)
    part = lax.dynamic_slice_in_dim(smalls, dev * d1, d1, axis=1)
    loss = smalls[CT + 3, bucket.size] / info[2, 0]
    bucket = smalls[CT + 3, : bucket.size].reshape(bucket.shape)
    return (layer_out.reshape(hidden.shape), loss, hidden_grad.reshape(hidden.shape), d_qkv, part[CT : CT + 2],
            d_out, part[OB], part[G1], part[S1], d_up, part[UB : UB + 4].reshape(-1), d_down, part[DB], part[G2], part[S2],
            bucket, part[CT + 2])


def solution(mesh):
    lead = P(("pb", "col"))
    row = P(("pb", "col"), None)
    act = P("pb", "col", None, None)
    side = P(None, ("pb", "col"))
    return jax.shard_map(
        shards,
        mesh=mesh,
        in_specs=(act, P("pb", "col"), P("pb"), P("pb", "col"), act, row, side, row, lead, lead, lead, row, lead, row, lead, lead, lead, P(), lead),
        out_specs=(act, P(), act, row, side, row, lead, lead, lead, row, lead, row, lead, lead, lead, P(), lead),
        check_vma=False,
    )
```

time: 801 us -> 365 us (0.46)
  waiting for transfers between devices: 489 us -> 71.6 us
  blocking collectives: 108 us -> 0 us
  starting transfers between devices: 0.31 us -> 40.4 us
  Pallas kernels: 138 us -> 175 us
    reduce_scatter x4 -> x0, waiting for transfers between devices: 328 us -> none  [shards(): lax.psum_scatter(w, ALL, scatter_dimension=0, tiled=True).astype(f32)]
    all_gather x4 -> x1, waiting for transfers between devices: 156 us -> 13 us  [shards(): w_rest = lax.all_gather(rest, ALL, axis=0, tiled=True)]
    ppermute x0 -> x47, waiting for transfers between devices: none -> 58.6 us  [the longest x12 18.5 us: shift_z(): return lax.ppermute(v, 'pb', [(i, (i + 2 * k) % 8) for i in range(8)])]
    psum x2 -> x0, blocking collectives: 58.4 us -> none  [the longest x1 37.8 us: shards(): smalls = lax.psum(jnp.concatenate([vg, vb[:2], score_grad], axis=0), ALL)]
    unnamed x2 -> x0, blocking collectives: 49.4 us -> none
    ppermute x0 -> x47, starting transfers between devices: none -> 40.4 us  [the longest x12 14.8 us: shift_z(): return lax.ppermute(v, 'pb', [(i, (i + 2 * k) % 8) for i in range(8)])]
    pallas_call x5 -> x10, Pallas kernels: 110 us -> 138 us  [the longest x3 31.5 us: attn_fwd(): pl.pallas_call(functools.partial(fwd_kernel, BQ, S), cost_estimate=takes(...]
    pallas_call x1 -> x3, Pallas kernels: 28.5 us -> 36.5 us  [attn_bwd(): pl.pallas_call(functools.partial(bwd_kernel, BQ, S, form, scale, kscale),...]
  transfers between devices with their start and end apart: 8 -> 48, of which waited for: 8 -> 23; matrix products, arithmetic and copies ran while one was open for 4% -> 11% of each run, Pallas kernels for 9% -> 31%
where the time goes in v2:
time: 365 us; the launch traced here: 358 us
  Pallas kernels  175 us (48%)
  waiting for transfers between devices  71.6 us (20%)
  starting transfers between devices  40.4 us (11%)
  other arithmetic  23.8 us (7%)
  local copies, waits for them, and re-layouts  22.9 us (6%)
  between operations  19.7 us (5%)
  matrix products  5.01 us (1%)
    pallas_call x3, Pallas kernels, attn_bwd(): pl.pallas_call(functools.partial(bwd_kernel, BQ, S, form, scale, kscale),...  36.5 us
    pallas_call x3, Pallas kernels, attn_fwd(): pl.pallas_call(functools.partial(fwd_kernel, BQ, S), cost_estimate=takes(...  31.5 us
    pallas_call x1, Pallas kernels, post_fwd(): pl.pallas_call(functools.partial(post_kernel, TR, mode), cost_estimate=ta...  25.4 us
    pallas_call x1, Pallas kernels, back1(): pl.pallas_call(functools.partial(back1_kernel, TR, len(scores), d1), cost...  23.5 us
    ppermute x12, waiting for transfers between devices, shift_z(): return lax.ppermute(v, 'pb', [(i, (i + 2 * k) % 8) for i in range(8)])  18.5 us
    pallas_call x1, Pallas kernels, back2(): pl.pallas_call(functools.partial(back2_kernel, TR), cost_estimate=takes(F...  16.6 us
    ppermute x12, starting transfers between devices, shift_z(): return lax.ppermute(v, 'pb', [(i, (i + 2 * k) % 8) for i in range(8)])  14.8 us
    ppermute x9, waiting for transfers between devices, swap_y(): return lax.ppermute(v, 'pb', [(i, i ^ 1) for i in range(8)])  13.8 us
  transfers between devices with their start and end apart: 48, of which 23 were waited for; matrix products, arithmetic and copies ran while one was open for 11% of the time, Pallas kernels for 31%

profile of v2, /device:TPU:0, one launch (start us, length us, event | category | flops | bytes accessed | tf_op | source)
XLA Modules:
  0.0 358.2 jit_solution(5194939801222457725)
XLA Ops:
  16.3 3.7 %collective-permute-start.3 = (bf16[1,48,1280]{2,1,0:T(8,128)(2,1)S(1)}, bf16[1,48,1280]{2,1,0:T(8,128)(2,1)S(1)}, u32[]{:S(2)}, u32[]{:S(2)}) collective-permute-start(bf16[1,48,1280]{2,1,0:T(8,128)(2,1)S(1)} %maximum_select_fusion.3), channel_id=1, source_target_pairs={{0,16},{4,20},{8,24},{12,28},{16,0},{20,4},{24,8},{28,12},{1,17},{... | collective-permute-start | bytes 368648 | tf_op jit(solution)/shard_map/ppermute | solution.py:468
  22.7 4.1 %collective-permute-done.3 = bf16[1,48,1280]{2,1,0:T(8,128)(2,1)S(1)} collective-permute-done((bf16[1,48,1280]{2,1,0:T(8,128)(2,1)S(1)}, bf16[1,48,1280]{2,1,0:T(8,128)(2,1)S(1)}, u32[]{:S(2)}, u32[]{:S(2)}) %collective-permute-start.3) | collective-permute-done | bytes 122912 | tf_op jit(solution)/shard_map/ppermute | solution.py:468
  36.9 4.5 %collective-permute-done.2 = bf16[2,48,1280]{2,1,0:T(8,128)(2,1)S(1)} collective-permute-done((bf16[2,48,1280]{2,1,0:T(8,128)(2,1)S(1)}, bf16[2,48,1280]{2,1,0:T(8,128)(2,1)S(1)}, u32[]{:S(2)}, u32[]{:S(2)}) %collective-permute-start.2) | collective-permute-done | bytes 245792 | tf_op jit(solution)/shard_map/ppermute | solution.py:466
  47.5 5.3 %collective-permute-done.7.refs_3_ = bf16[4,48,1280]{2,1,0:T(8,128)(2,1)} collective-permute-done((bf16[4,48,1280]{2,1,0:T(8,128)(2,1)}, bf16[4,48,1280]{2,1,0:T(8,128)(2,1)}, u32[]{:S(2)}, u32[]{:S(2)}) %collective-permute-start.7) | collective-permute-done | bytes 491552 | tf_op jit(solution)/shard_map/ppermute | solution.py:466
  52.8 4.9 %collective-permute-done.6.refs_2_ = bf16[4,48,1280]{2,1,0:T(8,128)(2,1)} collective-permute-done((bf16[4,48,1280]{2,1,0:T(8,128)(2,1)}, bf16[4,48,1280]{2,1,0:T(8,128)(2,1)}, u32[]{:S(2)}, u32[]{:S(2)}) %collective-permute-start.6) | collective-permute-done | bytes 491552 | tf_op jit(solution)/shard_map/ppermute | solution.py:465
  61.8 9.4 %shard_map.314 = (bf16[1024,2304]{1,0:T(8,128)(2,1)}, f32[24,768]{1,0:T(8,128)}) custom-call(s32[6]{0:T(128)} %stack.27.pos, bf16[4,48,1280]{2,1,0:T(8,128)(2,1)} %pad_maximum_fusion.1.refs_0_, bf16[4,48,1280]{2,1,0:T(8,128)(2,1)} %constant_dynamic-update-slice_fusion.2.refs_1_, bf16[4,48,1280]{2,1,0:T(8,128)(2,1)} %collective-permute-done.6.refs_2_, ...), custom_call_target="tpu_custom_call" | custom-call | flops 1150000000 | bytes 1000000 | tf_op jit(solution)/shard_map/pallas_call | solution.py:218
  71.2 10.8 %shard_map.316 = (bf16[1024,256]{1,0:T(8,128)(2,1)}, f32[1024,256]{1,0:T(8,128)}, f32[1024,256]{1,0:T(8,128)}, bf16[4,1024,1024]{2,1,0:T(8,128)(2,1)}) custom-call(bf16[1024,2304]{1,0:T(8,128)(2,1)} %get-tuple-element.150.q_ref.k_ref.v_ref, bf16[1024,2304]{1,0:T(8,128)(2,1)} %get-tuple-element.150.q_ref.k_ref.v_ref, ...), custom_call_target="tpu_custom_call" | custom-call | flops 2300000000 | bytes 2000000 | tf_op jit(solution)/shard_map/pallas_call | solution.py:75
  82.0 10.3 %shard_map.317 = (bf16[1024,256]{1,0:T(8,128)(2,1)}, f32[1024,256]{1,0:T(8,128)}, f32[1024,256]{1,0:T(8,128)}, bf16[4,1024,1024]{2,1,0:T(8,128)(2,1)}) custom-call(bf16[1024,2304]{1,0:T(8,128)(2,1)} %get-tuple-element.150.q_ref.k_ref.v_ref, bf16[1024,2304]{1,0:T(8,128)(2,1)} %get-tuple-element.150.q_ref.k_ref.v_ref, ...), custom_call_target="tpu_custom_call" | custom-call | flops 2300000000 | bytes 2000000 | tf_op jit(solution)/shard_map/pallas_call | solution.py:75
  92.3 10.4 %shard_map.315 = (bf16[1024,256]{1,0:T(8,128)(2,1)}, f32[1024,256]{1,0:T(8,128)}, f32[1024,256]{1,0:T(8,128)}, bf16[4,1024,1024]{2,1,0:T(8,128)(2,1)}) custom-call(bf16[1024,2304]{1,0:T(8,128)(2,1)} %get-tuple-element.150.q_ref.k_ref.v_ref, bf16[1024,2304]{1,0:T(8,128)(2,1)} %get-tuple-element.150.q_ref.k_ref.v_ref, ...), custom_call_target="tpu_custom_call" | custom-call | flops 2300000000 | bytes 2000000 | tf_op jit(solution)/shard_map/pallas_call | solution.py:75
  102.7 13.0 %all-gather.2.cloned.1.call-done.refs_0_.refs_4_ = bf16[768,6912]{1,0:T(8,128)(2,1)} async-done(((bf16[24,6912]{1,0:T(8,128)(2,1)}), bf16[768,6912]{1,0:T(8,128)(2,1)}) %all-gather.2.cloned.1.call-update) | async-done | bytes 10616848 | tf_op jit(solution)/shard_map/all_gather | solution.py:554
  115.7 25.4 %shard_map.318 = (bf16[1024,768]{1,0:T(8,128)(2,1)}, f32[1024,768]{1,0:T(8,128)}, f32[1024,768]{1,0:T(8,128)}, f32[1024,128]{1,0:T(8,128)}, bf16[1024,768]{1,0:T...) custom-call(s32[1]{0:T(128)} %bitcast.87.len_ref, ...), custom_call_target="tpu_custom_call" | custom-call | flops 1150000000 | bytes 1000000 | tf_op jit(solution)/shard_map/pallas_call | solution.py:278
  146.7 23.5 %shard_map.319 = (f32[1024,768]{1,0:T(8,128)}, bf16[1024,3072]{1,0:T(8,128)(2,1)}, f32[24,768]{1,0:T(8,128)}, bf16[16,48,1536]{2,1,0:T(8,128)(2,1)}, bf16[16,48,1536]{2,1,0:T(8,128)(2,1)}, /*index=5*/f32[8,128]{1,0:T(8,128)}) custom-call(s32[6]{0:T(128)} %stack.27.pos, s32[1]{0:T(128)} %bitcast.88.len_ref, f32[8,128]{1,0:T(8,128)} %get-tuple-element.156.refs_0_, ...), custom_call_target="tpu_custom_call" | custom-call | flops 1150000000 | bytes 1000000 | tf_op jit(solution)/shard_map/pallas_call | solution.py:356
  170.4 16.6 %shard_map.320 = (f32[1024,768]{1,0:T(8,128)}, bf16[1024,768]{1,0:T(8,128)(2,1)}, bf16[1024,768]{1,0:T(8,128)(2,1)}, f32[24,768]{1,0:T(8,128)}) custom-call(bf16[768,6912]{1,0:T(8,128)(2,1)} %all-gather.2.cloned.1.call-done.refs_0_.refs_4_, f32[1024,768]{1,0:T(8,128)} %get-tuple-element.162.refs_1_, f32[1024,768]{1,0:T(8,128)} %get-tuple-element.163.refs_2_, ...), custom_call_target="tpu_custom_call" | custom-call | flops 1150000000 | bytes 1000000 | tf_op jit(solution)/shard_map/pallas_call | solution.py:387
  188.7 13.1 %shard_map.321 = (bf16[16,48,1920]{2,1,0:T(8,128)(2,1)}, bf16[16,48,1920]{2,1,0:T(8,128)(2,1)}) custom-call(s32[6]{0:T(128)} %stack.27.pos, bf16[1024,256]{1,0:T(8,128)(2,1)} %get-tuple-element.151.refs_1_.m0, bf16[1024,256]{1,0:T(8,128)(2,1)} %get-tuple-element.152.refs_2_.m1, bf16[1024,256]{1,0:T(8,128)(2,1)} %get-tuple-element.153.refs_3_.m2, ...), custom_call_target="tpu_custom_call" | custom-call | flops 1150000000 | bytes 1000000 | tf_op jit(solution)/shard_map/pallas_call | solution.py:414
  208.4 12.6 %shard_map.322 = (bf16[1024,256]{1,0:T(8,128)(2,1)}, bf16[1024,256]{1,0:T(8,128)(2,1)}, bf16[1024,256]{1,0:T(8,128)(2,1)}, f32[4,128,384]{2,1,0:T(8,128)}, f32[4,8,128]{2,1,0:T(8,128)}) custom-call(bf16[1024,2304]{1,0:T(8,128)(2,1)} %get-tuple-element.150.q_ref.k_ref.v_ref, bf16[1024,2304]{1,0:T(8,128)(2,1)} %get-tuple-element.150.q_ref.k_ref.v_ref, ...), custom_call_target="tpu_custom_call" | custom-call | flops 2300000000 | bytes 2000000 | tf_op jit(solution)/shard_map/pallas_call | solution.py:140
  229.3 11.9 %shard_map.323 = (bf16[1024,256]{1,0:T(8,128)(2,1)}, bf16[1024,256]{1,0:T(8,128)(2,1)}, bf16[1024,256]{1,0:T(8,128)(2,1)}, f32[4,128,384]{2,1,0:T(8,128)}, f32[4,8,128]{2,1,0:T(8,128)}) custom-call(bf16[1024,2304]{1,0:T(8,128)(2,1)} %get-tuple-element.150.q_ref.k_ref.v_ref, bf16[1024,2304]{1,0:T(8,128)(2,1)} %get-tuple-element.150.q_ref.k_ref.v_ref, ...), custom_call_target="tpu_custom_call" | custom-call | flops 2300000000 | bytes 2000000 | tf_op jit(solution)/shard_map/pallas_call | solution.py:140
  243.7 3.6 %collective-permute-done.22 = bf16[2,48,1536]{2,1,0:T(8,128)(2,1)S(1)} collective-permute-done((bf16[2,48,1536]{2,1,0:T(8,128)(2,1)S(1)}, bf16[2,48,1536]{2,1,0:T(8,128)(2,1)S(1)}, u32[]{:S(2)}, u32[]{:S(2)}) %collective-permute-start.22) | collective-permute-done | bytes 294944 | tf_op jit(solution)/shard_map/ppermute | solution.py:465
  256.7 12.0 %shard_map.324 = (bf16[1024,256]{1,0:T(8,128)(2,1)}, bf16[1024,256]{1,0:T(8,128)(2,1)}, bf16[1024,256]{1,0:T(8,128)(2,1)}, f32[4,128,384]{2,1,0:T(8,128)}, f32[4,8,128]{2,1,0:T(8,128)}) custom-call(bf16[1024,2304]{1,0:T(8,128)(2,1)} %get-tuple-element.150.q_ref.k_ref.v_ref, bf16[1024,2304]{1,0:T(8,128)(2,1)} %get-tuple-element.150.q_ref.k_ref.v_ref, ...), custom_call_target="tpu_custom_call" | custom-call | flops 2300000000 | bytes 2000000 | tf_op jit(solution)/shard_map/pallas_call | solution.py:140
  270.1 4.0 %fusion.6 = f32[32,12]{0,1:T(8,128)S(1)} fusion(f32[12,128,384]{2,1,0:T(8,128)S(1)} %pad_maximum_fusion, s32[128,384]{1,0:T(8,128)S(1)} %copy-done.8), kind=kOutput, calls=%fused_computation.20 | convolution fusion | flops 228065280 | bytes 2557440 | tf_op jit(solution)/shard_map/hac,acb->bh/dot_general | solution.py:613
  275.0 9.1 %shard_map.325 = (bf16[16,48,1152]{2,1,0:T(8,128)(2,1)}, bf16[16,48,1152]{2,1,0:T(8,128)(2,1)}, f32[8,768]{1,0:T(8,128)}) custom-call(s32[6]{0:T(128)} %stack.27.pos, bf16[1024,768]{1,0:T(8,128)(2,1)} %bitcast.95, bf16[1024,256]{1,0:T(8,128)(2,1)} %get-tuple-element.231.refs_0_.refs_8_, bf16[1024,256]{1,0:T(8,128)(2,1)} %get-tuple-element.232.refs_1_.refs_9_, ...), custom_call_target="tpu_custom_call" | custom-call | flops 1150000000 | bytes 1000000 | tf_op jit(solution)/shard_map/pallas_call | solution.py:437
  293.5 9.6 %shard_map.326 = bf16[1024,768]{1,0:T(8,128)(2,1)} custom-call(s32[6]{0:T(128)} %stack.27.pos, bf16[4,48,1280]{2,1,0:T(8,128)(2,1)} %pad_maximum_fusion.1.refs_0_, bf16[4,48,1280]{2,1,0:T(8,128)(2,1)} %constant_dynamic-update-slice_fusion.2.refs_1_, bf16[4,48,1280]{2,1,0:T(8,128)(2,1)} %collective-permute-done.6.refs_2_, ...), custom_call_target="tpu_custom_call" | custom-call | flops 1150000000 | bytes 1000000 | tf_op jit(solution)/shard_map/pallas_call | solution.py:454
  309.1 4.1 %collective-permute-done.32 = f32[17,768]{1,0:T(8,128)S(1)} collective-permute-done((f32[17,768]{1,0:T(8,128)S(1)}, f32[17,768]{1,0:T(8,128)S(1)}, u32[]{:S(2)}, u32[]{:S(2)}) %collective-permute-start.32) | collective-permute-done | bytes 52256 | tf_op jit(solution)/shard_map/ppermute | solution.py:467
  314.1 5.8 %collective-permute-done.33 = f32[17,768]{1,0:T(8,128)S(1)} collective-permute-done((f32[17,768]{1,0:T(8,128)S(1)}, f32[17,768]{1,0:T(8,128)S(1)}, u32[]{:S(2)}, u32[]{:S(2)}) %collective-permute-start.33) | collective-permute-done | bytes 52256 | tf_op jit(solution)/shard_map/ppermute | solution.py:467
  340.6 7.3 %collective-permute-done.36 = bf16[48,1152]{1,0:T(8,128)(2,1)S(1)} collective-permute-done((bf16[48,1152]{1,0:T(8,128)(2,1)S(1)}, bf16[48,1152]{1,0:T(8,128)(2,1)S(1)}, u32[]{:S(2)}, u32[]{:S(2)}) %collective-permute-start.36) | collective-permute-done | bytes 110624 | tf_op jit(solution)/shard_map/ppermute | solution.py:468
  (266 shorter events, 103.6 us)
Async XLA Ops:
  7.2 108.5 %all-gather.2.cloned.1.call-start = ((), (), s32[]{:S(2)}) async-start(), calls=%async_computation | async-start | bytes 10948608 | tf_op jit(solution)/shard_map/all_gather | solution.py:554
  21.9 10.8 %collective-permute-start.1 = (bf16[1,48,1280]{2,1,0:T(8,128)(2,1)S(1)}, bf16[1,48,1280]{2,1,0:T(8,128)(2,1)S(1)}, u32[]{:S(2)}, u32[]{:S(2)}) collective-permute-start(bf16[1,48,1280]{2,1,0:T(8,128)(2,1)S(1)} %maximum_select_fusion.3), channel_id=1, source_target_pairs={{0,8},{4,12},{8,16},{12,20},{16,24},{20,28},{24,0},{28,4},{1,9},{5... | collective-permute-start | bytes 368648 | tf_op jit(solution)/shard_map/ppermute | solution.py:468
  36.4 16.4 %collective-permute-start.7 = (bf16[4,48,1280]{2,1,0:T(8,128)(2,1)}, bf16[4,48,1280]{2,1,0:T(8,128)(2,1)}, u32[]{:S(2)}, u32[]{:S(2)}) collective-permute-start(bf16[4,48,1280]{2,1,0:T(8,128)(2,1)} %constant_dynamic-update-slice_fusion.2.refs_1_), channel_id=1, source_target_pairs={{0,4},{4,0},{8,12},{12,8},{16,20},{20,16},{24,28},{28,24},{1,5},{5... | collective-permute-start | bytes 1474568 | tf_op jit(solution)/shard_map/ppermute | solution.py:466
  42.2 15.5 %collective-permute-start.6 = (bf16[4,48,1280]{2,1,0:T(8,128)(2,1)}, bf16[4,48,1280]{2,1,0:T(8,128)(2,1)}, u32[]{:S(2)}, u32[]{:S(2)}) collective-permute-start(bf16[4,48,1280]{2,1,0:T(8,128)(2,1)} %pad_maximum_fusion.1.refs_0_), channel_id=1, source_target_pairs={{0,2},{1,3},{2,0},{3,1},{4,6},{5,7},{6,4},{7,5},{8,10},{9,11},{10,... | collective-permute-start | bytes 1474568 | tf_op jit(solution)/shard_map/ppermute | solution.py:465
  46.9 13.6 %collective-permute-start.9 = (bf16[4,48,1280]{2,1,0:T(8,128)(2,1)}, bf16[4,48,1280]{2,1,0:T(8,128)(2,1)S(1)}, u32[]{:S(2)}, u32[]{:S(2)}) collective-permute-start(bf16[4,48,1280]{2,1,0:T(8,128)(2,1)} %constant_dynamic-update-slice_fusion.2.refs_1_), channel_id=1, source_target_pairs={{0,1},{1,0},{2,3},{3,2},{4,5},{5,4},{6,7},{7,6},{8,9},{9,8},{10,11... | collective-permute-start | bytes 1474568 | tf_op jit(solution)/shard_map/ppermute | solution.py:463
  47.0 13.6 %collective-permute-start.8 = (bf16[4,48,1280]{2,1,0:T(8,128)(2,1)}, bf16[4,48,1280]{2,1,0:T(8,128)(2,1)S(1)}, u32[]{:S(2)}, u32[]{:S(2)}) collective-permute-start(bf16[4,48,1280]{2,1,0:T(8,128)(2,1)} %pad_maximum_fusion.1.refs_0_), channel_id=1, source_target_pairs={{0,1},{1,0},{2,3},{3,2},{4,5},{5,4},{6,7},{7,6},{8,9},{9,8},{10,11... | collective-permute-start | bytes 1474568 | tf_op jit(solution)/shard_map/ppermute | solution.py:463
  170.2 16.8 %collective-permute-start.15 = (bf16[16,48,1536]{2,1,0:T(8,128)(2,1)}, bf16[16,48,1536]{2,1,0:T(8,128)(2,1)S(1)}, u32[]{:S(2)}, u32[]{:S(2)}) collective-permute-start(bf16[16,48,1536]{2,1,0:T(8,128)(2,1)} %get-tuple-element.170), channel_id=1, source_target_pairs={{0,1},{1,0},{2,3},{3,2},{4,5},{5,4},{6,7},{7,6},{8,9},{9,8},{10,11... | collective-permute-start | bytes 7077896 | tf_op jit(solution)/shard_map/ppermute | solution.py:463
  201.8 19.2 %collective-permute-start.18 = (bf16[16,48,1920]{2,1,0:T(8,128)(2,1)}, bf16[16,48,1920]{2,1,0:T(8,128)(2,1)S(1)}, u32[]{:S(2)}, u32[]{:S(2)}) collective-permute-start(bf16[16,48,1920]{2,1,0:T(8,128)(2,1)} %get-tuple-element.180), channel_id=1, source_target_pairs={{0,1},{1,0},{2,3},{3,2},{4,5},{5,4},{6,7},{7,6},{8,9},{9,8},{10,11... | collective-permute-start | bytes 8847368 | tf_op jit(solution)/shard_map/ppermute | solution.py:463
  206.3 16.5 %collective-permute-start.16 = (bf16[4,48,1536]{2,1,0:T(8,128)(2,1)}, bf16[4,48,1536]{2,1,0:T(8,128)(2,1)}, u32[]{:S(2)}, u32[]{:S(2)}) collective-permute-start(bf16[4,48,1536]{2,1,0:T(8,128)(2,1)} %get-tuple-element.334), channel_id=1, source_target_pairs={{0,2},{1,3},{2,0},{3,1},{4,6},{5,7},{6,4},{7,5},{8,10},{9,11},{10,... | collective-permute-start | bytes 1769480 | tf_op jit(solution)/shard_map/ppermute | solution.py:465
  207.0 15.9 %collective-permute-start.17 = (bf16[4,48,1536]{2,1,0:T(8,128)(2,1)}, bf16[4,48,1536]{2,1,0:T(8,128)(2,1)}, u32[]{:S(2)}, u32[]{:S(2)}) collective-permute-start(bf16[4,48,1536]{2,1,0:T(8,128)(2,1)} %get-tuple-element.333), channel_id=1, source_target_pairs={{0,4},{4,0},{8,12},{12,8},{16,20},{20,16},{24,28},{28,24},{1,5},{5... | collective-permute-start | bytes 1769480 | tf_op jit(solution)/shard_map/ppermute | solution.py:466
  222.8 19.6 %collective-permute-start.19 = (bf16[4,48,1920]{2,1,0:T(8,128)(2,1)}, bf16[4,48,1920]{2,1,0:T(8,128)(2,1)S(1)}, u32[]{:S(2)}, u32[]{:S(2)}) collective-permute-start(bf16[4,48,1920]{2,1,0:T(8,128)(2,1)} %get-tuple-element.330), channel_id=1, source_target_pairs={{0,2},{1,3},{2,0},{3,1},{4,6},{5,7},{6,4},{7,5},{8,10},{9,11},{10,... | collective-permute-start | bytes 2211848 | tf_op jit(solution)/shard_map/ppermute | solution.py:465
  223.7 19.6 %collective-permute-start.20 = (bf16[4,48,1920]{2,1,0:T(8,128)(2,1)}, bf16[4,48,1920]{2,1,0:T(8,128)(2,1)S(1)}, u32[]{:S(2)}, u32[]{:S(2)}) collective-permute-start(bf16[4,48,1920]{2,1,0:T(8,128)(2,1)} %get-tuple-element.329), channel_id=1, source_target_pairs={{0,4},{4,0},{8,12},{12,8},{16,20},{20,16},{24,28},{28,24},{1,5},{5... | collective-permute-start | bytes 2211848 | tf_op jit(solution)/shard_map/ppermute | solution.py:466
  227.2 20.1 %collective-permute-start.22 = (bf16[2,48,1536]{2,1,0:T(8,128)(2,1)S(1)}, bf16[2,48,1536]{2,1,0:T(8,128)(2,1)S(1)}, u32[]{:S(2)}, u32[]{:S(2)}) collective-permute-start(bf16[2,48,1536]{2,1,0:T(8,128)(2,1)S(1)} %get-tuple-element.345), channel_id=1, source_target_pairs={{0,2},{1,3},{2,0},{3,1},{4,6},{5,7},{6,4},{7,5},{8,10},{9,11},{10,... | collective-permute-start | bytes 884744 | tf_op jit(solution)/shard_map/ppermute | solution.py:465
  228.3 19.5 %collective-permute-start.21 = (bf16[2,48,1536]{2,1,0:T(8,128)(2,1)S(1)}, bf16[2,48,1536]{2,1,0:T(8,128)(2,1)S(1)}, u32[]{:S(2)}, u32[]{:S(2)}) collective-permute-start(bf16[2,48,1536]{2,1,0:T(8,128)(2,1)S(1)} %get-tuple-element.347), channel_id=1, source_target_pairs={{0,4},{4,0},{8,12},{12,8},{16,20},{20,16},{24,28},{28,24},{1,5},{5... | collective-permute-start | bytes 884744 | tf_op jit(solution)/shard_map/ppermute | solution.py:466
  248.5 36.5 %collective-permute-start.44 = (bf16[48,1536]{1,0:T(8,128)(2,1)}, bf16[48,1536]{1,0:T(8,128)(2,1)}, u32[]{:S(2)}, u32[]{:S(2)}) collective-permute-start(bf16[48,1536]{1,0:T(8,128)(2,1)} %get-tuple-element.358), channel_id=1, source_target_pairs={{0,16},{4,20},{8,24},{12,28},{16,0},{20,4},{24,8},{28,12},{1,17},{... | collective-permute-start | bytes 442376 | tf_op jit(solution)/shard_map/ppermute | solution.py:468
  250.1 34.8 %collective-permute-start.45 = (bf16[48,1536]{1,0:T(8,128)(2,1)S(1)}, bf16[48,1536]{1,0:T(8,128)(2,1)}, u32[]{:S(2)}, u32[]{:S(2)}) collective-permute-start(bf16[48,1536]{1,0:T(8,128)(2,1)S(1)} %get-tuple-element.357), channel_id=1, source_target_pairs={{0,8},{4,12},{8,16},{12,20},{16,24},{20,28},{24,0},{28,4},{1,9},{5... | collective-permute-start | bytes 442376 | tf_op jit(solution)/shard_map/ppermute | solution.py:468
  251.5 23.4 %collective-permute-start.24 = (bf16[2,48,1920]{2,1,0:T(8,128)(2,1)S(1)}, bf16[2,48,1920]{2,1,0:T(8,128)(2,1)S(1)}, u32[]{:S(2)}, u32[]{:S(2)}) collective-permute-start(bf16[2,48,1920]{2,1,0:T(8,128)(2,1)S(1)} %get-tuple-element.341), channel_id=1, source_target_pairs={{0,2},{1,3},{2,0},{3,1},{4,6},{5,7},{6,4},{7,5},{8,10},{9,11},{10,... | collective-permute-start | bytes 1105928 | tf_op jit(solution)/shard_map/ppermute | solution.py:465
  252.8 22.1 %collective-permute-start.23 = (bf16[2,48,1920]{2,1,0:T(8,128)(2,1)S(1)}, bf16[2,48,1920]{2,1,0:T(8,128)(2,1)S(1)}, u32[]{:S(2)}, u32[]{:S(2)}) collective-permute-start(bf16[2,48,1920]{2,1,0:T(8,128)(2,1)S(1)} %get-tuple-element.343), channel_id=1, source_target_pairs={{0,4},{4,0},{8,12},{12,8},{16,20},{20,16},{24,28},{28,24},{1,5},{5... | collective-permute-start | bytes 1105928 | tf_op jit(solution)/shard_map/ppermute | solution.py:466
  253.5 31.5 %collective-permute-start.43 = (bf16[48,1536]{1,0:T(8,128)(2,1)}, bf16[48,1536]{1,0:T(8,128)(2,1)S(1)}, u32[]{:S(2)}, u32[]{:S(2)}) collective-permute-start(bf16[48,1536]{1,0:T(8,128)(2,1)} %get-tuple-element.359), channel_id=1, source_target_pairs={{0,24},{4,28},{8,0},{12,4},{16,8},{20,12},{24,16},{28,20},{1,25},{... | collective-permute-start | bytes 442376 | tf_op jit(solution)/shard_map/ppermute | solution.py:468
  290.1 34.6 %collective-permute-start.40 = (bf16[48,1920]{1,0:T(8,128)(2,1)}, bf16[48,1920]{1,0:T(8,128)(2,1)}, u32[]{:S(2)}, u32[]{:S(2)}) collective-permute-start(bf16[48,1920]{1,0:T(8,128)(2,1)} %get-tuple-element.354), channel_id=1, source_target_pairs={{0,16},{4,20},{8,24},{12,28},{16,0},{20,4},{24,8},{28,12},{1,17},{... | collective-permute-start | bytes 552968 | tf_op jit(solution)/shard_map/ppermute | solution.py:468
  290.2 34.5 %collective-permute-start.41 = (bf16[48,1920]{1,0:T(8,128)(2,1)}, bf16[48,1920]{1,0:T(8,128)(2,1)}, u32[]{:S(2)}, u32[]{:S(2)}) collective-permute-start(bf16[48,1920]{1,0:T(8,128)(2,1)} %get-tuple-element.353), channel_id=1, source_target_pairs={{0,8},{4,12},{8,16},{12,20},{16,24},{20,28},{24,0},{28,4},{1,9},{5... | collective-permute-start | bytes 552968 | tf_op jit(solution)/shard_map/ppermute | solution.py:468
  304.7 19.8 %collective-permute-start.29 = (bf16[4,48,1152]{2,1,0:T(8,128)(2,1)S(1)}, bf16[4,48,1152]{2,1,0:T(8,128)(2,1)S(1)}, u32[]{:S(2)}, u32[]{:S(2)}) collective-permute-start(bf16[4,48,1152]{2,1,0:T(8,128)(2,1)S(1)} %get-tuple-element.338), channel_id=1, source_target_pairs={{0,2},{1,3},{2,0},{3,1},{4,6},{5,7},{6,4},{7,5},{8,10},{9,11},{10,... | collective-permute-start | bytes 1327112 | tf_op jit(solution)/shard_map/ppermute | solution.py:465
  305.4 19.1 %collective-permute-start.30 = (bf16[4,48,1152]{2,1,0:T(8,128)(2,1)S(1)}, bf16[4,48,1152]{2,1,0:T(8,128)(2,1)S(1)}, u32[]{:S(2)}, u32[]{:S(2)}) collective-permute-start(bf16[4,48,1152]{2,1,0:T(8,128)(2,1)S(1)} %get-tuple-element.337), channel_id=1, source_target_pairs={{0,4},{4,0},{8,12},{12,8},{16,20},{20,16},{24,28},{28,24},{1,5},{5... | collective-permute-start | bytes 1327112 | tf_op jit(solution)/shard_map/ppermute | solution.py:466
  337.2 10.7 %collective-permute-start.36 = (bf16[48,1152]{1,0:T(8,128)(2,1)S(1)}, bf16[48,1152]{1,0:T(8,128)(2,1)S(1)}, u32[]{:S(2)}, u32[]{:S(2)}) collective-permute-start(bf16[48,1152]{1,0:T(8,128)(2,1)S(1)} %get-tuple-element.361), channel_id=1, source_target_pairs={{0,16},{4,20},{8,24},{12,28},{16,0},{20,4},{24,8},{28,12},{1,17},{... | collective-permute-start | bytes 331784 | tf_op jit(solution)/shard_map/ppermute | solution.py:468
  (57 other events, 288.9 us)
Sparse Core Ops, SparseCore 0:
  11.9 103.7 all-gather.1

commit v3 on v2

--- a/solution.py
+++ b/solution.py
@@ -72,13 +72,13 @@
     S,W=qkv.shape; npair=W//3//128
     blk=lambda o: pl.BlockSpec((S,128),lambda p:(0,o*npair+p0+p))
     out=pl.BlockSpec((S,128),lambda p:(0,p))
-    return pl.pallas_call(functools.partial(fwd_kernel,BQ,S),cost_estimate=takes(n*FAST),grid=(n,),
+    return pl.pallas_call(functools.partial(fwd_kernel,BQ,S),cost_estimate=takes(n*5),grid=(n,),
         in_specs=[blk(0),blk(1),blk(2),pl.BlockSpec((2,S,128),lambda p:(p0+p,0,0)),pl.BlockSpec((2,T,3*T),lambda p:(p0+p,0,0))],
         out_specs=[out]*3+[pl.BlockSpec((2,S,S),lambda p:(p,0,0))],
         out_shape=[sd((S,n*128),bf),sd((S,n*128),f32),sd((S,n*128),f32),sd((2*n,S,S),bf)],
         compiler_params=pltpu.CompilerParams(vmem_limit_bytes=56*2**20),
         )(qkv,qkv,qkv,kx,strips)
-def bwd_kernel(BQ,S,form,scale,kscale,q_ref,k_ref,v_ref,gm_ref,mf_ref,linv_ref,p_ref,dq_ref,dk_ref,dv_ref,near_ref,far_ref,ds_ref):
+def bwd_kernel(BQ,S,form,scale,kscale,q_ref,k_ref,v_ref,gm_ref,mf_ref,linv_ref,p_ref,dq_ref,dk_ref,dv_ref,diag_ref,cs_ref,ds_ref):
     nblk=S//T
     lane=lax.broadcasted_iota(jnp.int32,(1,128),1)
     lanes=lax.broadcasted_iota(jnp.int32,(S,128),1)
@@ -112,40 +112,52 @@
                 for n in (-1,0,1):
                     if 0<=I+n<nblk:
                         near[n+1]=near[n+1]+ds[b*T:(b+1)*T,(I+n)*T:(I+n+1)*T].astype(f32)
-        for n in range(3): near_ref[h,:,n*T:(n+1)*T]=near[n]
         dq=jnp.concatenate(dq,axis=0)
         dqs.append(dq[:,:128])
         far=dq[:,128:]
         ib=rows//T
-        far_ref[h,0:1,:]=jnp.sum(jnp.where(lanes<=ib-2,far,0.0),axis=0,keepdims=True)
-        far_ref[h,1:2,:]=jnp.sum(jnp.where((lanes>=ib+2)&(lanes<nblk),far,0.0),axis=0,keepdims=True)
-        far_ref[h,2:8,:]=jnp.zeros((6,128),f32)
+        total=lambda m: jnp.sum(jnp.sum(jnp.where(m,far,0.0),axis=0,keepdims=True),axis=1,keepdims=True)
+        low=total(lanes<=ib-2);up=total((lanes>=ib+2)&(lanes<nblk))
+        W=4*T
+        y=jnp.concatenate(near+[jnp.zeros((T,T),f32)],axis=1)
+        n=T
+        while n>8:
+            n//=2
+            y=y[:n]+pltpu.roll(y[n:],W-n,1)
+        sub=lax.broadcasted_iota(jnp.int32,(8,W),0)
+        for b in range(3): y=jnp.where(((sub>>b)&1)==1,pltpu.roll(y,W-(1<<b),1),y)
+        place=lax.broadcasted_iota(jnp.int32,(1,W),1)
+        y=jnp.sum(y,axis=0,keepdims=True)+jnp.where(place==W-1,low,0.0)+jnp.where(place==2*T+1,up,0.0)
+        diag_ref[h]=jnp.broadcast_to(y,(8,W))
         if form=="T":
             dks.append(dg(qT[h*64:(h+1)*64],ds_ref[...],NN))
             dvs.append(dg(doT[h*64:(h+1)*64],p_ref[h],NN))
         else:
             dks.append(dg(ds_ref[...],q,TN))
             dvs.append(dg(p_ref[h],do,TN))
-    dq_ref[...]=(jnp.where(masks[0],dqs[0],dqs[1])*scale).astype(bf)
+    dq=(jnp.where(masks[0],dqs[0],dqs[1])*scale).astype(bf)
+    dq_ref[...]=dq
     if form=="T":
         dk_ref[...]=(jnp.concatenate(dks,axis=0)*kscale).T.astype(bf)
-        dv_ref[...]=jnp.concatenate(dvs,axis=0).T.astype(bf)
+        dv=jnp.concatenate(dvs,axis=0).T.astype(bf)
     else:
         dk_ref[...]=(jnp.where(masks[0],dks[0],dks[1])*kscale).astype(bf)
-        dv_ref[...]=jnp.where(masks[0],dvs[0],dvs[1]).astype(bf)
+        dv=jnp.where(masks[0],dvs[0],dvs[1]).astype(bf)
+    dv_ref[...]=dv
+    part=lax.broadcasted_iota(jnp.int32,(8,128),0)
+    cs_ref[...]=jnp.where(part==0,jnp.sum(dq.astype(f32),axis=0,keepdims=True),jnp.sum(dv.astype(f32),axis=0,keepdims=True))
 def attn_bwd(qkv,gm,mixed,linv,p,p0,n,BQ=512,form="T",scale=0.125,kscale=1.0):
     S,W=qkv.shape; npair=W//3//128
     blk=lambda o: pl.BlockSpec((S,128),lambda i:(0,o*npair+p0+i))
     own=pl.BlockSpec((S,128),lambda i:(0,i))
-    return pl.pallas_call(functools.partial(bwd_kernel,BQ,S,form,scale,kscale),cost_estimate=takes(n*FAST),grid=(n,),
+    return pl.pallas_call(functools.partial(bwd_kernel,BQ,S,form,scale,kscale),cost_estimate=takes(n*6),grid=(n,),
         in_specs=[blk(0),blk(1),blk(2),blk(0),own,own,pl.BlockSpec((2,S,S),lambda i:(i,0,0))],
-        out_specs=[own]*3+[pl.BlockSpec((2,T,3*T),lambda i:(i,0,0)),pl.BlockSpec((2,8,128),lambda i:(i,0,0))],
-        out_shape=[sd((S,n*128),bf)]*3+[sd((2*n,T,3*T),f32),sd((2*n,8,128),f32)],
+        out_specs=[own]*3+[pl.BlockSpec((2,8,4*T),lambda i:(i,0,0)),pl.BlockSpec((8,128),lambda i:(0,i))],
+        out_shape=[sd((S,n*128),bf)]*3+[sd((2*n,8,4*T),f32),sd((8,n*128),f32)],
         scratch_shapes=[pltpu.VMEM((S,S),bf)],
         compiler_params=pltpu.CompilerParams(vmem_limit_bytes=56*2**20),
         )(qkv,qkv,qkv,gm,mixed,linv,p)
 sd=jax.ShapeDtypeStruct
-FAST=1.0
 def takes(us): return pl.CostEstimate(flops=int(us*1.15e9),bytes_accessed=int(us*1e6),transcendentals=0)
 def dg(a,b,d=NN): return lax.dot_general(a,b,d,preferred_element_type=f32)
 QB,VB,OB,G1,S1,DB,G2,S2,SW,UB,CT,TG,NV=0,1,2,3,4,5,6,7,8,9,13,14,24
@@ -215,7 +227,7 @@
     o_ref[:,2*D:]=(dg(x,w_s[:,2*D:])+vec_ref[VB:VB+1,:]).astype(bf)
 def qkv_fwd(pos,pieces,hid,TR=256):
     R,D=hid.shape;N=3*D
-    return pl.pallas_call(qkv_kernel,cost_estimate=takes(FAST),grid=(R//TR,),
+    return pl.pallas_call(qkv_kernel,cost_estimate=takes(9),grid=(R//TR,),
         in_specs=[SMEM]+[ANYS]*8+[pl.BlockSpec((TR,D),lambda i:(i,0))],
         out_specs=[pl.BlockSpec((TR,N),lambda i:(i,0)),pl.BlockSpec((NV,D),lambda i:(0,0))],
         out_shape=[sd((R,N),bf),sd((NV,D),f32)],
@@ -232,7 +244,7 @@
     for j in range(dst.shape[0]//D):
         arrived(dst.at[pl.ds(j*D,D),:],sems.at[j])
 def post_kernel(TR,mode,len_ref,*refs):
-    w,m0,m1,m2,hid_ref,vec_ref,lo_ref,u1_ref,u2_ref,sc_ref,nl_ref,act_ref,gp_ref,fr_ref,os_ref,ow_ref,uw_ref,dw_ref,sems=refs
+    w,*parts,hid_ref,vec_ref,lo_ref,u1_ref,u2_ref,sc_ref,nl_ref,act_ref,gp_ref,fr_ref,os_ref,ow_ref,uw_ref,dw_ref,sems=refs
     D=hid_ref.shape[1];F=uw_ref.shape[1]
     i=pl.program_id(0)
     @pl.when(i==0)
@@ -241,15 +253,17 @@
         fetch(w,D,uw_ref,sems.at[5])
         fetch_down(w,D+F,dw_ref,sems)
         arrived(ow_ref,sems.at[4])
-        arrived(uw_ref,sems.at[5])
-        arrived_down(dw_ref,sems)
     vec=lambda n: vec_ref[n:n+1,:]
-    r=hid_ref[...].astype(f32)+(dg(jnp.concatenate([m0[...],m1[...],m2[...]],axis=1),ow_ref[...])+vec(OB))
+    r=hid_ref[...].astype(f32)+(dg(jnp.concatenate([m[...] for m in parts],axis=1),ow_ref[...])+vec(OB))
     u1,s1=norm(r)
-    u1_ref[...]=u1
+    u1_ref[...]=u1.astype(bf)
     n=u1*vec(G1)+vec(S1)
     nl=n.astype(bf)
     nl_ref[...]=nl
+    @pl.when(i==0)
+    def _():
+        arrived(uw_ref,sems.at[5])
+        arrived_down(dw_ref,sems)
     br=None
     for c in range(F//D):
         x=dg(nl,uw_ref[:,c*D:(c+1)*D])+vec(UB+c)
@@ -260,7 +274,7 @@
         b=dg(a,dw_ref[c*D:(c+1)*D,:])
         br=b if br is None else br+b
     u2,s2=norm(n+(br+vec(DB)))
-    u2_ref[...]=u2
+    u2_ref[...]=u2.astype(bf)
     fin=u2*vec(G2)+vec(S2)
     row=lax.broadcasted_iota(jnp.int32,(TR,D),0)+i*TR
     lo_ref[...]=jnp.where(row<len_ref[0],fin,0.0).astype(bf)
@@ -275,10 +289,10 @@
     R,D=hid.shape;F=4*D
     rb=lambda n: pl.BlockSpec((TR,n),lambda i:(i,0))
     cb=lambda a: pl.BlockSpec(a.shape,lambda i:(0,0))
-    return pl.pallas_call(functools.partial(post_kernel,TR,mode),cost_estimate=takes(FAST),grid=(R//TR,),
+    return pl.pallas_call(functools.partial(post_kernel,TR,mode),cost_estimate=takes(25),grid=(R//TR,),
         in_specs=[SMEM,ANYS]+[rb(m.shape[1]) for m in mixed]+[rb(D),cb(vec)],
         out_specs=[rb(D),rb(D),rb(D),rb(128),rb(D),rb(F),rb(F),pl.BlockSpec((8,D),lambda i:(0,0)),pl.BlockSpec((8,128),lambda i:(0,0))],
-        out_shape=[sd((R,D),bf),sd((R,D),f32),sd((R,D),f32),sd((R,128),f32),sd((R,D),bf),sd((R,F),bf),sd((R,F),bf),sd((8,D),f32),sd((8,128),f32)],
+        out_shape=[sd((R,D),bf),sd((R,D),bf),sd((R,D),bf),sd((R,128),f32),sd((R,D),bf),sd((R,F),bf),sd((R,F),bf),sd((8,D),f32),sd((8,128),f32)],
         scratch_shapes=[pltpu.VMEM((D,D),bf),pltpu.VMEM((D,F),bf),pltpu.VMEM((F,D),bf),pltpu.SemaphoreType.DMA((6,))],
         compiler_params=pltpu.CompilerParams(vmem_limit_bytes=60*2**20))(length,w,*mixed,hid,vec)
 def listwise(pos,ncol,d1,scores,vec_ref,info_ref):
@@ -306,124 +320,142 @@
     weighted=jnp.where(col==0,mine*entropy,0.0)
     row=lax.broadcasted_iota(jnp.int32,(8,128),0)
     info_ref[...]=jnp.where(row==0,gs,jnp.where(row==1,weighted,total))
-def back1_kernel(TR,ncol,d1,pos,len_ref,*refs):
+def whole1(a): return pl.BlockSpec(a.shape,lambda i:(0,)*len(a.shape),pipeline_mode=pl.Buffered(1))
+def mid_kernel(TR,ncol,d1,nm,pos,len_ref,*refs):
     s_refs=refs[:ncol]
-    (w,og_ref,u2_ref,sc_ref,act_ref,gp_ref,vec_ref,gr2_ref,gi_ref,vg_ref,kb_ref,sb_ref,info_ref,
-     dw_ref,gb_s,act_s,sems)=refs[ncol:]
-    D=og_ref.shape[1];F=act_ref.shape[1];H=D//2
+    w,act,nl=refs[ncol:ncol+3]
+    mixed=refs[ncol+3:ncol+3+nm]
+    (og_ref,u2_ref,u1_ref,sc_ref,gp_ref,vec_ref,ga_ref,gm_ref,vg_ref,info_ref,keep,send,
+     ow_s,uw_s,dw_s,act_s,nl_s,mix_s,gb_s,gi_s,ga_s,stage,sems,outs)=refs[ncol+3+nm:]
+    D=og_ref.shape[1];F=gp_ref.shape[1];H=D//2
     i=pl.program_id(0);n=pl.num_programs(0)
+    def whole_copies():
+        at=0
+        todo=[(act,act_s,6),(nl,nl_s,7)]
+        for j,m in enumerate(mixed):
+            todo.append((m,mix_s.at[:,at:at+m.shape[1]],8+j)); at+=m.shape[1]
+        return [pltpu.make_async_copy(a,b,sems.at[k]) for a,b,k in todo]
     @pl.when(i==0)
     def _():
-        fetch_down(w,D+F,dw_ref,sems)
+        fetch_down(w,D+F,dw_s,sems)
+        fetch(w,D,uw_s,sems.at[4])
+        fetch(w,0,ow_s,sems.at[5])
+        for c in whole_copies(): c.start()
         listwise(pos,ncol,d1,[r[0:1,0:1] for r in s_refs],vec_ref,info_ref)
         vg_ref[...]=jnp.zeros_like(vg_ref)
-        arrived_down(dw_ref,sems)
+        arrived_down(dw_s,sems)
     vec=lambda k: vec_ref[k:k+1,:]
     row=lax.broadcasted_iota(jnp.int32,(TR,D),0)+i*TR
     gf=og_ref[...].astype(f32)
     gf=gf+jnp.where(row==0,info_ref[0:1,0:1]*vec(SW),0.0)
     gf=jnp.where(row<len_ref[0],gf,0.0)
     def add(k,v): vg_ref[k:k+1,:]+=jnp.sum(v,axis=0,keepdims=True)
-    u2=u2_ref[...]; s2=sc_ref[:,1:2]
+    u2=u2_ref[...].astype(f32); s1=sc_ref[:,0:1]; s2=sc_ref[:,1:2]
     add(G2,gf*u2); add(S2,gf)
     gr2=norm_bwd(gf,u2,s2,vec(G2))
-    gr2_ref[...]=gr2
     gb=gr2.astype(bf)
     here=pl.ds(pl.multiple_of(i*TR,TR),TR)
-    gb_s[here,:]=gb; act_s[here,:]=act_ref[...]
+    gb_s[here,:]=gb
     add(DB,gb.astype(f32))
+    @pl.when(i==0)
+    def _():
+        arrived(uw_s,sems.at[4])
+        arrived(ow_s,sems.at[5])
+    gn=gr2
     for c in range(F//D):
-        ga=dg(gb,dw_ref[c*D:(c+1)*D,:],NT)
-        gi=(ga*gp_ref[:,c*D:(c+1)*D].astype(f32)).astype(bf)
-        gi_ref[:,c*D:(c+1)*D]=gi
+        g=dg(gb,dw_s[c*D:(c+1)*D,:],NT)
+        gi=(g*gp_ref[:,c*D:(c+1)*D].astype(f32)).astype(bf)
+        gi_s[here,c*D:(c+1)*D]=gi
         add(UB+c,gi.astype(f32))
+        gn=gn+dg(gi,uw_s[:,c*D:(c+1)*D],NT)
+    u1=u1_ref[...].astype(f32)
+    add(G1,gn*u1); add(S1,gn)
+    ga=norm_bwd(gn,u1,s1,vec(G1)).astype(bf)
+    ga_ref[...]=ga
+    ga_s[here,:]=ga
+    add(OB,ga.astype(f32))
+    gm_ref[...]=dg(ga,ow_s[...],NT).astype(bf)
     @pl.when(i==n-1)
     def _():
-        gball=gb_s[...]
+        for c in whole_copies(): c.wait()
         core=pos[C_]
         slots=[slot(pos,k) for k in range(BLK)]
-        for ref,h in ((sb_ref,1-core),(kb_ref,core)):
+        U=H+F//2
+        jobs=[]
+        for ref,h in ((send,1-core),(keep,core)):
             for c in range(F//D//2):
+                jobs.append((ref,h,c,"down"))
+            for c in range(F//D//2):
+                jobs.append((ref,h,c,"up"))
+        jobs.append((None,None,0,"out"))
+        copies=[]
+        for j,(ref,h,c,kind) in enumerate(jobs):
+            b=j&1
+            if j>=2:
+                for v in copies[j-2]: v.wait()
+            if kind!="out":
                 cols=pl.ds(pl.multiple_of(h*(F//2)+c*D,D),D)
-                t=dg(act_s[:,cols],gball,TN).astype(bf)
-                for k in range(BLK):
-                    ref[slots[k],:,c*D:(c+1)*D]=t[k*(D//BLK):(k+1)*(D//BLK)]
-def whole1(a): return pl.BlockSpec(a.shape,lambda i:(0,)*len(a.shape),pipeline_mode=pl.Buffered(1))
-def back1(pos,length,scores,d1,w,og,u2,sc,act,gp,vec,TR=256):
+            if kind=="down":
+                t=dg(act_s[:,cols],gb_s[...],TN)
+            elif kind=="up":
+                t=dg(nl_s[...],gi_s[:,cols],TN)
+            else:
+                t=dg(mix_s[...],ga_s[...],TN)
+            t=t.astype(bf)
+            for k in range(BLK):
+                stage[b,slots[k]]=t[k*(D//BLK):(k+1)*(D//BLK)]
+            if kind=="out":
+                halves=[pl.ds(pl.multiple_of(v*H,H),H) for v in (core,1-core)]
+                made=[pltpu.make_async_copy(stage.at[b,:,:,halves[m]],r.at[:,:,pl.ds(0,H)],outs.at[j+m]) for m,r in enumerate((keep,send))]
+            else:
+                off=(U if kind=="down" else H)+c*D
+                made=[pltpu.make_async_copy(stage.at[b],ref.at[:,:,pl.ds(off,D)],outs.at[j])]
+            for v in made: v.start()
+            copies.append(made)
+        for made in copies[-2:]:
+            for v in made: v.wait()
+def mid(pos,length,scores,d1,w,og,u2,u1,sc,act,gp,nl,mixed,vec,TR=256):
     R,D=og.shape;F=act.shape[1]
     rb=lambda n: pl.BlockSpec((TR,n),lambda i:(i,0))
-    gb=sd((BLK,D//BLK,F//2),bf)
-    return pl.pallas_call(functools.partial(back1_kernel,TR,len(scores),d1),cost_estimate=takes(FAST),grid=(R//TR,),
-        in_specs=[SMEM]*2+[whole1(v) for v in scores]+[ANYS]+[rb(D),rb(D),rb(128),rb(F),rb(F),whole1(vec)],
-        out_specs=[rb(D),rb(F),whole1(vec),whole1(gb),whole1(gb),whole1(scores[0])],
-        out_shape=[sd((R,D),f32),sd((R,F),bf),vec,gb,gb,sd((8,128),f32)],
-        scratch_shapes=[pltpu.VMEM((F,D),bf),pltpu.VMEM((R,D),bf),pltpu.VMEM((R,F),bf),pltpu.SemaphoreType.DMA((4,))],
-        compiler_params=pltpu.CompilerParams(vmem_limit_bytes=62*2**20))(pos,length,*scores,w,og,u2,sc,act,gp,vec)
-def back2_kernel(TR,*refs):
-    (w,gr2_ref,u1_ref,sc_ref,gi_ref,vec_ref,gr1_ref,ga_ref,gm_ref,vg_ref,ow_ref,uw_ref,sems)=refs
-    D=gr2_ref.shape[1]
-    i=pl.program_id(0)
-    @pl.when(i==0)
-    def _():
-        fetch(w,D,uw_ref,sems.at[0])
-        fetch(w,0,ow_ref,sems.at[1])
-        vg_ref[...]=jnp.zeros_like(vg_ref)
-        arrived(uw_ref,sems.at[0])
-        arrived(ow_ref,sems.at[1])
-    vec=lambda k: vec_ref[k:k+1,:]
-    def add(k,v): vg_ref[k:k+1,:]+=jnp.sum(v,axis=0,keepdims=True)
-    gn=gr2_ref[...]+dg(gi_ref[...],uw_ref[...],NT)
-    u1=u1_ref[...]
-    add(G1,gn*u1); add(S1,gn)
-    gr1=norm_bwd(gn,u1,sc_ref[:,0:1],vec(G1))
-    gr1_ref[...]=gr1
-    ga=gr1.astype(bf)
-    ga_ref[...]=ga
-    add(OB,ga.astype(f32))
-    gm_ref[...]=dg(ga,ow_ref[...],NT).astype(bf)
-def back2(w,gr2,u1,sc,gi,vec,TR=256):
-    R,D=gr2.shape;F=gi.shape[1]
-    rb=lambda n: pl.BlockSpec((TR,n),lambda i:(i,0))
-    return pl.pallas_call(functools.partial(back2_kernel,TR),cost_estimate=takes(FAST),grid=(R//TR,),
-        in_specs=[ANYS,rb(D),rb(D),rb(128),rb(F),whole1(vec)],
-        out_specs=[rb(D),rb(D),rb(D),whole1(vec)],
-        out_shape=[sd((R,D),f32),sd((R,D),bf),sd((R,D),bf),vec],
-        scratch_shapes=[pltpu.VMEM((D,D),bf),pltpu.VMEM((D,F),bf),pltpu.SemaphoreType.DMA((2,))],
-        compiler_params=pltpu.CompilerParams(vmem_limit_bytes=56*2**20))(w,gr2,u1,sc,gi,vec)
-def wup_kernel(pos,m0,m1,m2,ga_ref,nl_ref,gi_ref,ka_ref,sa_ref,tmp_s):
-    D=ga_ref.shape[1];F=gi_ref.shape[1];H=D//2
-    core=pos[C_]
-    slots=[slot(pos,k) for k in range(BLK)]
-    mine,other=[pl.ds(pl.multiple_of(h*H,H),H) for h in (core,1-core)]
-    nlall=nl_ref[...]
-    for ref,h in ((sa_ref,1-core),(ka_ref,core)):
-        for c in range(F//D//2):
-            cols=pl.ds(pl.multiple_of(h*(F//2)+c*D,D),D)
-            t=dg(nlall,gi_ref[:,cols],TN).astype(bf)
-            for k in range(BLK):
-                ref[slots[k],:,H+c*D:H+(c+1)*D]=t[k*(D//BLK):(k+1)*(D//BLK)]
-    tmp_s[...]=dg(jnp.concatenate([m0[...],m1[...],m2[...]],axis=1),ga_ref[...],TN).astype(bf)
-    for k in range(BLK):
-        rows=slice(k*(D//BLK),(k+1)*(D//BLK))
-        ka_ref[slots[k],:,:H]=tmp_s[rows,mine]
-        sa_ref[slots[k],:,:H]=tmp_s[rows,other]
+    o=sd((BLK,D//BLK,(D+2*F)//2),bf)
+    return pl.pallas_call(functools.partial(mid_kernel,TR,len(scores),d1,len(mixed)),cost_estimate=takes(32),grid=(R//TR,),
+        in_specs=[SMEM]*2+[whole1(v) for v in scores]+[ANYS]*(3+len(mixed))+[rb(D),rb(D),rb(D),rb(128),rb(F),whole1(vec)],
+        out_specs=[rb(D),rb(D),whole1(vec),whole1(scores[0]),ANYS,ANYS],
+        out_shape=[sd((R,D),bf),sd((R,D),bf),vec,sd((8,128),f32),o,o],
+        scratch_shapes=[pltpu.VMEM((D,D),bf),pltpu.VMEM((D,F),bf),pltpu.VMEM((F,D),bf),pltpu.VMEM((R,F),bf),pltpu.VMEM((R,D),bf),pltpu.VMEM((R,D),bf),
+                        pltpu.VMEM((R,D),bf),pltpu.VMEM((R,F),bf),pltpu.VMEM((R,D),bf),pltpu.VMEM((2,BLK,D//BLK,D),bf),
+                        pltpu.SemaphoreType.DMA((8+len(mixed),)),pltpu.SemaphoreType.DMA((10,))],
+        compiler_params=pltpu.CompilerParams(vmem_limit_bytes=60*2**20))(pos,length,*scores,w,act,nl,*mixed,og,u2,u1,sc,gp,vec)
 VM=pl.BlockSpec(memory_space=pltpu.VMEM)
-def wup(pos,mixed,ga,nl,gi):
-    R,D=ga.shape;F=gi.shape[1]
-    o=sd((BLK,D//BLK,(D+F)//2),bf)
-    return pl.pallas_call(wup_kernel,cost_estimate=takes(FAST),in_specs=[SMEM]+[VM]*6,out_specs=[VM]*2,out_shape=[o,o],
-        scratch_shapes=[pltpu.VMEM((D,D),bf)],
-        compiler_params=pltpu.CompilerParams(vmem_limit_bytes=56*2**20))(pos,*mixed,ga,nl,gi)
+def small_kernel(buckets,n,vg,info,first,*refs):
+    diags,sums,sm_ref=refs[:n],refs[n:2*n],refs[2*n]
+    D=first.shape[1]
+    sm_ref[...]=jnp.zeros_like(sm_ref)
+    sm_ref[:CT]=vg[:CT]
+    at=0
+    for r in sums:
+        sm_ref[CT:CT+2,at:at+r.shape[1]]=r[0:2]
+        at+=r.shape[1]
+    sm_ref[CT+2:CT+3]=info[0:1,0:1]*first[0:1]
+    place=lax.broadcasted_iota(jnp.int32,(4*T,128),0)
+    off=jnp.where(place<3*T,place-T,place-5*T)
+    which=jnp.where(off>0,buckets//2,0)
+    for e in EDGES: which=which+(jnp.abs(off)>=e).astype(jnp.int32)
+    onehot=(which==lax.broadcasted_iota(jnp.int32,(4*T,128),1)).astype(f32)
+    diag=jnp.concatenate([d[h,0:1] for d in diags for h in range(d.shape[0])],axis=0)
+    sums=lax.dot_general(diag,onehot,NN,precision=lax.Precision.HIGHEST,preferred_element_type=f32)
+    sm_ref[CT+3:CT+3+diag.shape[0],:128]=sums
+    sm_ref[31:32]=jnp.broadcast_to(info[1:2,0:1],(1,D))
+def small_sums(buckets,vg,info,first,diags,sums):
+    return pl.pallas_call(functools.partial(small_kernel,buckets,len(diags)),cost_estimate=takes(2),in_specs=[VM]*(3+2*len(diags)),out_specs=VM,
+        out_shape=sd((32,first.shape[1]),f32))(vg,info,first,*diags,*sums)
 def wqkv_kernel(pos,hid_ref,*refs):
-    parts=refs[:9]; k_ref,s_ref,vb_ref,g_s=refs[9:]
+    *parts,k_ref,s_ref,g_s=refs
     D=hid_ref.shape[1];N=3*D
-    vb_ref[...]=jnp.zeros_like(vb_ref)
-    w=parts[0].shape[1]
-    for j,r in enumerate(parts):
-        g=r[...]
-        g_s[:,j*w:(j+1)*w]=g
-        row,lane=j//3,(j%3)*w
-        if row!=1: vb_ref[row//2:row//2+1,lane:lane+w]=jnp.sum(g.astype(f32),axis=0,keepdims=True)
+    at=0
+    for r in parts:
+        g_s[:,at:at+r.shape[1]]=r[...]
+        at+=r.shape[1]
     x=hid_ref[...]
     core=pos[C_]
     slots=[slot(pos,k) for k in range(BLK)]
@@ -434,24 +466,24 @@
 def wqkv(pos,hid,parts):
     R,D=hid.shape;N=3*D
     g=sd((BLK,D//BLK,N//2),bf)
-    return pl.pallas_call(wqkv_kernel,cost_estimate=takes(FAST),
-        in_specs=[SMEM]+[VM]*10,out_specs=[VM]*3,out_shape=[g,g,sd((8,D),f32)],
+    return pl.pallas_call(wqkv_kernel,cost_estimate=takes(9),
+        in_specs=[SMEM,VM]+[VM]*len(parts),out_specs=[VM]*2,out_shape=[g,g],
         scratch_shapes=[pltpu.VMEM((R,N),bf)],
         compiler_params=pltpu.CompilerParams(vmem_limit_bytes=60*2**20))(pos,hid,*parts)
 def hgrad_kernel(pos,*refs):
     pieces=refs[:8]
-    parts=refs[8:17]; gr1_ref,hg_ref,w_s,sems=refs[17:]
+    *parts,gr1_ref,hg_ref,w_s,sems=refs[8:]
     D=gr1_ref.shape[1];N=3*D
     @pl.when(pl.program_id(0)==0)
     def _():
         load(pos,pieces,[(0,N//2,w_s)],sems.at[0])
         arrived(w_s,sems.at[0])
     g=jnp.concatenate([r[...] for r in parts],axis=1)
-    hg_ref[...]=(gr1_ref[...]+dg(g,w_s[...],NT)).astype(bf)
+    hg_ref[...]=(gr1_ref[...].astype(f32)+dg(g,w_s[...],NT)).astype(bf)
 def hgrad(pos,pieces,parts,gr1,TR=256):
     R,D=gr1.shape;N=3*D
     rb=lambda n: pl.BlockSpec((TR,n),lambda i:(i,0))
-    return pl.pallas_call(hgrad_kernel,cost_estimate=takes(FAST),grid=(R//TR,),
+    return pl.pallas_call(hgrad_kernel,cost_estimate=takes(10),grid=(R//TR,),
         in_specs=[SMEM]+[ANYS]*8+[rb(p.shape[1]) for p in parts]+[rb(D)],
         out_specs=rb(D),out_shape=sd((R,D),bf),
         scratch_shapes=[pltpu.VMEM((D,N),bf),pltpu.SemaphoreType.DMA((1,))],
@@ -498,18 +530,17 @@
     ka2,sa2=add2(ka[:2],ra[:2]),add2(ka[2:],ra[2:])
     kb2,sb2=add2(kb[:2],rb[:2]),add2(kb[2:],rb[2:])
     return ka2,kb2,swap_y(sa2),swap_x(sb2)
-def collect3(ka2,kb2,ra,rb):
-    t0=ka2[0].astype(f32)+ra[0].astype(f32)
-    t1=add2(ka2[1],ra[1])
-    t2=add2(kb2[0],rb[0]);t3=add2(kb2[1],rb[1])
-    return t0,shift_z(t1,3),shift_z(t2,2),shift_z(t3,1)
+def collect3(*panels):
+    t=[[ka2[0].astype(f32)+ra[0].astype(f32),add2(ka2[1],ra[1]),add2(kb2[0],rb[0]),add2(kb2[1],rb[1])] for ka2,kb2,ra,rb in panels]
+    return [jnp.concatenate(v,axis=1) if len(v)>1 else v[0] for v in zip(*t)]
+def send3(t0,t1,t2,t3): return t0,shift_z(t1,3),shift_z(t2,2),shift_z(t3,1)
 def collect4(t0,t1,t2,t3):
     t=t0+t1.astype(f32)+t2.astype(f32)+t3.astype(f32)
     c=lax.axis_index("col")&1
     h=t.shape[0]//2
     mine=lax.dynamic_slice_in_dim(t,c*h,h,0)
     other=swap_core(lax.dynamic_slice_in_dim(t,(1-c)*h,h,0).astype(bf)).astype(f32)
-    return mine,other,c
+    return mine,other
 def afters(vs,*first):
     return list(lax.optimization_barrier(tuple(vs)+tuple(first))[:len(vs)])
 def sides(mine,other,c):
@@ -566,81 +597,68 @@
         p_qkv = spread_plain([both[:, : 3 * D], jnp.concatenate([panel, panel], axis=1)])
     strips, kx = tables(rel_bias, length[0], S)
     qkv, vec = qkv_fwd(pos, p_qkv, tokens)
-    attn = [attn_fwd(qkv, kx, strips, 2 * i, 2) for i in range(3)]
+    calls = ((0, 2), (2, rel_bias.shape[1] // 2 - 2))
+    attn = [attn_fwd(qkv, kx, strips, *call) for call in calls]
     mixed = [v[0] for v in attn]
     layer_out, u1, u2, sc, nl, act, gp, first, own_score = post_fwd(length, w_rest, mixed, tokens, vec)
     scores = [own_score] + [swap_col(own_score, r) for r in range(1, ncol)]
-    gr2, gi, vg1, kb, sb, info = back1(pos, length, scores, d1, w_rest, out_grad.reshape(S, D), u2, sc, act, gp, vec)
+    ga, gm, vg, info, keep, send = mid(pos, length, scores, d1, w_rest, out_grad.reshape(S, D), u2, u1, sc, act, gp, nl, mixed, vec)
     if fast:
-        rb0 = swap_core(sb)
-    gr1, ga, gm, vg2 = back2(w_rest, gr2, u1, sc, gi, vec)
+        r0 = swap_core(send)
+    back = lambda i, g: attn_bwd(qkv, g, attn[i][2], attn[i][1], attn[i][3], *calls[i])
+    grads = [back(0, gm)]
     if fast:
-        cb1 = collect1(*afters([kb, rb0], gm))
-        nl = afters([nl], cb1[0])[0]
-    ka, sa = wup(pos, mixed, ga, nl, gi)
-    gm_1 = afters([gm], ka)[0]
-    if fast:
-        ra0 = swap_core(sa)
-    back = lambda i, g: attn_bwd(qkv, g, attn[i][2], attn[i][1], attn[i][3], 2 * i, 2)
-    grads = [back(0, gm_1)]
-    gm_2 = afters([gm], grads[0][0])[0]
-    if fast:
-        ca1 = collect1(*afters([ka, ra0], grads[0][0]))
-        cb2 = collect2(*afters(cb1, ca1[0], ca1[1]))
-        gm_2 = afters([gm], cb2[0], cb2[1])[0]
+        c1 = collect1(*afters([keep, r0], grads[0][0]))
+        gm_2 = afters([gm], c1[0], c1[1])[0]
+    else:
+        gm_2 = gm
     grads.append(back(1, gm_2))
-    gm_3 = afters([gm], grads[1][0])[0]
-    if fast:
-        ca2 = collect2(*afters(ca1, grads[1][0]))
-        cb3 = collect3(*afters(cb2, ca2[0], ca2[1]))
-        gm_3 = afters([gm], ca2[0], ca2[1], cb3[0])[0]
-    grads.append(back(2, gm_3))
     parts = [g[j] for j in range(3) for g in grads]
-    if fast:
-        ca3 = collect3(*afters(ca2, grads[2][0]))
-        parts = afters(parts, ca3[0])
-    kq, sq, vb = wqkv(pos, tokens, parts)
-    if fast:
-        rq0 = swap_core(sq)
-        mb, ob, _ = collect4(*afters(cb3, kq))
-        cq1 = collect1(kq, rq0)
-        parts = afters(parts, cq1[0], cq1[1])
-    hidden_grad = hgrad(pos, p_qkv, parts, gr1)
-    near = cat([g[3] for g in grads])
-    far = cat([g[4] for g in grads])
-    ids = strip_ids()
-    onehot = (ids[:, :, None] == jnp.arange(rel_bias.shape[0], dtype=jnp.int32)).astype(f32)
-    bucket = jnp.einsum("hac,acb->bh", near, onehot, precision=lax.Precision.HIGHEST)
-    far = jnp.sum(far, axis=2)
-    bucket = bucket.at[15].add(far[:, 0]).at[31].add(far[:, 1])
-    weighted = info[1, :1]
-    last = jnp.concatenate([bucket.reshape(-1), weighted, jnp.zeros((D - bucket.size - 1,), f32)])
-    smalls = jnp.concatenate([(vg1 + vg2)[:CT], vb[:2], info[0, 0] * first[:1], last[None]], axis=0)
+    smalls = small_sums(rel_bias.shape[0], vg, info, first, [g[3] for g in grads], [g[4] for g in grads])
     h = D // 2
     if fast:
         smalls = smalls + swap_core(smalls)
-        smalls = smalls + swap_x(smalls)
+        travel = swap_x(smalls)
+        c2 = collect2(*afters(c1, smalls))
+        smalls = smalls + afters([travel], c2[0], c2[1])[0]
+        travel = swap_y(smalls)
+        parts = afters(parts, smalls, c2[0], c2[1])
+    kq, sq = wqkv(pos, tokens, parts)
+    if fast:
+        smalls = smalls + afters([travel], kq)[0]
+        rq0 = swap_core(afters([sq], smalls)[0])
+        c3 = collect3(afters(c2, kq, smalls))
+        cq1 = collect1(kq, afters([rq0], *c3)[0])
+        c3 = send3(*c3)
+        parts = afters(parts, cq1[0], cq1[1])
+        hidden_grad = hgrad(pos, p_qkv, parts, ga)
         cq2 = collect2(*afters(cq1, hidden_grad))
-        smalls = smalls + swap_y(afters([smalls], hidden_grad)[0])
-        ma, oa, _ = collect4(*afters(ca3, cq2[0], cq2[1]))
-        d_down = sides(mb, ob, c)
-        cq3 = collect3(*cq2)
-        smalls = smalls + flip_z(afters([smalls], cq3[0])[0], 1)
-        d_qkv = sides(*collect4(*cq3))
-        smalls = smalls + flip_z(smalls, 2)
-        d_out = sides(ma[:, :h], oa[:, :h], c)
-        d_up = sides(ma[:, h:], oa[:, h:], c)
+        m, o = collect4(*afters(c3, cq2[0], cq2[1]))
+        travel = flip_z(afters([smalls], m)[0], 1)
+        cq3 = collect3(afters(cq2, m))
+        n = (D + F) // 2
+        d_out = sides(m[:, :h], o[:, :h], c)
+        d_up = sides(m[:, h:n], o[:, h:n], c)
+        d_down = sides(m[:, n:], o[:, n:], c)
+        smalls = smalls + afters([travel], *cq3)[0]
+        travel = flip_z(smalls, 2)
+        m, o = collect4(*send3(*cq3))
+        smalls = smalls + afters([travel], m)[0]
+        d_qkv = sides(m, o, c)
     else:
+        hidden_grad = hgrad(pos, p_qkv, parts, ga)
         scatter = lambda w: lax.psum_scatter(w, ALL, scatter_dimension=0, tiled=True).astype(f32)
-        d_down, d_qkv = scatter(natural(kb, sb)), scatter(natural(kq, sq))
-        d_out = scatter(natural(ka[:, :, :h], sa[:, :, :h]))
-        d_up = scatter(natural(ka[:, :, h:], sa[:, :, h:]))
+        n = (D + F) // 2
+        d_qkv = scatter(natural(kq, sq))
+        d_out = scatter(natural(keep[:, :, :h], send[:, :, :h]))
+        d_up = scatter(natural(keep[:, :, h:n], send[:, :, h:n]))
+        d_down = scatter(natural(keep[:, :, n:], send[:, :, n:]))
         smalls = lax.psum(smalls, ALL)
     d_down = cat([d_down[:, j * D : (j + 1) * D] for j in range(4)])
     d_up = d_up.reshape(d1, 4, n_dev, d1).transpose(0, 2, 1, 3).reshape(d1, F)
     part = lax.dynamic_slice_in_dim(smalls, dev * d1, d1, axis=1)
-    loss = smalls[CT + 3, bucket.size] / info[2, 0]
-    bucket = smalls[CT + 3, : bucket.size].reshape(bucket.shape)
+    loss = smalls[31, 0] / info[2, 0]
+    bucket = smalls[CT + 3 : CT + 3 + rel_bias.shape[1], : rel_bias.shape[0]].T
     return (layer_out.reshape(hidden.shape), loss, hidden_grad.reshape(hidden.shape), d_qkv, part[CT : CT + 2],
             d_out, part[OB], part[G1], part[S1], d_up, part[UB : UB + 4].reshape(-1), d_down, part[DB], part[G2], part[S2],
             bucket, part[CT + 2])

time: 365 us -> 336 us (0.921)
  Pallas kernels: 175 us -> 155 us
  waiting for transfers between devices: 71.6 us -> 66.8 us
  matrix products: 5.01 us -> 1.04 us
    pallas_call x6 -> x5, Pallas kernels: 81.3 us -> 69.8 us  [the longest x1 40.3 us: mid(): pl.pallas_call(functools.partial(mid_kernel, TR, len(scores), d1, len(mix...]
    ppermute x2, starting transfers between devices: 0.9 us -> 6.82 us  [flip_z(): return lax.ppermute(v, 'pb', [(i, i ^ 2 * m) for i in range(8)])]
    ppermute x2, waiting for transfers between devices: 9.89 us -> 4.29 us  [flip_z(): return lax.ppermute(v, 'pb', [(i, i ^ 2 * m) for i in range(8)])]
    all_gather x1, waiting for transfers between devices: 13 us -> 17.6 us  [shards(): w_rest = lax.all_gather(rest, ALL, axis=0, tiled=True)]
    convert_element_type x15 -> x10, other arithmetic: 9.35 us -> 13.9 us  [add2(): return (a.astype(f32) + b.astype(f32)).astype(bf)]
    dot_general x1 -> x0, matrix products: 3.98 us -> none  [shards(): jnp.einsum('hac,acb->bh', near, onehot, precision=lax.Precision.HIGHEST)]
    ppermute x9 -> x7, waiting for transfers between devices: 13.8 us -> 10.2 us  [swap_y(): return lax.ppermute(v, 'pb', [(i, i ^ 1) for i in range(8)])]
    pallas_call x3 -> x2, Pallas kernels: 36.5 us -> 32.9 us  [attn_bwd(): pl.pallas_call(functools.partial(bwd_kernel, BQ, S, form, scale, kscale),...]
  transfers between devices with their start and end apart: 48 -> 39, of which waited for: 23 -> 16; matrix products, arithmetic and copies ran while one was open for 11% -> 10% of each run, Pallas kernels for 31% -> 27%
where the time goes in v3:
time: 336 us; the launch traced here: 330 us
  Pallas kernels  155 us (46%)
  waiting for transfers between devices  66.8 us (20%)
  starting transfers between devices  42.8 us (13%)
  other arithmetic  24.1 us (7%)
  local copies, waits for them, and re-layouts  20.6 us (6%)
  between operations  19.4 us (6%)
    pallas_call x1, Pallas kernels, mid(): pl.pallas_call(functools.partial(mid_kernel, TR, len(scores), d1, len(mix...  40.3 us
    pallas_call x2, Pallas kernels, attn_bwd(): pl.pallas_call(functools.partial(bwd_kernel, BQ, S, form, scale, kscale),...  32.9 us
    pallas_call x2, Pallas kernels, attn_fwd(): pl.pallas_call(functools.partial(fwd_kernel, BQ, S), cost_estimate=takes(...  28.2 us
    pallas_call x1, Pallas kernels, post_fwd(): pl.pallas_call(functools.partial(post_kernel, TR, mode), cost_estimate=ta...  24.1 us
    all_gather x1, waiting for transfers between devices, shards(): w_rest = lax.all_gather(rest, ALL, axis=0, tiled=True)  17.6 us
    ppermute x9, starting transfers between devices, shift_z(): return lax.ppermute(v, 'pb', [(i, (i + 2 * k) % 8) for i in range(8)])  17.2 us
    ppermute x9, waiting for transfers between devices, shift_z(): return lax.ppermute(v, 'pb', [(i, (i + 2 * k) % 8) for i in range(8)])  16.8 us
    ppermute x7, waiting for transfers between devices, swap_x(): return lax.ppermute(v, 'col', [(i, i ^ 2) for i in range(4)])  14.5 us
  transfers between devices with their start and end apart: 39, of which 16 were waited for; matrix products, arithmetic and copies ran while one was open for 10% of the time, Pallas kernels for 27%

profile of v3, /device:TPU:0, one launch (start us, length us, event | category | flops | bytes accessed | tf_op | source)
XLA Modules:
  0.0 329.6 jit_solution(8654374632894987740)
XLA Ops:
  15.6 3.7 %collective-permute-start.3 = (bf16[1,48,1280]{2,1,0:T(8,128)(2,1)S(1)}, bf16[1,48,1280]{2,1,0:T(8,128)(2,1)S(1)}, u32[]{:S(2)}, u32[]{:S(2)}) collective-permute-start(bf16[1,48,1280]{2,1,0:T(8,128)(2,1)S(1)} %maximum_select_fusion.3), channel_id=1, source_target_pairs={{0,16},{4,20},{8,24},{12,28},{16,0},{20,4},{24,8},{28,12},{1,17},{... | collective-permute-start | bytes 368648 | tf_op jit(solution)/shard_map/ppermute | solution.py:500
  22.0 4.1 %collective-permute-done.3 = bf16[1,48,1280]{2,1,0:T(8,128)(2,1)S(1)} collective-permute-done((bf16[1,48,1280]{2,1,0:T(8,128)(2,1)S(1)}, bf16[1,48,1280]{2,1,0:T(8,128)(2,1)S(1)}, u32[]{:S(2)}, u32[]{:S(2)}) %collective-permute-start.3) | collective-permute-done | bytes 122912 | tf_op jit(solution)/shard_map/ppermute | solution.py:500
  35.8 4.2 %collective-permute-done.2 = bf16[2,48,1280]{2,1,0:T(8,128)(2,1)S(1)} collective-permute-done((bf16[2,48,1280]{2,1,0:T(8,128)(2,1)S(1)}, bf16[2,48,1280]{2,1,0:T(8,128)(2,1)S(1)}, u32[]{:S(2)}, u32[]{:S(2)}) %collective-permute-start.2) | collective-permute-done | bytes 245792 | tf_op jit(solution)/shard_map/ppermute | solution.py:498
  46.2 4.5 %collective-permute-done.7.refs_3_ = bf16[4,48,1280]{2,1,0:T(8,128)(2,1)} collective-permute-done((bf16[4,48,1280]{2,1,0:T(8,128)(2,1)}, bf16[4,48,1280]{2,1,0:T(8,128)(2,1)}, u32[]{:S(2)}, u32[]{:S(2)}) %collective-permute-start.7) | collective-permute-done | bytes 491552 | tf_op jit(solution)/shard_map/ppermute | solution.py:498
  50.7 4.8 %collective-permute-done.6.refs_2_ = bf16[4,48,1280]{2,1,0:T(8,128)(2,1)} collective-permute-done((bf16[4,48,1280]{2,1,0:T(8,128)(2,1)}, bf16[4,48,1280]{2,1,0:T(8,128)(2,1)}, u32[]{:S(2)}, u32[]{:S(2)}) %collective-permute-start.6) | collective-permute-done | bytes 491552 | tf_op jit(solution)/shard_map/ppermute | solution.py:497
  59.5 9.4 %shard_map.314 = (bf16[1024,2304]{1,0:T(8,128)(2,1)}, f32[24,768]{1,0:T(8,128)}) custom-call(s32[6]{0:T(128)} %stack.27.pos, bf16[4,48,1280]{2,1,0:T(8,128)(2,1)} %pad_maximum_fusion.refs_0_, bf16[4,48,1280]{2,1,0:T(8,128)(2,1)} %constant_dynamic-update-slice_fusion.2.refs_1_, bf16[4,48,1280]{2,1,0:T(8,128)(2,1)} %collective-permute-done.6.refs_2_, ...), custom_call_target="tpu_custom_call" | custom-call | flops 10350000128 | bytes 9000000 | tf_op jit(solution)/shard_map/pallas_call | solution.py:230
  68.9 10.4 %shard_map.315 = (bf16[1024,256]{1,0:T(8,128)(2,1)}, f32[1024,256]{1,0:T(8,128)}, f32[1024,256]{1,0:T(8,128)}, bf16[4,1024,1024]{2,1,0:T(8,128)(2,1)}) custom-call(bf16[1024,2304]{1,0:T(8,128)(2,1)} %get-tuple-element.96.q_ref.k_ref.v_ref, bf16[1024,2304]{1,0:T(8,128)(2,1)} %get-tuple-element.96.q_ref.k_ref.v_ref, ...), custom_call_target="tpu_custom_call" | custom-call | flops 11500000256 | bytes 10000000 | tf_op jit(solution)/shard_map/pallas_call | solution.py:75
  79.3 17.8 %shard_map.316 = (bf16[1024,512]{1,0:T(8,128)(2,1)}, f32[1024,512]{1,0:T(8,128)}, f32[1024,512]{1,0:T(8,128)}, bf16[8,1024,1024]{2,1,0:T(8,128)(2,1)}) custom-call(bf16[1024,2304]{1,0:T(8,128)(2,1)} %get-tuple-element.96.q_ref.k_ref.v_ref, bf16[1024,2304]{1,0:T(8,128)(2,1)} %get-tuple-element.96.q_ref.k_ref.v_ref, ...), custom_call_target="tpu_custom_call" | custom-call | flops 23000000512 | bytes 20000000 | tf_op jit(solution)/shard_map/pallas_call | solution.py:75
  97.1 17.6 %all-gather.2.cloned.1.call-done.refs_0_.refs_4_ = bf16[768,6912]{1,0:T(8,128)(2,1)} async-done(((bf16[24,6912]{1,0:T(8,128)(2,1)}), bf16[768,6912]{1,0:T(8,128)(2,1)}) %all-gather.2.cloned.1.call-update) | async-done | bytes 10616848 | tf_op jit(solution)/shard_map/all_gather | solution.py:585
  114.7 24.1 %shard_map.317 = (bf16[1024,768]{1,0:T(8,128)(2,1)}, bf16[1024,768]{1,0:T(8,128)(2,1)}, bf16[1024,768]{1,0:T(8,128)(2,1)}, f32[1024,128]{1,0:T(8,128)}, bf16[102...) custom-call(s32[1]{0:T(128)} %bitcast.69.len_ref, ...), custom_call_target="tpu_custom_call" | custom-call | flops 28750000128 | bytes 25000000 | tf_op jit(solution)/shard_map/pallas_call | solution.py:292
  144.5 40.3 %shard_map.318 = (bf16[1024,768]{1,0:T(8,128)(2,1)}, bf16[1024,768]{1,0:T(8,128)(2,1)}, f32[24,768]{1,0:T(8,128)}, f32[8,128]{1,0:T(8,128)}, bf16[16,48,3456]{2,...) custom-call(s32[6]{0:T(128)} %stack.27.pos, s32[1]{0:T(128)} %bitcast.70.len_ref, f32[8,128]{1,0:T(8,128)} %get-tuple-element.101.refs_0_, ...), custom_call_target="tpu_custom_call" | custom-call | flops 36800000000 | bytes 32000000 | tf_op jit(solution)/shard_map/pallas_call | solution.py:421
  184.9 12.2 %shard_map.319 = (bf16[1024,256]{1,0:T(8,128)(2,1)}, bf16[1024,256]{1,0:T(8,128)(2,1)}, bf16[1024,256]{1,0:T(8,128)(2,1)}, f32[4,8,512]{2,1,0:T(8,128)}, f32[8,256]{1,0:T(8,128)}) custom-call(bf16[1024,2304]{1,0:T(8,128)(2,1)} %get-tuple-element.96.q_ref.k_ref.v_ref, bf16[1024,2304]{1,0:T(8,128)(2,1)} %get-tuple-element.96.q_ref.k_ref.v_ref, ...), custom_call_target="tpu_custom_call" | custom-call | flops 13799999488 | bytes 12000000 | tf_op jit(solution)/shard_map/pallas_call | solution.py:153
  197.1 4.2 %add_convert_fusion = (bf16[4,48,3456]{2,1,0:T(8,128)(2,1)}, bf16[4,48,3456]{2,1,0:T(8,128)(2,1)}, bf16[4,48,3456]{2,1,0:T(8,128)(2,1)S(1)}, bf16[4,48,3456]{2,1,0:T(8,128)(2,1)S(1)}) fusion(bf16[16,48,3456]{2,1,0:T(8,128)(2,1)} %collective-permute-done.15, bf16[16,48,3456]{2,1,0:T(8,128)(2,1)S(1)} %bitcast.73), kind=kLoop, calls=%fused_computation.4 | loop fusion | flops 10616832 | bytes 15925248 | tf_op jit(solution)/shard_map/convert_element_type | solution.py:525
  203.5 20.7 %shard_map.320 = (bf16[1024,512]{1,0:T(8,128)(2,1)}, bf16[1024,512]{1,0:T(8,128)(2,1)}, bf16[1024,512]{1,0:T(8,128)(2,1)}, f32[8,8,512]{2,1,0:T(8,128)}, f32[8,512]{1,0:T(8,128)}) custom-call(bf16[1024,2304]{1,0:T(8,128)(2,1)} %get-tuple-element.96.q_ref.k_ref.v_ref, bf16[1024,2304]{1,0:T(8,128)(2,1)} %get-tuple-element.96.q_ref.k_ref.v_ref, ...), custom_call_target="tpu_custom_call" | custom-call | flops 27599998976 | bytes 24000000 | tf_op jit(solution)/shard_map/pallas_call | solution.py:153
  229.2 4.4 %collective-permute-done.18 = bf16[4,48,3456]{2,1,0:T(8,128)(2,1)} collective-permute-done((bf16[4,48,3456]{2,1,0:T(8,128)(2,1)}, bf16[4,48,3456]{2,1,0:T(8,128)(2,1)}, u32[]{:S(2)}, u32[]{:S(2)}) %collective-permute-start.18) | collective-permute-done | bytes 1327136 | tf_op jit(solution)/shard_map/ppermute | solution.py:497
  241.9 8.6 %shard_map.322 = (bf16[16,48,1152]{2,1,0:T(8,128)(2,1)}, bf16[16,48,1152]{2,1,0:T(8,128)(2,1)}) custom-call(s32[6]{0:T(128)} %stack.27.pos, bf16[1024,768]{1,0:T(8,128)(2,1)} %bitcast.81, bf16[1024,256]{1,0:T(8,128)(2,1)} %get-tuple-element.153.refs_0_.refs_8_, bf16[1024,512]{1,0:T(8,128)(2,1)} %get-tuple-element.154.refs_1_.refs_9_, ...), custom_call_target="tpu_custom_call" | custom-call | flops 10350000128 | bytes 9000000 | tf_op jit(solution)/shard_map/pallas_call | solution.py:469
  250.6 5.3 %collective-permute-done.22 = bf16[2,48,3456]{2,1,0:T(8,128)(2,1)S(1)} collective-permute-done((bf16[2,48,3456]{2,1,0:T(8,128)(2,1)}, bf16[2,48,3456]{2,1,0:T(8,128)(2,1)S(1)}, u32[]{:S(2)}, u32[]{:S(2)}) %collective-permute-start.22) | collective-permute-done | bytes 663584 | tf_op jit(solution)/shard_map/ppermute | solution.py:497
  261.6 3.2 collective-permute-start.23
  268.1 9.6 %shard_map.323 = bf16[1024,768]{1,0:T(8,128)(2,1)} custom-call(s32[6]{0:T(128)} %stack.27.pos, bf16[4,48,1280]{2,1,0:T(8,128)(2,1)} %pad_maximum_fusion.refs_0_, bf16[4,48,1280]{2,1,0:T(8,128)(2,1)} %constant_dynamic-update-slice_fusion.2.refs_1_, bf16[4,48,1280]{2,1,0:T(8,128)(2,1)} %collective-permute-done.6.refs_2_, ...), custom_call_target="tpu_custom_call" | custom-call | flops 11500000256 | bytes 10000000 | tf_op jit(solution)/shard_map/pallas_call | solution.py:486
  279.3 3.8 %collective-permute-done.24 = bf16[48,3456]{1,0:T(8,128)(2,1)} collective-permute-done((bf16[48,3456]{1,0:T(8,128)(2,1)}, bf16[48,3456]{1,0:T(8,128)(2,1)}, u32[]{:S(2)}, u32[]{:S(2)}) %collective-permute-start.24) | collective-permute-done | bytes 331808 | tf_op jit(solution)/shard_map/ppermute | solution.py:500
  287.3 6.7 %collective-permute-start.29 = (f32[32,768]{1,0:T(8,128)S(1)}, f32[32,768]{1,0:T(8,128)}, u32[]{:S(2)}, u32[]{:S(2)}) collective-permute-start(f32[32,768]{1,0:T(8,128)S(1)} %add.294), channel_id=1, source_target_pairs={{0,8},{4,12},{8,0},{12,4},{16,24},{20,28},{24,16},{28,20},{1,9},{5... | collective-permute-start | bytes 294920 | tf_op jit(solution)/shard_map/ppermute | solution.py:499
  301.9 3.5 %collective-permute-start.33 = (bf16[48,1152]{1,0:T(8,128)(2,1)S(1)}, bf16[48,1152]{1,0:T(8,128)(2,1)S(1)}, u32[]{:S(2)}, u32[]{:S(2)}) collective-permute-start(bf16[48,1152]{1,0:T(8,128)(2,1)S(1)} %fusion.23), channel_id=1, source_target_pairs={{0,24},{4,28},{8,0},{12,4},{16,8},{20,12},{24,16},{28,20},{1,25},{... | collective-permute-start | bytes 331784 | tf_op jit(solution)/shard_map/ppermute | solution.py:500
  307.1 4.9 %collective-permute-done.34 = bf16[48,1152]{1,0:T(8,128)(2,1)S(1)} collective-permute-done((bf16[48,1152]{1,0:T(8,128)(2,1)S(1)}, bf16[48,1152]{1,0:T(8,128)(2,1)S(1)}, u32[]{:S(2)}, u32[]{:S(2)}) %collective-permute-start.34) | collective-permute-done | bytes 110624 | tf_op jit(solution)/shard_map/ppermute | solution.py:500
  312.1 4.3 %collective-permute-done.32 = f32[32,768]{1,0:T(8,128)S(1)} collective-permute-done((f32[32,768]{1,0:T(8,128)S(1)}, f32[32,768]{1,0:T(8,128)S(1)}, u32[]{:S(2)}, u32[]{:S(2)}) %collective-permute-start.32) | collective-permute-done | bytes 98336 | tf_op jit(solution)/shard_map/ppermute | solution.py:499
  (201 shorter events, 78.0 us)
Async XLA Ops:
  7.2 107.5 %all-gather.2.cloned.1.call-start = ((), (), s32[]{:S(2)}) async-start(), calls=%async_computation | async-start | bytes 10948608 | tf_op jit(solution)/shard_map/all_gather | solution.py:585
  15.6 10.5 %collective-permute-start.3 = (bf16[1,48,1280]{2,1,0:T(8,128)(2,1)S(1)}, bf16[1,48,1280]{2,1,0:T(8,128)(2,1)S(1)}, u32[]{:S(2)}, u32[]{:S(2)}) collective-permute-start(bf16[1,48,1280]{2,1,0:T(8,128)(2,1)S(1)} %maximum_select_fusion.3), channel_id=1, source_target_pairs={{0,16},{4,20},{8,24},{12,28},{16,0},{20,4},{24,8},{28,12},{1,17},{... | collective-permute-start | bytes 368648 | tf_op jit(solution)/shard_map/ppermute | solution.py:500
  21.2 10.3 %collective-permute-start.1 = (bf16[1,48,1280]{2,1,0:T(8,128)(2,1)S(1)}, bf16[1,48,1280]{2,1,0:T(8,128)(2,1)S(1)}, u32[]{:S(2)}, u32[]{:S(2)}) collective-permute-start(bf16[1,48,1280]{2,1,0:T(8,128)(2,1)S(1)} %maximum_select_fusion.3), channel_id=1, source_target_pairs={{0,8},{4,12},{8,16},{12,20},{16,24},{20,28},{24,0},{28,4},{1,9},{5... | collective-permute-start | bytes 368648 | tf_op jit(solution)/shard_map/ppermute | solution.py:500
  35.2 15.4 %collective-permute-start.7 = (bf16[4,48,1280]{2,1,0:T(8,128)(2,1)}, bf16[4,48,1280]{2,1,0:T(8,128)(2,1)}, u32[]{:S(2)}, u32[]{:S(2)}) collective-permute-start(bf16[4,48,1280]{2,1,0:T(8,128)(2,1)} %constant_dynamic-update-slice_fusion.2.refs_1_), channel_id=1, source_target_pairs={{0,4},{4,0},{8,12},{12,8},{16,20},{20,16},{24,28},{28,24},{1,5},{5... | collective-permute-start | bytes 1474568 | tf_op jit(solution)/shard_map/ppermute | solution.py:498
  40.9 14.5 %collective-permute-start.6 = (bf16[4,48,1280]{2,1,0:T(8,128)(2,1)}, bf16[4,48,1280]{2,1,0:T(8,128)(2,1)}, u32[]{:S(2)}, u32[]{:S(2)}) collective-permute-start(bf16[4,48,1280]{2,1,0:T(8,128)(2,1)} %pad_maximum_fusion.refs_0_), channel_id=1, source_target_pairs={{0,2},{1,3},{2,0},{3,1},{4,6},{5,7},{6,4},{7,5},{8,10},{9,11},{10,... | collective-permute-start | bytes 1474568 | tf_op jit(solution)/shard_map/ppermute | solution.py:497
  45.6 12.6 %collective-permute-start.9 = (bf16[4,48,1280]{2,1,0:T(8,128)(2,1)}, bf16[4,48,1280]{2,1,0:T(8,128)(2,1)S(1)}, u32[]{:S(2)}, u32[]{:S(2)}) collective-permute-start(bf16[4,48,1280]{2,1,0:T(8,128)(2,1)} %constant_dynamic-update-slice_fusion.2.refs_1_), channel_id=1, source_target_pairs={{0,1},{1,0},{2,3},{3,2},{4,5},{5,4},{6,7},{7,6},{8,9},{9,8},{10,11... | collective-permute-start | bytes 1474568 | tf_op jit(solution)/shard_map/ppermute | solution.py:495
  45.7 12.5 %collective-permute-start.8 = (bf16[4,48,1280]{2,1,0:T(8,128)(2,1)}, bf16[4,48,1280]{2,1,0:T(8,128)(2,1)S(1)}, u32[]{:S(2)}, u32[]{:S(2)}) collective-permute-start(bf16[4,48,1280]{2,1,0:T(8,128)(2,1)} %pad_maximum_fusion.refs_0_), channel_id=1, source_target_pairs={{0,1},{1,0},{2,3},{3,2},{4,5},{5,4},{6,7},{7,6},{8,9},{9,8},{10,11... | collective-permute-start | bytes 1474568 | tf_op jit(solution)/shard_map/ppermute | solution.py:495
  184.7 12.4 %collective-permute-start.15 = (bf16[16,48,3456]{2,1,0:T(8,128)(2,1)}, bf16[16,48,3456]{2,1,0:T(8,128)(2,1)}, u32[]{:S(2)}, u32[]{:S(2)}) collective-permute-start(bf16[16,48,3456]{2,1,0:T(8,128)(2,1)} %get-tuple-element.117), channel_id=1, source_target_pairs={{0,1},{1,0},{2,3},{3,2},{4,5},{5,4},{6,7},{7,6},{8,9},{9,8},{10,11... | collective-permute-start | bytes 15925256 | tf_op jit(solution)/shard_map/ppermute | solution.py:495
  201.4 32.2 %collective-permute-start.18 = (bf16[4,48,3456]{2,1,0:T(8,128)(2,1)}, bf16[4,48,3456]{2,1,0:T(8,128)(2,1)}, u32[]{:S(2)}, u32[]{:S(2)}) collective-permute-start(bf16[4,48,3456]{2,1,0:T(8,128)(2,1)} %get-tuple-element.178), channel_id=1, source_target_pairs={{0,2},{1,3},{2,0},{3,1},{4,6},{5,7},{6,4},{7,5},{8,10},{9,11},{10,... | collective-permute-start | bytes 3981320 | tf_op jit(solution)/shard_map/ppermute | solution.py:497
  202.0 31.6 %collective-permute-start.19 = (bf16[4,48,3456]{2,1,0:T(8,128)(2,1)}, bf16[4,48,3456]{2,1,0:T(8,128)(2,1)}, u32[]{:S(2)}, u32[]{:S(2)}) collective-permute-start(bf16[4,48,3456]{2,1,0:T(8,128)(2,1)} %get-tuple-element.177), channel_id=1, source_target_pairs={{0,4},{4,0},{8,12},{12,8},{16,20},{20,16},{24,28},{28,24},{1,5},{5... | collective-permute-start | bytes 3981320 | tf_op jit(solution)/shard_map/ppermute | solution.py:498
  238.5 12.0 %collective-permute-start.20 = (f32[32,768]{1,0:T(8,128)S(1)}, f32[32,768]{1,0:T(8,128)S(1)}, u32[]{:S(2)}, u32[]{:S(2)}) collective-permute-start(f32[32,768]{1,0:T(8,128)S(1)} %add.293), channel_id=1, source_target_pairs={{0,4},{4,0},{8,12},{12,8},{16,20},{20,16},{24,28},{28,24},{1,5},{5... | collective-permute-start | bytes 294920 | tf_op jit(solution)/shard_map/ppermute | solution.py:498
  239.9 16.0 %collective-permute-start.22 = (bf16[2,48,3456]{2,1,0:T(8,128)(2,1)}, bf16[2,48,3456]{2,1,0:T(8,128)(2,1)S(1)}, u32[]{:S(2)}, u32[]{:S(2)}) collective-permute-start(bf16[2,48,3456]{2,1,0:T(8,128)(2,1)} %get-tuple-element.185), channel_id=1, source_target_pairs={{0,2},{1,3},{2,0},{3,1},{4,6},{5,7},{6,4},{7,5},{8,10},{9,11},{10,... | collective-permute-start | bytes 1990664 | tf_op jit(solution)/shard_map/ppermute | solution.py:497
  240.7 16.6 %collective-permute-start.21 = (bf16[2,48,3456]{2,1,0:T(8,128)(2,1)}, bf16[2,48,3456]{2,1,0:T(8,128)(2,1)S(1)}, u32[]{:S(2)}, u32[]{:S(2)}) collective-permute-start(bf16[2,48,3456]{2,1,0:T(8,128)(2,1)} %get-tuple-element.187), channel_id=1, source_target_pairs={{0,4},{4,0},{8,12},{12,8},{16,20},{20,16},{24,28},{28,24},{1,5},{5... | collective-permute-start | bytes 1990664 | tf_op jit(solution)/shard_map/ppermute | solution.py:498
  250.5 14.4 %collective-permute-start.26 = (bf16[16,48,1152]{2,1,0:T(8,128)(2,1)}, bf16[16,48,1152]{2,1,0:T(8,128)(2,1)S(1)}, u32[]{:S(2)}, u32[]{:S(2)}) collective-permute-start(bf16[16,48,1152]{2,1,0:T(8,128)(2,1)} %get-tuple-element.151), channel_id=1, source_target_pairs={{0,1},{1,0},{2,3},{3,2},{4,5},{5,4},{6,7},{7,6},{8,9},{9,8},{10,11... | collective-permute-start | bytes 5308424 | tf_op jit(solution)/shard_map/ppermute | solution.py:495
  258.3 24.8 %collective-permute-start.24 = (bf16[48,3456]{1,0:T(8,128)(2,1)}, bf16[48,3456]{1,0:T(8,128)(2,1)}, u32[]{:S(2)}, u32[]{:S(2)}) collective-permute-start(bf16[48,3456]{1,0:T(8,128)(2,1)} %get-tuple-element.190), channel_id=1, source_target_pairs={{0,16},{4,20},{8,24},{12,28},{16,0},{20,4},{24,8},{28,12},{1,17},{... | collective-permute-start | bytes 995336 | tf_op jit(solution)/shard_map/ppermute | solution.py:500
  260.1 23.0 %collective-permute-start.25 = (bf16[48,3456]{1,0:T(8,128)(2,1)}, bf16[48,3456]{1,0:T(8,128)(2,1)}, u32[]{:S(2)}, u32[]{:S(2)}) collective-permute-start(bf16[48,3456]{1,0:T(8,128)(2,1)} %get-tuple-element.189), channel_id=1, source_target_pairs={{0,8},{4,12},{8,16},{12,20},{16,24},{20,28},{24,0},{28,4},{1,9},{5... | collective-permute-start | bytes 995336 | tf_op jit(solution)/shard_map/ppermute | solution.py:500
  261.6 21.5 %collective-permute-start.23 = (bf16[48,3456]{1,0:T(8,128)(2,1)}, bf16[48,3456]{1,0:T(8,128)(2,1)}, u32[]{:S(2)}, u32[]{:S(2)}) collective-permute-start(bf16[48,3456]{1,0:T(8,128)(2,1)} %get-tuple-element.191), channel_id=1, source_target_pairs={{0,24},{4,28},{8,0},{12,4},{16,8},{20,12},{24,16},{28,20},{1,25},{... | collective-permute-start | bytes 995336 | tf_op jit(solution)/shard_map/ppermute | solution.py:500
  266.1 11.6 %collective-permute-start.27 = (bf16[4,48,1152]{2,1,0:T(8,128)(2,1)}, bf16[4,48,1152]{2,1,0:T(8,128)(2,1)S(1)}, u32[]{:S(2)}, u32[]{:S(2)}) collective-permute-start(bf16[4,48,1152]{2,1,0:T(8,128)(2,1)} %get-tuple-element.182), channel_id=1, source_target_pairs={{0,2},{1,3},{2,0},{3,1},{4,6},{5,7},{6,4},{7,5},{8,10},{9,11},{10,... | collective-permute-start | bytes 1327112 | tf_op jit(solution)/shard_map/ppermute | solution.py:497
  267.4 10.3 %collective-permute-start.28 = (bf16[4,48,1152]{2,1,0:T(8,128)(2,1)S(1)}, bf16[4,48,1152]{2,1,0:T(8,128)(2,1)S(1)}, u32[]{:S(2)}, u32[]{:S(2)}) collective-permute-start(bf16[4,48,1152]{2,1,0:T(8,128)(2,1)S(1)} %get-tuple-element.181), channel_id=1, source_target_pairs={{0,4},{4,0},{8,12},{12,8},{16,20},{20,16},{24,28},{28,24},{1,5},{5... | collective-permute-start | bytes 1327112 | tf_op jit(solution)/shard_map/ppermute | solution.py:498
  285.2 14.3 %collective-permute-start.31 = (bf16[2,48,1152]{2,1,0:T(8,128)(2,1)}, bf16[2,48,1152]{2,1,0:T(8,128)(2,1)S(1)}, u32[]{:S(2)}, u32[]{:S(2)}) collective-permute-start(bf16[2,48,1152]{2,1,0:T(8,128)(2,1)} %get-tuple-element.193), channel_id=1, source_target_pairs={{0,2},{1,3},{2,0},{3,1},{4,6},{5,7},{6,4},{7,5},{8,10},{9,11},{10,... | collective-permute-start | bytes 663560 | tf_op jit(solution)/shard_map/ppermute | solution.py:497
  286.7 12.8 %collective-permute-start.30 = (bf16[2,48,1152]{2,1,0:T(8,128)(2,1)}, bf16[2,48,1152]{2,1,0:T(8,128)(2,1)S(1)}, u32[]{:S(2)}, u32[]{:S(2)}) collective-permute-start(bf16[2,48,1152]{2,1,0:T(8,128)(2,1)} %get-tuple-element.195), channel_id=1, source_target_pairs={{0,4},{4,0},{8,12},{12,8},{16,20},{20,16},{24,28},{28,24},{1,5},{5... | collective-permute-start | bytes 663560 | tf_op jit(solution)/shard_map/ppermute | solution.py:498
  287.3 18.8 %collective-permute-start.29 = (f32[32,768]{1,0:T(8,128)S(1)}, f32[32,768]{1,0:T(8,128)}, u32[]{:S(2)}, u32[]{:S(2)}) collective-permute-start(f32[32,768]{1,0:T(8,128)S(1)} %add.294), channel_id=1, source_target_pairs={{0,8},{4,12},{8,0},{12,4},{16,24},{20,28},{24,16},{28,20},{1,9},{5... | collective-permute-start | bytes 294920 | tf_op jit(solution)/shard_map/ppermute | solution.py:499
  299.5 12.4 %collective-permute-start.34 = (bf16[48,1152]{1,0:T(8,128)(2,1)S(1)}, bf16[48,1152]{1,0:T(8,128)(2,1)S(1)}, u32[]{:S(2)}, u32[]{:S(2)}) collective-permute-start(bf16[48,1152]{1,0:T(8,128)(2,1)S(1)} %get-tuple-element.202), channel_id=1, source_target_pairs={{0,16},{4,20},{8,24},{12,28},{16,0},{20,4},{24,8},{28,12},{1,17},{... | collective-permute-start | bytes 331784 | tf_op jit(solution)/shard_map/ppermute | solution.py:500
  301.5 10.4 %collective-permute-start.35 = (bf16[48,1152]{1,0:T(8,128)(2,1)S(1)}, bf16[48,1152]{1,0:T(8,128)(2,1)S(1)}, u32[]{:S(2)}, u32[]{:S(2)}) collective-permute-start(bf16[48,1152]{1,0:T(8,128)(2,1)S(1)} %get-tuple-element.201), channel_id=1, source_target_pairs={{0,8},{4,12},{8,16},{12,20},{16,24},{20,28},{24,0},{28,4},{1,9},{5... | collective-permute-start | bytes 331784 | tf_op jit(solution)/shard_map/ppermute | solution.py:500
  (39 other events, 183.9 us)
Sparse Core Ops, SparseCore 0:
  11.9 102.7 all-gather.1

commit v4 on v3

--- a/solution.py
+++ b/solution.py
@@ -180,6 +180,7 @@
 def whole(a): return pl.BlockSpec(memory_space=pltpu.VMEM)
 
 BLK=16
+SUB=2
 RELA=((0,0,0),(0,0,1),(0,1,0),(0,1,1))
 RELB=((0,0,2),(0,0,3),(1,0,2),(1,0,3))
 RELXA=((1,0,0),(1,0,1),(1,1,0),(1,1,1))
@@ -253,39 +254,50 @@
         fetch(w,D,uw_ref,sems.at[5])
         fetch_down(w,D+F,dw_ref,sems)
         arrived(ow_ref,sems.at[4])
-    vec=lambda n: vec_ref[n:n+1,:]
-    r=hid_ref[...].astype(f32)+(dg(jnp.concatenate([m[...] for m in parts],axis=1),ow_ref[...])+vec(OB))
-    u1,s1=norm(r)
-    u1_ref[...]=u1.astype(bf)
-    n=u1*vec(G1)+vec(S1)
-    nl=n.astype(bf)
-    nl_ref[...]=nl
-    @pl.when(i==0)
-    def _():
         arrived(uw_ref,sems.at[5])
         arrived_down(dw_ref,sems)
-    br=None
-    for c in range(F//D):
-        x=dg(nl,uw_ref[:,c*D:(c+1)*D])+vec(UB+c)
-        a,gp=gelu_both(x,mode)
-        a=a.astype(bf)
-        act_ref[:,c*D:(c+1)*D]=a
-        gp_ref[:,c*D:(c+1)*D]=gp.astype(bf)
-        b=dg(a,dw_ref[c*D:(c+1)*D,:])
-        br=b if br is None else br+b
-    u2,s2=norm(n+(br+vec(DB)))
-    u2_ref[...]=u2.astype(bf)
-    fin=u2*vec(G2)+vec(S2)
-    row=lax.broadcasted_iota(jnp.int32,(TR,D),0)+i*TR
-    lo_ref[...]=jnp.where(row<len_ref[0],fin,0.0).astype(bf)
-    lane=lax.broadcasted_iota(jnp.int32,(TR,128),1)
-    sc_ref[...]=jnp.where(lane==0,s1,s2)
+    vec=lambda n: vec_ref[n:n+1,:]
+    HR=TR//SUB
+    halves=[slice(q*HR,(q+1)*HR) for q in range(SUB)]
+    def one(h):
+        r=hid_ref[h,:].astype(f32)+(dg(jnp.concatenate([m[h,:] for m in parts],axis=1),ow_ref[...])+vec(OB))
+        return norm(r)
+    def two(h,u1):
+        u1_ref[h,:]=u1.astype(bf)
+        n=u1*vec(G1)+vec(S1)
+        nl=n.astype(bf)
+        nl_ref[h,:]=nl
+        return n,nl
+    def three(h,nl):
+        br=None
+        for c in range(F//D):
+            x=dg(nl,uw_ref[:,c*D:(c+1)*D])+vec(UB+c)
+            a,gp=gelu_both(x,mode)
+            a=a.astype(bf)
+            act_ref[h,c*D:(c+1)*D]=a
+            gp_ref[h,c*D:(c+1)*D]=gp.astype(bf)
+            b=dg(a,dw_ref[c*D:(c+1)*D,:])
+            br=b if br is None else br+b
+        return br
+    def four(q,h,n,br,s1):
+        u2,s2=norm(n+(br+vec(DB)))
+        u2_ref[h,:]=u2.astype(bf)
+        fin=u2*vec(G2)+vec(S2)
+        row=lax.broadcasted_iota(jnp.int32,(HR,D),0)+i*TR+q*HR
+        lo_ref[h,:]=jnp.where(row<len_ref[0],fin,0.0).astype(bf)
+        lane=lax.broadcasted_iota(jnp.int32,(HR,128),1)
+        sc_ref[h,:]=jnp.where(lane==0,s1,s2)
+        return fin
+    us=[one(h) for h in halves]
+    ns=[two(h,u[0]) for h,u in zip(halves,us)]
+    brs=[three(h,n[1]) for h,n in zip(halves,ns)]
+    fin=[four(q,h,ns[q][0],brs[q],us[q][1]) for q,h in enumerate(halves)][0]
     @pl.when(i==0)
     def _():
         fr_ref[...]=fin[:8]
         own=jnp.sum(fin[:1]*vec(SW),axis=1,keepdims=True)
         os_ref[...]=jnp.broadcast_to(own,(8,128))
-def post_fwd(length,w,mixed,hid,vec,TR=256,mode="erf"):
+def post_fwd(length,w,mixed,hid,vec,TR=512,mode="erf"):
     R,D=hid.shape;F=4*D
     rb=lambda n: pl.BlockSpec((TR,n),lambda i:(i,0))
     cb=lambda a: pl.BlockSpec(a.shape,lambda i:(0,0))
@@ -344,37 +356,46 @@
         listwise(pos,ncol,d1,[r[0:1,0:1] for r in s_refs],vec_ref,info_ref)
         vg_ref[...]=jnp.zeros_like(vg_ref)
         arrived_down(dw_s,sems)
-    vec=lambda k: vec_ref[k:k+1,:]
-    row=lax.broadcasted_iota(jnp.int32,(TR,D),0)+i*TR
-    gf=og_ref[...].astype(f32)
-    gf=gf+jnp.where(row==0,info_ref[0:1,0:1]*vec(SW),0.0)
-    gf=jnp.where(row<len_ref[0],gf,0.0)
-    def add(k,v): vg_ref[k:k+1,:]+=jnp.sum(v,axis=0,keepdims=True)
-    u2=u2_ref[...].astype(f32); s1=sc_ref[:,0:1]; s2=sc_ref[:,1:2]
-    add(G2,gf*u2); add(S2,gf)
-    gr2=norm_bwd(gf,u2,s2,vec(G2))
-    gb=gr2.astype(bf)
-    here=pl.ds(pl.multiple_of(i*TR,TR),TR)
-    gb_s[here,:]=gb
-    add(DB,gb.astype(f32))
-    @pl.when(i==0)
-    def _():
         arrived(uw_s,sems.at[4])
         arrived(ow_s,sems.at[5])
-    gn=gr2
-    for c in range(F//D):
-        g=dg(gb,dw_s[c*D:(c+1)*D,:],NT)
-        gi=(g*gp_ref[:,c*D:(c+1)*D].astype(f32)).astype(bf)
-        gi_s[here,c*D:(c+1)*D]=gi
-        add(UB+c,gi.astype(f32))
-        gn=gn+dg(gi,uw_s[:,c*D:(c+1)*D],NT)
-    u1=u1_ref[...].astype(f32)
-    add(G1,gn*u1); add(S1,gn)
-    ga=norm_bwd(gn,u1,s1,vec(G1)).astype(bf)
-    ga_ref[...]=ga
-    ga_s[here,:]=ga
-    add(OB,ga.astype(f32))
-    gm_ref[...]=dg(ga,ow_s[...],NT).astype(bf)
+    vec=lambda k: vec_ref[k:k+1,:]
+    def add(k,v): vg_ref[k:k+1,:]+=jnp.sum(v,axis=0,keepdims=True)
+    HR=TR
+    halves=[slice(0,TR)]
+    def one(q,h):
+        row=lax.broadcasted_iota(jnp.int32,(HR,D),0)+i*TR+q*HR
+        gf=og_ref[h,:].astype(f32)
+        gf=gf+jnp.where(row==0,info_ref[0:1,0:1]*vec(SW),0.0)
+        gf=jnp.where(row<len_ref[0],gf,0.0)
+        u2=u2_ref[h,:].astype(f32)
+        add(G2,gf*u2); add(S2,gf)
+        gr2=norm_bwd(gf,u2,sc_ref[h,1:2],vec(G2))
+        gb=gr2.astype(bf)
+        here=pl.ds(pl.multiple_of(i*TR+q*HR,HR),HR)
+        gb_s[here,:]=gb
+        add(DB,gb.astype(f32))
+        return here,gr2,gb
+    def two(h,here,gr2,gb):
+        gn=gr2
+        for c in range(F//D):
+            g=dg(gb,dw_s[c*D:(c+1)*D,:],NT)
+            gi=(g*gp_ref[h,c*D:(c+1)*D].astype(f32)).astype(bf)
+            gi_s[here,c*D:(c+1)*D]=gi
+            add(UB+c,gi.astype(f32))
+            gn=gn+dg(gi,uw_s[:,c*D:(c+1)*D],NT)
+        return gn
+    def three(h,here,gn):
+        u1=u1_ref[h,:].astype(f32)
+        add(G1,gn*u1); add(S1,gn)
+        ga=norm_bwd(gn,u1,sc_ref[h,0:1],vec(G1)).astype(bf)
+        ga_ref[h,:]=ga
+        ga_s[here,:]=ga
+        add(OB,ga.astype(f32))
+        return ga
+    a=[one(q,h) for q,h in enumerate(halves)]
+    gns=[two(h,*v) for h,v in zip(halves,a)]
+    gas=[three(h,v[0],gn) for h,v,gn in zip(halves,a,gns)]
+    for h,ga in zip(halves,gas): gm_ref[h,:]=dg(ga,ow_s[...],NT).astype(bf)
     @pl.when(i==n-1)
     def _():
         for c in whole_copies(): c.wait()
@@ -603,6 +624,12 @@
     layer_out, u1, u2, sc, nl, act, gp, first, own_score = post_fwd(length, w_rest, mixed, tokens, vec)
     scores = [own_score] + [swap_col(own_score, r) for r in range(1, ncol)]
     ga, gm, vg, info, keep, send = mid(pos, length, scores, d1, w_rest, out_grad.reshape(S, D), u2, u1, sc, act, gp, nl, mixed, vec)
+    def home(down, up):
+        down = cat([down[:, j * D : (j + 1) * D] for j in range(4)])
+        return down, up.reshape(d1, 4, n_dev, d1).transpose(0, 2, 1, 3).reshape(d1, F)
+    def own_part(v):
+        part = lax.dynamic_slice_in_dim(v, dev * d1, d1, axis=1)
+        return part, v[31, 0] / info[2, 0], v[CT + 3 : CT + 3 + rel_bias.shape[1], : rel_bias.shape[0]].T
     if fast:
         r0 = swap_core(send)
     back = lambda i, g: attn_bwd(qkv, g, attn[i][2], attn[i][1], attn[i][3], *calls[i])
@@ -627,23 +654,26 @@
     if fast:
         smalls = smalls + afters([travel], kq)[0]
         rq0 = swap_core(afters([sq], smalls)[0])
+        smalls = smalls + flip_z(smalls, 1)
+        travel = flip_z(smalls, 2)
         c3 = collect3(afters(c2, kq, smalls))
+        smalls = smalls + afters([travel], *c3)[0]
+        c3 = afters(c3, smalls)
         cq1 = collect1(kq, afters([rq0], *c3)[0])
         c3 = send3(*c3)
-        parts = afters(parts, cq1[0], cq1[1])
+        parts = afters(parts, cq1[0], cq1[1], smalls)
         hidden_grad = hgrad(pos, p_qkv, parts, ga)
         cq2 = collect2(*afters(cq1, hidden_grad))
-        m, o = collect4(*afters(c3, cq2[0], cq2[1]))
-        travel = flip_z(afters([smalls], m)[0], 1)
-        cq3 = collect3(afters(cq2, m))
+        cq3 = collect3(cq2)
+        m, o = collect4(*afters(c3, *cq3))
+        cq3 = send3(*cq3)
         n = (D + F) // 2
         d_out = sides(m[:, :h], o[:, :h], c)
         d_up = sides(m[:, h:n], o[:, h:n], c)
         d_down = sides(m[:, n:], o[:, n:], c)
-        smalls = smalls + afters([travel], *cq3)[0]
-        travel = flip_z(smalls, 2)
-        m, o = collect4(*send3(*cq3))
-        smalls = smalls + afters([travel], m)[0]
+        d_down, d_up = home(d_down, d_up)
+        little = own_part(smalls)
+        m, o = collect4(*afters(cq3, d_out, d_up, d_down, *little))
         d_qkv = sides(m, o, c)
     else:
         hidden_grad = hgrad(pos, p_qkv, parts, ga)
@@ -653,12 +683,9 @@
         d_out = scatter(natural(keep[:, :, :h], send[:, :, :h]))
         d_up = scatter(natural(keep[:, :, h:n], send[:, :, h:n]))
         d_down = scatter(natural(keep[:, :, n:], send[:, :, n:]))
-        smalls = lax.psum(smalls, ALL)
-    d_down = cat([d_down[:, j * D : (j + 1) * D] for j in range(4)])
-    d_up = d_up.reshape(d1, 4, n_dev, d1).transpose(0, 2, 1, 3).reshape(d1, F)
-    part = lax.dynamic_slice_in_dim(smalls, dev * d1, d1, axis=1)
-    loss = smalls[31, 0] / info[2, 0]
-    bucket = smalls[CT + 3 : CT + 3 + rel_bias.shape[1], : rel_bias.shape[0]].T
+        d_down, d_up = home(d_down, d_up)
+        little = own_part(lax.psum(smalls, ALL))
+    part, loss, bucket = little
     return (layer_out.reshape(hidden.shape), loss, hidden_grad.reshape(hidden.shape), d_qkv, part[CT : CT + 2],
             d_out, part[OB], part[G1], part[S1], d_up, part[UB : UB + 4].reshape(-1), d_down, part[DB], part[G2], part[S2],
             bucket, part[CT + 2])

time: 336 us -> 321 us (0.955)
  waiting for transfers between devices: 66.8 us -> 58.4 us
  starting transfers between devices: 42.8 us -> 37.4 us
    ppermute x9, waiting for transfers between devices: 16.8 us -> 7.91 us  [shift_z(): return lax.ppermute(v, 'pb', [(i, (i + 2 * k) % 8) for i in range(8)])]
    ppermute x2, starting transfers between devices: 6.82 us -> 3.18 us  [flip_z(): return lax.ppermute(v, 'pb', [(i, i ^ 2 * m) for i in range(8)])]
  transfers between devices with their start and end apart: 39 -> 39, of which waited for: 16 -> 16; matrix products, arithmetic and copies ran while one was open for 10% -> 11% of each run, Pallas kernels for 27% -> 28%
where the time goes in v4:
time: 321 us; the launch traced here: 316 us
  Pallas kernels  154 us (48%)
  waiting for transfers between devices  58.4 us (18%)
  starting transfers between devices  37.4 us (12%)
  other arithmetic  23.4 us (7%)
  local copies, waits for them, and re-layouts  21.7 us (7%)
  between operations  19.4 us (6%)
    pallas_call x1, Pallas kernels, mid(): pl.pallas_call(functools.partial(mid_kernel, TR, len(scores), d1, len(mix...  40.4 us
    pallas_call x2, Pallas kernels, attn_bwd(): pl.pallas_call(functools.partial(bwd_kernel, BQ, S, form, scale, kscale),...  32.9 us
    pallas_call x2, Pallas kernels, attn_fwd(): pl.pallas_call(functools.partial(fwd_kernel, BQ, S), cost_estimate=takes(...  28.1 us
    pallas_call x1, Pallas kernels, post_fwd(): pl.pallas_call(functools.partial(post_kernel, TR, mode), cost_estimate=ta...  24.3 us
    all_gather x1, waiting for transfers between devices, shards(): w_rest = lax.all_gather(rest, ALL, axis=0, tiled=True)  18.4 us
    ppermute x9, starting transfers between devices, shift_z(): return lax.ppermute(v, 'pb', [(i, (i + 2 * k) % 8) for i in range(8)])  15.3 us
    convert_element_type x10, other arithmetic, add2(): return (a.astype(f32) + b.astype(f32)).astype(bf)  14.2 us
    ppermute x7, waiting for transfers between devices, swap_x(): return lax.ppermute(v, 'col', [(i, i ^ 2) for i in range(4)])  13.1 us
  transfers between devices with their start and end apart: 39, of which 16 were waited for; matrix products, arithmetic and copies ran while one was open for 11% of the time, Pallas kernels for 28%

profile of v4, /device:TPU:0, one launch (start us, length us, event | category | flops | bytes accessed | tf_op | source)
XLA Modules:
  0.0 315.6 jit_solution(11194245858299097267)
XLA Ops:
  15.6 3.7 %collective-permute-start.3 = (bf16[1,48,1280]{2,1,0:T(8,128)(2,1)S(1)}, bf16[1,48,1280]{2,1,0:T(8,128)(2,1)S(1)}, u32[]{:S(2)}, u32[]{:S(2)}) collective-permute-start(bf16[1,48,1280]{2,1,0:T(8,128)(2,1)S(1)} %maximum_select_fusion.3), channel_id=1, source_target_pairs={{0,16},{4,20},{8,24},{12,28},{16,0},{20,4},{24,8},{28,12},{1,17},{... | collective-permute-start | bytes 368648 | tf_op jit(solution)/shard_map/ppermute | solution.py:521
  22.2 3.8 %collective-permute-done.3 = bf16[1,48,1280]{2,1,0:T(8,128)(2,1)S(1)} collective-permute-done((bf16[1,48,1280]{2,1,0:T(8,128)(2,1)S(1)}, bf16[1,48,1280]{2,1,0:T(8,128)(2,1)S(1)}, u32[]{:S(2)}, u32[]{:S(2)}) %collective-permute-start.3) | collective-permute-done | bytes 122912 | tf_op jit(solution)/shard_map/ppermute | solution.py:521
  28.4 3.1 collective-permute-done.1
  35.8 4.2 %collective-permute-done.2 = bf16[2,48,1280]{2,1,0:T(8,128)(2,1)S(1)} collective-permute-done((bf16[2,48,1280]{2,1,0:T(8,128)(2,1)S(1)}, bf16[2,48,1280]{2,1,0:T(8,128)(2,1)S(1)}, u32[]{:S(2)}, u32[]{:S(2)}) %collective-permute-start.2) | collective-permute-done | bytes 245792 | tf_op jit(solution)/shard_map/ppermute | solution.py:519
  46.2 4.4 %collective-permute-done.7.refs_3_ = bf16[4,48,1280]{2,1,0:T(8,128)(2,1)} collective-permute-done((bf16[4,48,1280]{2,1,0:T(8,128)(2,1)}, bf16[4,48,1280]{2,1,0:T(8,128)(2,1)}, u32[]{:S(2)}, u32[]{:S(2)}) %collective-permute-start.7) | collective-permute-done | bytes 491552 | tf_op jit(solution)/shard_map/ppermute | solution.py:519
  50.7 4.8 %collective-permute-done.6.refs_2_ = bf16[4,48,1280]{2,1,0:T(8,128)(2,1)} collective-permute-done((bf16[4,48,1280]{2,1,0:T(8,128)(2,1)}, bf16[4,48,1280]{2,1,0:T(8,128)(2,1)}, u32[]{:S(2)}, u32[]{:S(2)}) %collective-permute-start.6) | collective-permute-done | bytes 491552 | tf_op jit(solution)/shard_map/ppermute | solution.py:518
  55.7 2.6 select_convert_fusion.kx_ref
  59.5 8.9 %shard_map.314 = (bf16[1024,2304]{1,0:T(8,128)(2,1)}, f32[24,768]{1,0:T(8,128)}) custom-call(s32[6]{0:T(128)} %stack.27.pos, bf16[4,48,1280]{2,1,0:T(8,128)(2,1)} %pad_maximum_fusion.refs_0_, bf16[4,48,1280]{2,1,0:T(8,128)(2,1)} %constant_dynamic-update-slice_fusion.2.refs_1_, bf16[4,48,1280]{2,1,0:T(8,128)(2,1)} %collective-permute-done.6.refs_2_, ...), custom_call_target="tpu_custom_call" | custom-call | flops 10350000128 | bytes 9000000 | tf_op jit(solution)/shard_map/pallas_call | solution.py:231
  68.4 10.3 %shard_map.315 = (bf16[1024,256]{1,0:T(8,128)(2,1)}, f32[1024,256]{1,0:T(8,128)}, f32[1024,256]{1,0:T(8,128)}, bf16[4,1024,1024]{2,1,0:T(8,128)(2,1)}) custom-call(bf16[1024,2304]{1,0:T(8,128)(2,1)} %get-tuple-element.98.q_ref.k_ref.v_ref, bf16[1024,2304]{1,0:T(8,128)(2,1)} %get-tuple-element.98.q_ref.k_ref.v_ref, ...), custom_call_target="tpu_custom_call" | custom-call | flops 11500000256 | bytes 10000000 | tf_op jit(solution)/shard_map/pallas_call | solution.py:75
  78.7 17.8 %shard_map.316 = (bf16[1024,512]{1,0:T(8,128)(2,1)}, f32[1024,512]{1,0:T(8,128)}, f32[1024,512]{1,0:T(8,128)}, bf16[8,1024,1024]{2,1,0:T(8,128)(2,1)}) custom-call(bf16[1024,2304]{1,0:T(8,128)(2,1)} %get-tuple-element.98.q_ref.k_ref.v_ref, bf16[1024,2304]{1,0:T(8,128)(2,1)} %get-tuple-element.98.q_ref.k_ref.v_ref, ...), custom_call_target="tpu_custom_call" | custom-call | flops 23000000512 | bytes 20000000 | tf_op jit(solution)/shard_map/pallas_call | solution.py:75
  96.6 18.4 %all-gather.2.cloned.1.call-done.refs_0_.refs_4_ = bf16[768,6912]{1,0:T(8,128)(2,1)} async-done(((bf16[24,6912]{1,0:T(8,128)(2,1)}), bf16[768,6912]{1,0:T(8,128)(2,1)}) %all-gather.2.cloned.1.call-update) | async-done | bytes 10616848 | tf_op jit(solution)/shard_map/all_gather | solution.py:606
  115.0 24.3 %shard_map.317 = (bf16[1024,768]{1,0:T(8,128)(2,1)}, bf16[1024,768]{1,0:T(8,128)(2,1)}, bf16[1024,768]{1,0:T(8,128)(2,1)}, f32[1024,128]{1,0:T(8,128)}, bf16[102...) custom-call(s32[1]{0:T(128)} %bitcast.67.len_ref, ...), custom_call_target="tpu_custom_call" | custom-call | flops 28750000128 | bytes 25000000 | tf_op jit(solution)/shard_map/pallas_call | solution.py:304
  144.8 40.4 %shard_map.318 = (bf16[1024,768]{1,0:T(8,128)(2,1)}, bf16[1024,768]{1,0:T(8,128)(2,1)}, f32[24,768]{1,0:T(8,128)}, f32[8,128]{1,0:T(8,128)}, bf16[16,48,3456]{2,...) custom-call(s32[6]{0:T(128)} %stack.27.pos, s32[1]{0:T(128)} %bitcast.68.len_ref, f32[8,128]{1,0:T(8,128)} %get-tuple-element.103.refs_0_, ...), custom_call_target="tpu_custom_call" | custom-call | flops 36800000000 | bytes 32000000 | tf_op jit(solution)/shard_map/pallas_call | solution.py:442
  185.4 12.2 %shard_map.319 = (bf16[1024,256]{1,0:T(8,128)(2,1)}, bf16[1024,256]{1,0:T(8,128)(2,1)}, bf16[1024,256]{1,0:T(8,128)(2,1)}, f32[4,8,512]{2,1,0:T(8,128)}, f32[8,256]{1,0:T(8,128)}) custom-call(bf16[1024,2304]{1,0:T(8,128)(2,1)} %get-tuple-element.98.q_ref.k_ref.v_ref, bf16[1024,2304]{1,0:T(8,128)(2,1)} %get-tuple-element.98.q_ref.k_ref.v_ref, ...), custom_call_target="tpu_custom_call" | custom-call | flops 13799999488 | bytes 12000000 | tf_op jit(solution)/shard_map/pallas_call | solution.py:153
  197.6 4.2 %add_convert_fusion = (bf16[4,48,3456]{2,1,0:T(8,128)(2,1)}, bf16[4,48,3456]{2,1,0:T(8,128)(2,1)}, bf16[4,48,3456]{2,1,0:T(8,128)(2,1)S(1)}, bf16[4,48,3456]{2,1,0:T(8,128)(2,1)S(1)}) fusion(bf16[16,48,3456]{2,1,0:T(8,128)(2,1)} %collective-permute-done.15, bf16[16,48,3456]{2,1,0:T(8,128)(2,1)S(1)} %bitcast.71), kind=kLoop, calls=%fused_computation.4 | loop fusion | flops 10616832 | bytes 15925248 | tf_op jit(solution)/shard_map/convert_element_type | solution.py:546
  203.9 20.7 %shard_map.320 = (bf16[1024,512]{1,0:T(8,128)(2,1)}, bf16[1024,512]{1,0:T(8,128)(2,1)}, bf16[1024,512]{1,0:T(8,128)(2,1)}, f32[8,8,512]{2,1,0:T(8,128)}, f32[8,512]{1,0:T(8,128)}) custom-call(bf16[1024,2304]{1,0:T(8,128)(2,1)} %get-tuple-element.98.q_ref.k_ref.v_ref, bf16[1024,2304]{1,0:T(8,128)(2,1)} %get-tuple-element.98.q_ref.k_ref.v_ref, ...), custom_call_target="tpu_custom_call" | custom-call | flops 27599998976 | bytes 24000000 | tf_op jit(solution)/shard_map/pallas_call | solution.py:153
  229.7 4.5 %collective-permute-done.18 = bf16[4,48,3456]{2,1,0:T(8,128)(2,1)} collective-permute-done((bf16[4,48,3456]{2,1,0:T(8,128)(2,1)}, bf16[4,48,3456]{2,1,0:T(8,128)(2,1)}, u32[]{:S(2)}, u32[]{:S(2)}) %collective-permute-start.18) | collective-permute-done | bytes 1327136 | tf_op jit(solution)/shard_map/ppermute | solution.py:518
  234.1 2.7 add_convert_fusion.4
  242.6 8.6 %shard_map.322 = (bf16[16,48,1152]{2,1,0:T(8,128)(2,1)}, bf16[16,48,1152]{2,1,0:T(8,128)(2,1)}) custom-call(s32[6]{0:T(128)} %stack.27.pos, bf16[1024,768]{1,0:T(8,128)(2,1)} %bitcast.79, bf16[1024,256]{1,0:T(8,128)(2,1)} %get-tuple-element.160.refs_0_.refs_8_, bf16[1024,512]{1,0:T(8,128)(2,1)} %get-tuple-element.161.refs_1_.refs_9_, ...), custom_call_target="tpu_custom_call" | custom-call | flops 10350000128 | bytes 9000000 | tf_op jit(solution)/shard_map/pallas_call | solution.py:490
  269.8 2.6 add_convert_fusion.8
  274.5 9.1 %shard_map.323 = bf16[1024,768]{1,0:T(8,128)(2,1)} custom-call(s32[6]{0:T(128)} %stack.27.pos, bf16[4,48,1280]{2,1,0:T(8,128)(2,1)} %pad_maximum_fusion.refs_0_, bf16[4,48,1280]{2,1,0:T(8,128)(2,1)} %constant_dynamic-update-slice_fusion.2.refs_1_, bf16[4,48,1280]{2,1,0:T(8,128)(2,1)} %collective-permute-done.6.refs_2_, ...), custom_call_target="tpu_custom_call" | custom-call | flops 11500000256 | bytes 10000000 | tf_op jit(solution)/shard_map/pallas_call | solution.py:507
  286.0 3.8 %collective-permute-done.30 = bf16[2,48,1152]{2,1,0:T(8,128)(2,1)S(1)} collective-permute-done((bf16[2,48,1152]{2,1,0:T(8,128)(2,1)S(1)}, bf16[2,48,1152]{2,1,0:T(8,128)(2,1)S(1)}, u32[]{:S(2)}, u32[]{:S(2)}) %collective-permute-start.30) | collective-permute-done | bytes 221216 | tf_op jit(solution)/shard_map/ppermute | solution.py:518
  293.3 3.1 collective-permute-start.29
  301.4 2.6 reshape.424
  (207 shorter events, 75.5 us)
Async XLA Ops:
  7.2 107.8 %all-gather.2.cloned.1.call-start = ((), (), s32[]{:S(2)}) async-start(), calls=%async_computation | async-start | bytes 10948608 | tf_op jit(solution)/shard_map/all_gather | solution.py:606
  15.6 10.5 %collective-permute-start.3 = (bf16[1,48,1280]{2,1,0:T(8,128)(2,1)S(1)}, bf16[1,48,1280]{2,1,0:T(8,128)(2,1)S(1)}, u32[]{:S(2)}, u32[]{:S(2)}) collective-permute-start(bf16[1,48,1280]{2,1,0:T(8,128)(2,1)S(1)} %maximum_select_fusion.3), channel_id=1, source_target_pairs={{0,16},{4,20},{8,24},{12,28},{16,0},{20,4},{24,8},{28,12},{1,17},{... | collective-permute-start | bytes 368648 | tf_op jit(solution)/shard_map/ppermute | solution.py:521
  21.2 10.3 %collective-permute-start.1 = (bf16[1,48,1280]{2,1,0:T(8,128)(2,1)S(1)}, bf16[1,48,1280]{2,1,0:T(8,128)(2,1)S(1)}, u32[]{:S(2)}, u32[]{:S(2)}) collective-permute-start(bf16[1,48,1280]{2,1,0:T(8,128)(2,1)S(1)} %maximum_select_fusion.3), channel_id=1, source_target_pairs={{0,8},{4,12},{8,16},{12,20},{16,24},{20,28},{24,0},{28,4},{1,9},{5... | collective-permute-start | bytes 368648 | tf_op jit(solution)/shard_map/ppermute | solution.py:521
  31.5 8.5 %collective-permute-start.2 = (bf16[2,48,1280]{2,1,0:T(8,128)(2,1)S(1)}, bf16[2,48,1280]{2,1,0:T(8,128)(2,1)S(1)}, u32[]{:S(2)}, u32[]{:S(2)}) collective-permute-start(bf16[2,48,1280]{2,1,0:T(8,128)(2,1)S(1)} %pad_maximum_fusion.2), channel_id=1, source_target_pairs={{0,4},{4,0},{8,12},{12,8},{16,20},{20,16},{24,28},{28,24},{1,5},{5... | collective-permute-start | bytes 737288 | tf_op jit(solution)/shard_map/ppermute | solution.py:519
  35.2 15.4 %collective-permute-start.7 = (bf16[4,48,1280]{2,1,0:T(8,128)(2,1)}, bf16[4,48,1280]{2,1,0:T(8,128)(2,1)}, u32[]{:S(2)}, u32[]{:S(2)}) collective-permute-start(bf16[4,48,1280]{2,1,0:T(8,128)(2,1)} %constant_dynamic-update-slice_fusion.2.refs_1_), channel_id=1, source_target_pairs={{0,4},{4,0},{8,12},{12,8},{16,20},{20,16},{24,28},{28,24},{1,5},{5... | collective-permute-start | bytes 1474568 | tf_op jit(solution)/shard_map/ppermute | solution.py:519
  40.9 14.6 %collective-permute-start.6 = (bf16[4,48,1280]{2,1,0:T(8,128)(2,1)}, bf16[4,48,1280]{2,1,0:T(8,128)(2,1)}, u32[]{:S(2)}, u32[]{:S(2)}) collective-permute-start(bf16[4,48,1280]{2,1,0:T(8,128)(2,1)} %pad_maximum_fusion.refs_0_), channel_id=1, source_target_pairs={{0,2},{1,3},{2,0},{3,1},{4,6},{5,7},{6,4},{7,5},{8,10},{9,11},{10,... | collective-permute-start | bytes 1474568 | tf_op jit(solution)/shard_map/ppermute | solution.py:518
  45.7 12.6 %collective-permute-start.9 = (bf16[4,48,1280]{2,1,0:T(8,128)(2,1)}, bf16[4,48,1280]{2,1,0:T(8,128)(2,1)S(1)}, u32[]{:S(2)}, u32[]{:S(2)}) collective-permute-start(bf16[4,48,1280]{2,1,0:T(8,128)(2,1)} %constant_dynamic-update-slice_fusion.2.refs_1_), channel_id=1, source_target_pairs={{0,1},{1,0},{2,3},{3,2},{4,5},{5,4},{6,7},{7,6},{8,9},{9,8},{10,11... | collective-permute-start | bytes 1474568 | tf_op jit(solution)/shard_map/ppermute | solution.py:516
  45.7 12.5 %collective-permute-start.8 = (bf16[4,48,1280]{2,1,0:T(8,128)(2,1)}, bf16[4,48,1280]{2,1,0:T(8,128)(2,1)S(1)}, u32[]{:S(2)}, u32[]{:S(2)}) collective-permute-start(bf16[4,48,1280]{2,1,0:T(8,128)(2,1)} %pad_maximum_fusion.refs_0_), channel_id=1, source_target_pairs={{0,1},{1,0},{2,3},{3,2},{4,5},{5,4},{6,7},{7,6},{8,9},{9,8},{10,11... | collective-permute-start | bytes 1474568 | tf_op jit(solution)/shard_map/ppermute | solution.py:516
  185.2 12.3 %collective-permute-start.15 = (bf16[16,48,3456]{2,1,0:T(8,128)(2,1)}, bf16[16,48,3456]{2,1,0:T(8,128)(2,1)}, u32[]{:S(2)}, u32[]{:S(2)}) collective-permute-start(bf16[16,48,3456]{2,1,0:T(8,128)(2,1)} %get-tuple-element.119), channel_id=1, source_target_pairs={{0,1},{1,0},{2,3},{3,2},{4,5},{5,4},{6,7},{7,6},{8,9},{9,8},{10,11... | collective-permute-start | bytes 15925256 | tf_op jit(solution)/shard_map/ppermute | solution.py:516
  201.9 32.2 %collective-permute-start.18 = (bf16[4,48,3456]{2,1,0:T(8,128)(2,1)}, bf16[4,48,3456]{2,1,0:T(8,128)(2,1)}, u32[]{:S(2)}, u32[]{:S(2)}) collective-permute-start(bf16[4,48,3456]{2,1,0:T(8,128)(2,1)} %get-tuple-element.182), channel_id=1, source_target_pairs={{0,2},{1,3},{2,0},{3,1},{4,6},{5,7},{6,4},{7,5},{8,10},{9,11},{10,... | collective-permute-start | bytes 3981320 | tf_op jit(solution)/shard_map/ppermute | solution.py:518
  202.5 31.6 %collective-permute-start.19 = (bf16[4,48,3456]{2,1,0:T(8,128)(2,1)}, bf16[4,48,3456]{2,1,0:T(8,128)(2,1)}, u32[]{:S(2)}, u32[]{:S(2)}) collective-permute-start(bf16[4,48,3456]{2,1,0:T(8,128)(2,1)} %get-tuple-element.181), channel_id=1, source_target_pairs={{0,4},{4,0},{8,12},{12,8},{16,20},{20,16},{24,28},{28,24},{1,5},{5... | collective-permute-start | bytes 3981320 | tf_op jit(solution)/shard_map/ppermute | solution.py:519
  229.0 10.2 %collective-permute-start.17 = (f32[32,768]{1,0:T(8,128)S(1)}, f32[32,768]{1,0:T(8,128)S(1)}, u32[]{:S(2)}, u32[]{:S(2)}) collective-permute-start(f32[32,768]{1,0:T(8,128)S(1)} %add.288), channel_id=1, source_target_pairs={{0,2},{1,3},{2,0},{3,1},{4,6},{5,7},{6,4},{7,5},{8,10},{9,11},{10,... | collective-permute-start | bytes 294920 | tf_op jit(solution)/shard_map/ppermute | solution.py:518
  239.2 12.0 %collective-permute-start.20 = (f32[32,768]{1,0:T(8,128)S(1)}, f32[32,768]{1,0:T(8,128)S(1)}, u32[]{:S(2)}, u32[]{:S(2)}) collective-permute-start(f32[32,768]{1,0:T(8,128)S(1)} %add.293), channel_id=1, source_target_pairs={{0,4},{4,0},{8,12},{12,8},{16,20},{20,16},{24,28},{28,24},{1,5},{5... | collective-permute-start | bytes 294920 | tf_op jit(solution)/shard_map/ppermute | solution.py:519
  240.6 17.2 %collective-permute-start.24 = (bf16[2,48,3456]{2,1,0:T(8,128)(2,1)}, bf16[2,48,3456]{2,1,0:T(8,128)(2,1)S(1)}, u32[]{:S(2)}, u32[]{:S(2)}) collective-permute-start(bf16[2,48,3456]{2,1,0:T(8,128)(2,1)} %get-tuple-element.189), channel_id=1, source_target_pairs={{0,2},{1,3},{2,0},{3,1},{4,6},{5,7},{6,4},{7,5},{8,10},{9,11},{10,... | collective-permute-start | bytes 1990664 | tf_op jit(solution)/shard_map/ppermute | solution.py:518
  241.4 17.2 %collective-permute-start.23 = (bf16[2,48,3456]{2,1,0:T(8,128)(2,1)}, bf16[2,48,3456]{2,1,0:T(8,128)(2,1)S(1)}, u32[]{:S(2)}, u32[]{:S(2)}) collective-permute-start(bf16[2,48,3456]{2,1,0:T(8,128)(2,1)} %get-tuple-element.191), channel_id=1, source_target_pairs={{0,4},{4,0},{8,12},{12,8},{16,20},{20,16},{24,28},{28,24},{1,5},{5... | collective-permute-start | bytes 1990664 | tf_op jit(solution)/shard_map/ppermute | solution.py:519
  253.7 16.1 %collective-permute-start.25 = (bf16[16,48,1152]{2,1,0:T(8,128)(2,1)}, bf16[16,48,1152]{2,1,0:T(8,128)(2,1)}, u32[]{:S(2)}, u32[]{:S(2)}) collective-permute-start(bf16[16,48,1152]{2,1,0:T(8,128)(2,1)} %get-tuple-element.154), channel_id=1, source_target_pairs={{0,1},{1,0},{2,3},{3,2},{4,5},{5,4},{6,7},{7,6},{8,9},{9,8},{10,11... | collective-permute-start | bytes 5308424 | tf_op jit(solution)/shard_map/ppermute | solution.py:516
  263.1 30.2 %collective-permute-start.33 = (bf16[48,3456]{1,0:T(8,128)(2,1)}, bf16[48,3456]{1,0:T(8,128)(2,1)}, u32[]{:S(2)}, u32[]{:S(2)}) collective-permute-start(bf16[48,3456]{1,0:T(8,128)(2,1)} %get-tuple-element.156), channel_id=1, source_target_pairs={{0,24},{4,28},{8,0},{12,4},{16,8},{20,12},{24,16},{28,20},{1,25},{... | collective-permute-start | bytes 995336 | tf_op jit(solution)/shard_map/ppermute | solution.py:521
  264.8 31.6 %collective-permute-start.34 = (bf16[48,3456]{1,0:T(8,128)(2,1)}, bf16[48,3456]{1,0:T(8,128)(2,1)}, u32[]{:S(2)}, u32[]{:S(2)}) collective-permute-start(bf16[48,3456]{1,0:T(8,128)(2,1)} %get-tuple-element.157), channel_id=1, source_target_pairs={{0,16},{4,20},{8,24},{12,28},{16,0},{20,4},{24,8},{28,12},{1,17},{... | collective-permute-start | bytes 995336 | tf_op jit(solution)/shard_map/ppermute | solution.py:521
  264.8 31.6 %collective-permute-start.35 = (bf16[48,3456]{1,0:T(8,128)(2,1)}, bf16[48,3456]{1,0:T(8,128)(2,1)}, u32[]{:S(2)}, u32[]{:S(2)}) collective-permute-start(bf16[48,3456]{1,0:T(8,128)(2,1)} %get-tuple-element.158), channel_id=1, source_target_pairs={{0,8},{4,12},{8,16},{12,20},{16,24},{20,28},{24,0},{28,4},{1,9},{5... | collective-permute-start | bytes 995336 | tf_op jit(solution)/shard_map/ppermute | solution.py:521
  272.4 11.2 %collective-permute-start.26 = (bf16[4,48,1152]{2,1,0:T(8,128)(2,1)}, bf16[4,48,1152]{2,1,0:T(8,128)(2,1)S(1)}, u32[]{:S(2)}, u32[]{:S(2)}) collective-permute-start(bf16[4,48,1152]{2,1,0:T(8,128)(2,1)} %get-tuple-element.186), channel_id=1, source_target_pairs={{0,2},{1,3},{2,0},{3,1},{4,6},{5,7},{6,4},{7,5},{8,10},{9,11},{10,... | collective-permute-start | bytes 1327112 | tf_op jit(solution)/shard_map/ppermute | solution.py:518
  273.2 10.5 %collective-permute-start.27 = (bf16[4,48,1152]{2,1,0:T(8,128)(2,1)S(1)}, bf16[4,48,1152]{2,1,0:T(8,128)(2,1)S(1)}, u32[]{:S(2)}, u32[]{:S(2)}) collective-permute-start(bf16[4,48,1152]{2,1,0:T(8,128)(2,1)S(1)} %get-tuple-element.185), channel_id=1, source_target_pairs={{0,4},{4,0},{8,12},{12,8},{16,20},{20,16},{24,28},{28,24},{1,5},{5... | collective-permute-start | bytes 1327112 | tf_op jit(solution)/shard_map/ppermute | solution.py:519
  289.8 15.5 %collective-permute-start.31 = (bf16[48,1152]{1,0:T(8,128)(2,1)S(1)}, bf16[48,1152]{1,0:T(8,128)(2,1)S(1)}, u32[]{:S(2)}, u32[]{:S(2)}) collective-permute-start(bf16[48,1152]{1,0:T(8,128)(2,1)S(1)} %get-tuple-element.204), channel_id=1, source_target_pairs={{0,16},{4,20},{8,24},{12,28},{16,0},{20,4},{24,8},{28,12},{1,17},{... | collective-permute-start | bytes 331784 | tf_op jit(solution)/shard_map/ppermute | solution.py:521
  292.0 13.3 %collective-permute-start.32 = (bf16[48,1152]{1,0:T(8,128)(2,1)S(1)}, bf16[48,1152]{1,0:T(8,128)(2,1)S(1)}, u32[]{:S(2)}, u32[]{:S(2)}) collective-permute-start(bf16[48,1152]{1,0:T(8,128)(2,1)S(1)} %get-tuple-element.203), channel_id=1, source_target_pairs={{0,8},{4,12},{8,16},{12,20},{16,24},{20,28},{24,0},{28,4},{1,9},{5... | collective-permute-start | bytes 331784 | tf_op jit(solution)/shard_map/ppermute | solution.py:521
  293.3 12.0 %collective-permute-start.29 = (bf16[48,1152]{1,0:T(8,128)(2,1)S(1)}, bf16[48,1152]{1,0:T(8,128)(2,1)S(1)}, u32[]{:S(2)}, u32[]{:S(2)}) collective-permute-start(bf16[48,1152]{1,0:T(8,128)(2,1)S(1)} %get-tuple-element.205), channel_id=1, source_target_pairs={{0,24},{4,28},{8,0},{12,4},{16,8},{20,12},{24,16},{28,20},{1,25},{... | collective-permute-start | bytes 331784 | tf_op jit(solution)/shard_map/ppermute | solution.py:521
  (42 other events, 169.0 us)
Sparse Core Ops, SparseCore 0:
  11.9 102.9 all-gather.1

commit v5 on v4

--- a/solution.py
+++ b/solution.py
@@ -254,8 +254,6 @@
         fetch(w,D,uw_ref,sems.at[5])
         fetch_down(w,D+F,dw_ref,sems)
         arrived(ow_ref,sems.at[4])
-        arrived(uw_ref,sems.at[5])
-        arrived_down(dw_ref,sems)
     vec=lambda n: vec_ref[n:n+1,:]
     HR=TR//SUB
     halves=[slice(q*HR,(q+1)*HR) for q in range(SUB)]
@@ -290,6 +288,10 @@
         return fin
     us=[one(h) for h in halves]
     ns=[two(h,u[0]) for h,u in zip(halves,us)]
+    @pl.when(i==0)
+    def _():
+        arrived(uw_ref,sems.at[5])
+        arrived_down(dw_ref,sems)
     brs=[three(h,n[1]) for h,n in zip(halves,ns)]
     fin=[four(q,h,ns[q][0],brs[q],us[q][1]) for q,h in enumerate(halves)][0]
     @pl.when(i==0)
@@ -352,12 +354,12 @@
         fetch_down(w,D+F,dw_s,sems)
         fetch(w,D,uw_s,sems.at[4])
         fetch(w,0,ow_s,sems.at[5])
-        for c in whole_copies(): c.start()
         listwise(pos,ncol,d1,[r[0:1,0:1] for r in s_refs],vec_ref,info_ref)
         vg_ref[...]=jnp.zeros_like(vg_ref)
         arrived_down(dw_s,sems)
-        arrived(uw_s,sems.at[4])
-        arrived(ow_s,sems.at[5])
+    @pl.when(i==1)
+    def _():
+        for c in whole_copies(): c.start()
     vec=lambda k: vec_ref[k:k+1,:]
     def add(k,v): vg_ref[k:k+1,:]+=jnp.sum(v,axis=0,keepdims=True)
     HR=TR
@@ -393,6 +395,10 @@
         add(OB,ga.astype(f32))
         return ga
     a=[one(q,h) for q,h in enumerate(halves)]
+    @pl.when(i==0)
+    def _():
+        arrived(uw_s,sems.at[4])
+        arrived(ow_s,sems.at[5])
     gns=[two(h,*v) for h,v in zip(halves,a)]
     gas=[three(h,v[0],gn) for h,v,gn in zip(halves,a,gns)]
     for h,ga in zip(halves,gas): gm_ref[h,:]=dg(ga,ow_s[...],NT).astype(bf)

time: 321 us -> 321 us (level)
  no operation moved by 1% of the time
where the time goes in v5:
time: 321 us; the launch traced here: 315 us
  Pallas kernels  154 us (48%)
  waiting for transfers between devices  58.4 us (18%)
  starting transfers between devices  37.4 us (12%)
  other arithmetic  23.4 us (7%)
  local copies, waits for them, and re-layouts  21.7 us (7%)
  between operations  19.4 us (6%)
    pallas_call x1, Pallas kernels, mid(): pl.pallas_call(functools.partial(mid_kernel, TR, len(scores), d1, len(mix...  40.3 us
    pallas_call x2, Pallas kernels, attn_bwd(): pl.pallas_call(functools.partial(bwd_kernel, BQ, S, form, scale, kscale),...  32.9 us
    pallas_call x2, Pallas kernels, attn_fwd(): pl.pallas_call(functools.partial(fwd_kernel, BQ, S), cost_estimate=takes(...  28.1 us
    pallas_call x1, Pallas kernels, post_fwd(): pl.pallas_call(functools.partial(post_kernel, TR, mode), cost_estimate=ta...  24 us
    all_gather x1, waiting for transfers between devices, shards(): w_rest = lax.all_gather(rest, ALL, axis=0, tiled=True)  18.4 us
    ppermute x9, starting transfers between devices, shift_z(): return lax.ppermute(v, 'pb', [(i, (i + 2 * k) % 8) for i in range(8)])  15.4 us
    convert_element_type x10, other arithmetic, add2(): return (a.astype(f32) + b.astype(f32)).astype(bf)  14.2 us
    ppermute x7, waiting for transfers between devices, swap_x(): return lax.ppermute(v, 'col', [(i, i ^ 2) for i in range(4)])  13.1 us
  transfers between devices with their start and end apart: 39, of which 16 were waited for; matrix products, arithmetic and copies ran while one was open for 11% of the time, Pallas kernels for 28%

profile of v5, /device:TPU:0, one launch (start us, length us, event | category | flops | bytes accessed | tf_op | source)
XLA Modules:
  0.0 315.2 jit_solution(5806622508685474477)
XLA Ops:
  15.6 3.7 %collective-permute-start.3 = (bf16[1,48,1280]{2,1,0:T(8,128)(2,1)S(1)}, bf16[1,48,1280]{2,1,0:T(8,128)(2,1)S(1)}, u32[]{:S(2)}, u32[]{:S(2)}) collective-permute-start(bf16[1,48,1280]{2,1,0:T(8,128)(2,1)S(1)} %maximum_select_fusion.3), channel_id=1, source_target_pairs={{0,16},{4,20},{8,24},{12,28},{16,0},{20,4},{24,8},{28,12},{1,17},{... | collective-permute-start | bytes 368648 | tf_op jit(solution)/shard_map/ppermute | solution.py:527
  22.2 3.8 %collective-permute-done.3 = bf16[1,48,1280]{2,1,0:T(8,128)(2,1)S(1)} collective-permute-done((bf16[1,48,1280]{2,1,0:T(8,128)(2,1)S(1)}, bf16[1,48,1280]{2,1,0:T(8,128)(2,1)S(1)}, u32[]{:S(2)}, u32[]{:S(2)}) %collective-permute-start.3) | collective-permute-done | bytes 122912 | tf_op jit(solution)/shard_map/ppermute | solution.py:527
  28.4 3.1 collective-permute-done.1
  35.8 4.2 %collective-permute-done.2 = bf16[2,48,1280]{2,1,0:T(8,128)(2,1)S(1)} collective-permute-done((bf16[2,48,1280]{2,1,0:T(8,128)(2,1)S(1)}, bf16[2,48,1280]{2,1,0:T(8,128)(2,1)S(1)}, u32[]{:S(2)}, u32[]{:S(2)}) %collective-permute-start.2) | collective-permute-done | bytes 245792 | tf_op jit(solution)/shard_map/ppermute | solution.py:525
  46.2 4.4 %collective-permute-done.7.refs_3_ = bf16[4,48,1280]{2,1,0:T(8,128)(2,1)} collective-permute-done((bf16[4,48,1280]{2,1,0:T(8,128)(2,1)}, bf16[4,48,1280]{2,1,0:T(8,128)(2,1)}, u32[]{:S(2)}, u32[]{:S(2)}) %collective-permute-start.7) | collective-permute-done | bytes 491552 | tf_op jit(solution)/shard_map/ppermute | solution.py:525
  50.7 4.8 %collective-permute-done.6.refs_2_ = bf16[4,48,1280]{2,1,0:T(8,128)(2,1)} collective-permute-done((bf16[4,48,1280]{2,1,0:T(8,128)(2,1)}, bf16[4,48,1280]{2,1,0:T(8,128)(2,1)}, u32[]{:S(2)}, u32[]{:S(2)}) %collective-permute-start.6) | collective-permute-done | bytes 491552 | tf_op jit(solution)/shard_map/ppermute | solution.py:524
  55.7 2.6 select_convert_fusion.kx_ref
  59.5 8.9 %shard_map.314 = (bf16[1024,2304]{1,0:T(8,128)(2,1)}, f32[24,768]{1,0:T(8,128)}) custom-call(s32[6]{0:T(128)} %stack.27.pos, bf16[4,48,1280]{2,1,0:T(8,128)(2,1)} %pad_maximum_fusion.refs_0_, bf16[4,48,1280]{2,1,0:T(8,128)(2,1)} %constant_dynamic-update-slice_fusion.2.refs_1_, bf16[4,48,1280]{2,1,0:T(8,128)(2,1)} %collective-permute-done.6.refs_2_, ...), custom_call_target="tpu_custom_call" | custom-call | flops 10350000128 | bytes 9000000 | tf_op jit(solution)/shard_map/pallas_call | solution.py:231
  68.4 10.3 %shard_map.315 = (bf16[1024,256]{1,0:T(8,128)(2,1)}, f32[1024,256]{1,0:T(8,128)}, f32[1024,256]{1,0:T(8,128)}, bf16[4,1024,1024]{2,1,0:T(8,128)(2,1)}) custom-call(bf16[1024,2304]{1,0:T(8,128)(2,1)} %get-tuple-element.98.q_ref.k_ref.v_ref, bf16[1024,2304]{1,0:T(8,128)(2,1)} %get-tuple-element.98.q_ref.k_ref.v_ref, ...), custom_call_target="tpu_custom_call" | custom-call | flops 11500000256 | bytes 10000000 | tf_op jit(solution)/shard_map/pallas_call | solution.py:75
  78.7 17.8 %shard_map.316 = (bf16[1024,512]{1,0:T(8,128)(2,1)}, f32[1024,512]{1,0:T(8,128)}, f32[1024,512]{1,0:T(8,128)}, bf16[8,1024,1024]{2,1,0:T(8,128)(2,1)}) custom-call(bf16[1024,2304]{1,0:T(8,128)(2,1)} %get-tuple-element.98.q_ref.k_ref.v_ref, bf16[1024,2304]{1,0:T(8,128)(2,1)} %get-tuple-element.98.q_ref.k_ref.v_ref, ...), custom_call_target="tpu_custom_call" | custom-call | flops 23000000512 | bytes 20000000 | tf_op jit(solution)/shard_map/pallas_call | solution.py:75
  96.6 18.4 %all-gather.2.cloned.1.call-done.refs_0_.refs_4_ = bf16[768,6912]{1,0:T(8,128)(2,1)} async-done(((bf16[24,6912]{1,0:T(8,128)(2,1)}), bf16[768,6912]{1,0:T(8,128)(2,1)}) %all-gather.2.cloned.1.call-update) | async-done | bytes 10616848 | tf_op jit(solution)/shard_map/all_gather | solution.py:612
  115.0 24.0 %shard_map.317 = (bf16[1024,768]{1,0:T(8,128)(2,1)}, bf16[1024,768]{1,0:T(8,128)(2,1)}, bf16[1024,768]{1,0:T(8,128)(2,1)}, f32[1024,128]{1,0:T(8,128)}, bf16[102...) custom-call(s32[1]{0:T(128)} %bitcast.67.len_ref, ...), custom_call_target="tpu_custom_call" | custom-call | flops 28750000128 | bytes 25000000 | tf_op jit(solution)/shard_map/pallas_call | solution.py:306
  144.6 40.3 %shard_map.318 = (bf16[1024,768]{1,0:T(8,128)(2,1)}, bf16[1024,768]{1,0:T(8,128)(2,1)}, f32[24,768]{1,0:T(8,128)}, f32[8,128]{1,0:T(8,128)}, bf16[16,48,3456]{2,...) custom-call(s32[6]{0:T(128)} %stack.27.pos, s32[1]{0:T(128)} %bitcast.68.len_ref, f32[8,128]{1,0:T(8,128)} %get-tuple-element.103.refs_0_, ...), custom_call_target="tpu_custom_call" | custom-call | flops 36800000000 | bytes 32000000 | tf_op jit(solution)/shard_map/pallas_call | solution.py:448
  185.1 12.2 %shard_map.319 = (bf16[1024,256]{1,0:T(8,128)(2,1)}, bf16[1024,256]{1,0:T(8,128)(2,1)}, bf16[1024,256]{1,0:T(8,128)(2,1)}, f32[4,8,512]{2,1,0:T(8,128)}, f32[8,256]{1,0:T(8,128)}) custom-call(bf16[1024,2304]{1,0:T(8,128)(2,1)} %get-tuple-element.98.q_ref.k_ref.v_ref, bf16[1024,2304]{1,0:T(8,128)(2,1)} %get-tuple-element.98.q_ref.k_ref.v_ref, ...), custom_call_target="tpu_custom_call" | custom-call | flops 13799999488 | bytes 12000000 | tf_op jit(solution)/shard_map/pallas_call | solution.py:153
  197.3 4.2 %add_convert_fusion = (bf16[4,48,3456]{2,1,0:T(8,128)(2,1)}, bf16[4,48,3456]{2,1,0:T(8,128)(2,1)}, bf16[4,48,3456]{2,1,0:T(8,128)(2,1)S(1)}, bf16[4,48,3456]{2,1,0:T(8,128)(2,1)S(1)}) fusion(bf16[16,48,3456]{2,1,0:T(8,128)(2,1)} %collective-permute-done.15, bf16[16,48,3456]{2,1,0:T(8,128)(2,1)S(1)} %bitcast.71), kind=kLoop, calls=%fused_computation.4 | loop fusion | flops 10616832 | bytes 15925248 | tf_op jit(solution)/shard_map/convert_element_type | solution.py:552
  203.6 20.7 %shard_map.320 = (bf16[1024,512]{1,0:T(8,128)(2,1)}, bf16[1024,512]{1,0:T(8,128)(2,1)}, bf16[1024,512]{1,0:T(8,128)(2,1)}, f32[8,8,512]{2,1,0:T(8,128)}, f32[8,512]{1,0:T(8,128)}) custom-call(bf16[1024,2304]{1,0:T(8,128)(2,1)} %get-tuple-element.98.q_ref.k_ref.v_ref, bf16[1024,2304]{1,0:T(8,128)(2,1)} %get-tuple-element.98.q_ref.k_ref.v_ref, ...), custom_call_target="tpu_custom_call" | custom-call | flops 27599998976 | bytes 24000000 | tf_op jit(solution)/shard_map/pallas_call | solution.py:153
  229.3 4.5 %collective-permute-done.18 = bf16[4,48,3456]{2,1,0:T(8,128)(2,1)} collective-permute-done((bf16[4,48,3456]{2,1,0:T(8,128)(2,1)}, bf16[4,48,3456]{2,1,0:T(8,128)(2,1)}, u32[]{:S(2)}, u32[]{:S(2)}) %collective-permute-start.18) | collective-permute-done | bytes 1327136 | tf_op jit(solution)/shard_map/ppermute | solution.py:524
  233.8 2.7 add_convert_fusion.4
  242.2 8.6 %shard_map.322 = (bf16[16,48,1152]{2,1,0:T(8,128)(2,1)}, bf16[16,48,1152]{2,1,0:T(8,128)(2,1)}) custom-call(s32[6]{0:T(128)} %stack.27.pos, bf16[1024,768]{1,0:T(8,128)(2,1)} %bitcast.79, bf16[1024,256]{1,0:T(8,128)(2,1)} %get-tuple-element.160.refs_0_.refs_8_, bf16[1024,512]{1,0:T(8,128)(2,1)} %get-tuple-element.161.refs_1_.refs_9_, ...), custom_call_target="tpu_custom_call" | custom-call | flops 10350000128 | bytes 9000000 | tf_op jit(solution)/shard_map/pallas_call | solution.py:496
  269.4 2.6 add_convert_fusion.8
  274.1 9.1 %shard_map.323 = bf16[1024,768]{1,0:T(8,128)(2,1)} custom-call(s32[6]{0:T(128)} %stack.27.pos, bf16[4,48,1280]{2,1,0:T(8,128)(2,1)} %pad_maximum_fusion.refs_0_, bf16[4,48,1280]{2,1,0:T(8,128)(2,1)} %constant_dynamic-update-slice_fusion.2.refs_1_, bf16[4,48,1280]{2,1,0:T(8,128)(2,1)} %collective-permute-done.6.refs_2_, ...), custom_call_target="tpu_custom_call" | custom-call | flops 11500000256 | bytes 10000000 | tf_op jit(solution)/shard_map/pallas_call | solution.py:513
  285.6 3.8 %collective-permute-done.30 = bf16[2,48,1152]{2,1,0:T(8,128)(2,1)S(1)} collective-permute-done((bf16[2,48,1152]{2,1,0:T(8,128)(2,1)S(1)}, bf16[2,48,1152]{2,1,0:T(8,128)(2,1)S(1)}, u32[]{:S(2)}, u32[]{:S(2)}) %collective-permute-start.30) | collective-permute-done | bytes 221216 | tf_op jit(solution)/shard_map/ppermute | solution.py:524
  292.9 3.1 collective-permute-start.29
  301.0 2.6 reshape.424
  (207 shorter events, 75.5 us)
Async XLA Ops:
  7.2 107.8 %all-gather.2.cloned.1.call-start = ((), (), s32[]{:S(2)}) async-start(), calls=%async_computation | async-start | bytes 10948608 | tf_op jit(solution)/shard_map/all_gather | solution.py:612
  15.6 10.5 %collective-permute-start.3 = (bf16[1,48,1280]{2,1,0:T(8,128)(2,1)S(1)}, bf16[1,48,1280]{2,1,0:T(8,128)(2,1)S(1)}, u32[]{:S(2)}, u32[]{:S(2)}) collective-permute-start(bf16[1,48,1280]{2,1,0:T(8,128)(2,1)S(1)} %maximum_select_fusion.3), channel_id=1, source_target_pairs={{0,16},{4,20},{8,24},{12,28},{16,0},{20,4},{24,8},{28,12},{1,17},{... | collective-permute-start | bytes 368648 | tf_op jit(solution)/shard_map/ppermute | solution.py:527
  21.2 10.3 %collective-permute-start.1 = (bf16[1,48,1280]{2,1,0:T(8,128)(2,1)S(1)}, bf16[1,48,1280]{2,1,0:T(8,128)(2,1)S(1)}, u32[]{:S(2)}, u32[]{:S(2)}) collective-permute-start(bf16[1,48,1280]{2,1,0:T(8,128)(2,1)S(1)} %maximum_select_fusion.3), channel_id=1, source_target_pairs={{0,8},{4,12},{8,16},{12,20},{16,24},{20,28},{24,0},{28,4},{1,9},{5... | collective-permute-start | bytes 368648 | tf_op jit(solution)/shard_map/ppermute | solution.py:527
  31.5 8.5 %collective-permute-start.2 = (bf16[2,48,1280]{2,1,0:T(8,128)(2,1)S(1)}, bf16[2,48,1280]{2,1,0:T(8,128)(2,1)S(1)}, u32[]{:S(2)}, u32[]{:S(2)}) collective-permute-start(bf16[2,48,1280]{2,1,0:T(8,128)(2,1)S(1)} %pad_maximum_fusion.2), channel_id=1, source_target_pairs={{0,4},{4,0},{8,12},{12,8},{16,20},{20,16},{24,28},{28,24},{1,5},{5... | collective-permute-start | bytes 737288 | tf_op jit(solution)/shard_map/ppermute | solution.py:525
  35.2 15.4 %collective-permute-start.7 = (bf16[4,48,1280]{2,1,0:T(8,128)(2,1)}, bf16[4,48,1280]{2,1,0:T(8,128)(2,1)}, u32[]{:S(2)}, u32[]{:S(2)}) collective-permute-start(bf16[4,48,1280]{2,1,0:T(8,128)(2,1)} %constant_dynamic-update-slice_fusion.2.refs_1_), channel_id=1, source_target_pairs={{0,4},{4,0},{8,12},{12,8},{16,20},{20,16},{24,28},{28,24},{1,5},{5... | collective-permute-start | bytes 1474568 | tf_op jit(solution)/shard_map/ppermute | solution.py:525
  40.9 14.6 %collective-permute-start.6 = (bf16[4,48,1280]{2,1,0:T(8,128)(2,1)}, bf16[4,48,1280]{2,1,0:T(8,128)(2,1)}, u32[]{:S(2)}, u32[]{:S(2)}) collective-permute-start(bf16[4,48,1280]{2,1,0:T(8,128)(2,1)} %pad_maximum_fusion.refs_0_), channel_id=1, source_target_pairs={{0,2},{1,3},{2,0},{3,1},{4,6},{5,7},{6,4},{7,5},{8,10},{9,11},{10,... | collective-permute-start | bytes 1474568 | tf_op jit(solution)/shard_map/ppermute | solution.py:524
  45.7 12.6 %collective-permute-start.9 = (bf16[4,48,1280]{2,1,0:T(8,128)(2,1)}, bf16[4,48,1280]{2,1,0:T(8,128)(2,1)S(1)}, u32[]{:S(2)}, u32[]{:S(2)}) collective-permute-start(bf16[4,48,1280]{2,1,0:T(8,128)(2,1)} %constant_dynamic-update-slice_fusion.2.refs_1_), channel_id=1, source_target_pairs={{0,1},{1,0},{2,3},{3,2},{4,5},{5,4},{6,7},{7,6},{8,9},{9,8},{10,11... | collective-permute-start | bytes 1474568 | tf_op jit(solution)/shard_map/ppermute | solution.py:522
  45.7 12.5 %collective-permute-start.8 = (bf16[4,48,1280]{2,1,0:T(8,128)(2,1)}, bf16[4,48,1280]{2,1,0:T(8,128)(2,1)S(1)}, u32[]{:S(2)}, u32[]{:S(2)}) collective-permute-start(bf16[4,48,1280]{2,1,0:T(8,128)(2,1)} %pad_maximum_fusion.refs_0_), channel_id=1, source_target_pairs={{0,1},{1,0},{2,3},{3,2},{4,5},{5,4},{6,7},{7,6},{8,9},{9,8},{10,11... | collective-permute-start | bytes 1474568 | tf_op jit(solution)/shard_map/ppermute | solution.py:522
  184.9 12.4 %collective-permute-start.15 = (bf16[16,48,3456]{2,1,0:T(8,128)(2,1)}, bf16[16,48,3456]{2,1,0:T(8,128)(2,1)}, u32[]{:S(2)}, u32[]{:S(2)}) collective-permute-start(bf16[16,48,3456]{2,1,0:T(8,128)(2,1)} %get-tuple-element.119), channel_id=1, source_target_pairs={{0,1},{1,0},{2,3},{3,2},{4,5},{5,4},{6,7},{7,6},{8,9},{9,8},{10,11... | collective-permute-start | bytes 15925256 | tf_op jit(solution)/shard_map/ppermute | solution.py:522
  201.5 32.3 %collective-permute-start.18 = (bf16[4,48,3456]{2,1,0:T(8,128)(2,1)}, bf16[4,48,3456]{2,1,0:T(8,128)(2,1)}, u32[]{:S(2)}, u32[]{:S(2)}) collective-permute-start(bf16[4,48,3456]{2,1,0:T(8,128)(2,1)} %get-tuple-element.182), channel_id=1, source_target_pairs={{0,2},{1,3},{2,0},{3,1},{4,6},{5,7},{6,4},{7,5},{8,10},{9,11},{10,... | collective-permute-start | bytes 3981320 | tf_op jit(solution)/shard_map/ppermute | solution.py:524
  202.1 31.7 %collective-permute-start.19 = (bf16[4,48,3456]{2,1,0:T(8,128)(2,1)}, bf16[4,48,3456]{2,1,0:T(8,128)(2,1)}, u32[]{:S(2)}, u32[]{:S(2)}) collective-permute-start(bf16[4,48,3456]{2,1,0:T(8,128)(2,1)} %get-tuple-element.181), channel_id=1, source_target_pairs={{0,4},{4,0},{8,12},{12,8},{16,20},{20,16},{24,28},{28,24},{1,5},{5... | collective-permute-start | bytes 3981320 | tf_op jit(solution)/shard_map/ppermute | solution.py:525
  228.7 10.2 %collective-permute-start.17 = (f32[32,768]{1,0:T(8,128)S(1)}, f32[32,768]{1,0:T(8,128)S(1)}, u32[]{:S(2)}, u32[]{:S(2)}) collective-permute-start(f32[32,768]{1,0:T(8,128)S(1)} %add.288), channel_id=1, source_target_pairs={{0,2},{1,3},{2,0},{3,1},{4,6},{5,7},{6,4},{7,5},{8,10},{9,11},{10,... | collective-permute-start | bytes 294920 | tf_op jit(solution)/shard_map/ppermute | solution.py:524
  238.9 11.9 %collective-permute-start.20 = (f32[32,768]{1,0:T(8,128)S(1)}, f32[32,768]{1,0:T(8,128)S(1)}, u32[]{:S(2)}, u32[]{:S(2)}) collective-permute-start(f32[32,768]{1,0:T(8,128)S(1)} %add.293), channel_id=1, source_target_pairs={{0,4},{4,0},{8,12},{12,8},{16,20},{20,16},{24,28},{28,24},{1,5},{5... | collective-permute-start | bytes 294920 | tf_op jit(solution)/shard_map/ppermute | solution.py:525
  240.2 17.2 %collective-permute-start.24 = (bf16[2,48,3456]{2,1,0:T(8,128)(2,1)}, bf16[2,48,3456]{2,1,0:T(8,128)(2,1)S(1)}, u32[]{:S(2)}, u32[]{:S(2)}) collective-permute-start(bf16[2,48,3456]{2,1,0:T(8,128)(2,1)} %get-tuple-element.189), channel_id=1, source_target_pairs={{0,2},{1,3},{2,0},{3,1},{4,6},{5,7},{6,4},{7,5},{8,10},{9,11},{10,... | collective-permute-start | bytes 1990664 | tf_op jit(solution)/shard_map/ppermute | solution.py:524
  241.0 17.2 %collective-permute-start.23 = (bf16[2,48,3456]{2,1,0:T(8,128)(2,1)}, bf16[2,48,3456]{2,1,0:T(8,128)(2,1)S(1)}, u32[]{:S(2)}, u32[]{:S(2)}) collective-permute-start(bf16[2,48,3456]{2,1,0:T(8,128)(2,1)} %get-tuple-element.191), channel_id=1, source_target_pairs={{0,4},{4,0},{8,12},{12,8},{16,20},{20,16},{24,28},{28,24},{1,5},{5... | collective-permute-start | bytes 1990664 | tf_op jit(solution)/shard_map/ppermute | solution.py:525
  253.3 16.1 %collective-permute-start.25 = (bf16[16,48,1152]{2,1,0:T(8,128)(2,1)}, bf16[16,48,1152]{2,1,0:T(8,128)(2,1)}, u32[]{:S(2)}, u32[]{:S(2)}) collective-permute-start(bf16[16,48,1152]{2,1,0:T(8,128)(2,1)} %get-tuple-element.154), channel_id=1, source_target_pairs={{0,1},{1,0},{2,3},{3,2},{4,5},{5,4},{6,7},{7,6},{8,9},{9,8},{10,11... | collective-permute-start | bytes 5308424 | tf_op jit(solution)/shard_map/ppermute | solution.py:522
  262.7 30.2 %collective-permute-start.33 = (bf16[48,3456]{1,0:T(8,128)(2,1)}, bf16[48,3456]{1,0:T(8,128)(2,1)}, u32[]{:S(2)}, u32[]{:S(2)}) collective-permute-start(bf16[48,3456]{1,0:T(8,128)(2,1)} %get-tuple-element.156), channel_id=1, source_target_pairs={{0,24},{4,28},{8,0},{12,4},{16,8},{20,12},{24,16},{28,20},{1,25},{... | collective-permute-start | bytes 995336 | tf_op jit(solution)/shard_map/ppermute | solution.py:527
  264.5 31.5 %collective-permute-start.34 = (bf16[48,3456]{1,0:T(8,128)(2,1)}, bf16[48,3456]{1,0:T(8,128)(2,1)}, u32[]{:S(2)}, u32[]{:S(2)}) collective-permute-start(bf16[48,3456]{1,0:T(8,128)(2,1)} %get-tuple-element.157), channel_id=1, source_target_pairs={{0,16},{4,20},{8,24},{12,28},{16,0},{20,4},{24,8},{28,12},{1,17},{... | collective-permute-start | bytes 995336 | tf_op jit(solution)/shard_map/ppermute | solution.py:527
  264.5 31.5 %collective-permute-start.35 = (bf16[48,3456]{1,0:T(8,128)(2,1)}, bf16[48,3456]{1,0:T(8,128)(2,1)}, u32[]{:S(2)}, u32[]{:S(2)}) collective-permute-start(bf16[48,3456]{1,0:T(8,128)(2,1)} %get-tuple-element.158), channel_id=1, source_target_pairs={{0,8},{4,12},{8,16},{12,20},{16,24},{20,28},{24,0},{28,4},{1,9},{5... | collective-permute-start | bytes 995336 | tf_op jit(solution)/shard_map/ppermute | solution.py:527
  272.0 11.2 %collective-permute-start.26 = (bf16[4,48,1152]{2,1,0:T(8,128)(2,1)}, bf16[4,48,1152]{2,1,0:T(8,128)(2,1)S(1)}, u32[]{:S(2)}, u32[]{:S(2)}) collective-permute-start(bf16[4,48,1152]{2,1,0:T(8,128)(2,1)} %get-tuple-element.186), channel_id=1, source_target_pairs={{0,2},{1,3},{2,0},{3,1},{4,6},{5,7},{6,4},{7,5},{8,10},{9,11},{10,... | collective-permute-start | bytes 1327112 | tf_op jit(solution)/shard_map/ppermute | solution.py:524
  272.9 10.4 %collective-permute-start.27 = (bf16[4,48,1152]{2,1,0:T(8,128)(2,1)S(1)}, bf16[4,48,1152]{2,1,0:T(8,128)(2,1)S(1)}, u32[]{:S(2)}, u32[]{:S(2)}) collective-permute-start(bf16[4,48,1152]{2,1,0:T(8,128)(2,1)S(1)} %get-tuple-element.185), channel_id=1, source_target_pairs={{0,4},{4,0},{8,12},{12,8},{16,20},{20,16},{24,28},{28,24},{1,5},{5... | collective-permute-start | bytes 1327112 | tf_op jit(solution)/shard_map/ppermute | solution.py:525
  289.4 15.5 %collective-permute-start.31 = (bf16[48,1152]{1,0:T(8,128)(2,1)S(1)}, bf16[48,1152]{1,0:T(8,128)(2,1)S(1)}, u32[]{:S(2)}, u32[]{:S(2)}) collective-permute-start(bf16[48,1152]{1,0:T(8,128)(2,1)S(1)} %get-tuple-element.204), channel_id=1, source_target_pairs={{0,16},{4,20},{8,24},{12,28},{16,0},{20,4},{24,8},{28,12},{1,17},{... | collective-permute-start | bytes 331784 | tf_op jit(solution)/shard_map/ppermute | solution.py:527
  291.6 13.3 %collective-permute-start.32 = (bf16[48,1152]{1,0:T(8,128)(2,1)S(1)}, bf16[48,1152]{1,0:T(8,128)(2,1)S(1)}, u32[]{:S(2)}, u32[]{:S(2)}) collective-permute-start(bf16[48,1152]{1,0:T(8,128)(2,1)S(1)} %get-tuple-element.203), channel_id=1, source_target_pairs={{0,8},{4,12},{8,16},{12,20},{16,24},{20,28},{24,0},{28,4},{1,9},{5... | collective-permute-start | bytes 331784 | tf_op jit(solution)/shard_map/ppermute | solution.py:527
  292.9 12.0 %collective-permute-start.29 = (bf16[48,1152]{1,0:T(8,128)(2,1)S(1)}, bf16[48,1152]{1,0:T(8,128)(2,1)S(1)}, u32[]{:S(2)}, u32[]{:S(2)}) collective-permute-start(bf16[48,1152]{1,0:T(8,128)(2,1)S(1)} %get-tuple-element.205), channel_id=1, source_target_pairs={{0,24},{4,28},{8,0},{12,4},{16,8},{20,12},{24,16},{28,20},{1,25},{... | collective-permute-start | bytes 331784 | tf_op jit(solution)/shard_map/ppermute | solution.py:527
  (42 other events, 168.9 us)
Sparse Core Ops, SparseCore 0:
  11.9 102.9 all-gather.1
